TPU v7x, 32 devices: a whole 2x2x4 slice. The times are simulated.
32 devices in a mesh: dp: 8 (over y, x, core), tensor: 4 (over z).
Axes of the slice: x: 2, y: 2, z: 4, core: 2. Of those that a mesh axis runs over, the one named last changes fastest.
Arguments:
- tokens: bfloat16 [8192, 1536], P(('dp', 'tensor')), may hold values from -6 to 6
- first_gain: float32 [1536], replicated, may hold values from 0.25 to 1.75
- query_weight: bfloat16 [1536, 768], P(None, 'tensor'), may hold values from -0.0625 to 0.0625
- key_weight: bfloat16 [1536, 768], P(None, 'tensor'), may hold values from -0.0625 to 0.0625
- value_weight: bfloat16 [1536, 768], P(None, 'tensor'), may hold values from -0.15625 to 0.15625
- out_weight: bfloat16 [1536, 768], P(None, 'tensor'), may hold values from -0.875 to 0.875
- bucket_table: float32 [32, 12], P(None, 'tensor'), may hold values from -3 to 3
- second_gain: float32 [1536], replicated, may hold values from 0.25 to 1.75
- gate_weight: bfloat16 [1536, 3968], P(None, 'tensor'), may hold values from -0.15625 to 0.15625
- up_weight: bfloat16 [1536, 3968], P(None, 'tensor'), may hold values from -0.15625 to 0.15625
- down_weight: bfloat16 [1536, 3968], P(None, 'tensor'), may hold values from -0.09375 to 0.09375
- piece_start: int32 [8, 2], P('dp'), may hold values from 0 to 768, as said below
- bucket_index: int32 [2047], replicated, may hold values from 0 to 31, as said below
- cotangent: bfloat16 [8192, 1536], P(('dp', 'tensor')), may hold values from -6 to 6
Outputs:
- layer_out: bfloat16 [8192, 1536], P(('dp', 'tensor'))
- input_grad: bfloat16 [8192, 1536], P(('dp', 'tensor'))
- first_gain_grad: float32 [1536], replicated
- query_grad: float32 [1536, 768], P('dp', 'tensor')
- key_grad: float32 [1536, 768], P('dp', 'tensor')
- value_grad: float32 [1536, 768], P('dp', 'tensor')
- out_grad: float32 [1536, 768], P('dp', 'tensor')
- table_grad: float32 [32, 12], P(None, 'tensor')
- second_gain_grad: float32 [1536], replicated
- gate_grad: float32 [1536, 3968], P('dp', 'tensor')
- up_grad: float32 [1536, 3968], P('dp', 'tensor')
- down_grad: float32 [1536, 3968], P('dp', 'tensor')
Inputs may be any that keep to these rules, and one draw needn't show every extreme that they name: `piece_start`: piece p of a sequence lies within positions p * 512 to (p + 1) * 512 - 1, so pieces never intersect. bucket_index[d + 1023] is the bucket of key minus query position d: for d <= 0 it lies below 16 and equals |d| when |d| < 8; for d > 0 it is 16 plus the bucket that -d has, so it equals |d| + 32 // 2 when |d| < 8; it never falls as |d| grows on either side.
All inputs are finite; a program needn't handle non-finite values.
Results may differ from a plain program's by a relative error of at most 0.02.
Values may be sent and summed in bfloat16 or wider, within the bound.
A program may use at most 192 MiB of HBM per device.

v0:
```python
import jax
import jax.numpy as jnp
from jax import lax
from jax.sharding import PartitionSpec as P

NB = 32
LEN = 1024
QBLK = 512
PIECE = 256
NPIECE = 2


EPSILON = 1e-06
MASKED = -1000000000.0
HIGHEST = lax.Precision.HIGHEST


def normed(row_block, gain_vec):
    inv_rms = lax.rsqrt(jnp.mean(row_block * row_block, axis=-1, keepdims=True) + EPSILON)
    return row_block * inv_rms * gain_vec


def gelu_tanh(values):
    return jax.nn.gelu(values, approximate=True)


def piece_labels(starts_row, position):
    inside = (position[None, :] >= starts_row[:, None]) & (
        position[None, :] < starts_row[:, None] + PIECE
    )
    labels = jnp.arange(1, NPIECE + 1, dtype=jnp.int32)
    return jnp.sum(inside.astype(jnp.int32) * labels[:, None], axis=0) - 1


def bias_rows(distance_bias, query_start):
    width = QBLK + LEN - 1
    window = lax.dynamic_slice_in_dim(distance_bias, LEN - QBLK - query_start, width, 1)
    heads = window.shape[0]
    tiled = jnp.tile(window, (1, QBLK + 1))[:, : QBLK * (width + 1)]
    skewed = tiled.reshape(heads, QBLK, width + 1)[:, :, :LEN]
    return jnp.flip(skewed, axis=1)


def diagonal_sums(grad_block):
    width = QBLK + LEN - 1
    heads = grad_block.shape[0]
    flipped = jnp.flip(grad_block, axis=1)
    padded = jnp.pad(flipped, ((0, 0), (0, 0), (0, width + 1 - LEN)))
    flat = jnp.pad(padded.reshape(heads, QBLK * (width + 1)), ((0, 0), (0, LEN - 1)))
    return jnp.sum(flat.reshape(heads, QBLK + 1, width), axis=1)


def block_scores(query_block, key_seq, distance_bias, starts_row, query_start):
    query_pos = query_start + jnp.arange(QBLK, dtype=jnp.int32)
    key_pos = jnp.arange(LEN, dtype=jnp.int32)
    query_piece = piece_labels(starts_row, query_pos)
    key_piece = piece_labels(starts_row, key_pos)
    allowed = (key_pos[None, :] <= query_pos[:, None]) | (
        query_piece[:, None] == key_piece[None, :]
    ) & (query_piece[:, None] >= 0)
    raw_scores = jnp.einsum(
        "qhd,khd->hqk", query_block, key_seq, preferred_element_type=jnp.float32
    )
    return jnp.where(allowed[None], raw_scores + bias_rows(distance_bias, query_start), MASKED)


def locate(block_id):
    per_seq = LEN // QBLK
    sequence = block_id // per_seq
    query_start = block_id % per_seq * QBLK
    return (sequence, query_start, sequence * LEN + query_start)


def per_device(
    tokens,
    first_gain,
    query_weight,
    key_weight,
    value_weight,
    out_weight,
    bucket_table,
    second_gain,
    gate_weight,
    up_weight,
    down_weight,
    piece_start,
    bucket_index,
    cotangent,
):
    own_rows = tokens.shape[0]
    groups = piece_start.shape[0]
    all_rows = groups * LEN
    head_count = bucket_table.shape[1]
    inner_dev = query_weight.shape[1]
    head_dim = inner_dev // head_count
    block_count = all_rows // QBLK
    contract_cols = (((1,), (1,)), ((), ()))
    contract_rows = (((0,), (0,)), ((), ()))
    distance_hot = (bucket_index[:, None] == jnp.arange(NB, dtype=jnp.int32)[None, :]).astype(
        jnp.float32
    )
    distance_bias = jnp.dot(distance_hot, bucket_table, precision=HIGHEST).T
    inputs = tokens.astype(jnp.float32)
    norm_first = normed(inputs, first_gain).astype(jnp.bfloat16)
    first_all = lax.all_gather(norm_first, "tensor", axis=0, tiled=True)
    query_low = jnp.dot(first_all, query_weight, preferred_element_type=jnp.float32).astype(
        jnp.bfloat16
    )
    key_low = jnp.dot(first_all, key_weight, preferred_element_type=jnp.float32).astype(
        jnp.bfloat16
    )
    value_low = jnp.dot(first_all, value_weight, preferred_element_type=jnp.float32).astype(
        jnp.bfloat16
    )
    query_heads = query_low.reshape(all_rows, head_count, head_dim)
    key_heads = key_low.reshape(all_rows, head_count, head_dim)
    value_heads = value_low.reshape(all_rows, head_count, head_dim)

    def forward_block(block_id):
        sequence, query_start, row_start = locate(block_id)
        query_block = lax.dynamic_slice_in_dim(query_heads, row_start, QBLK, 0)
        scores = block_scores(
            query_block, key_heads, distance_bias, piece_start[sequence], query_start
        )
        peak = jnp.max(scores, axis=-1, keepdims=True)
        powered = jnp.exp(scores - peak)
        row_total = jnp.sum(powered, axis=-1, keepdims=True)
        softmax_low = (powered / row_total).astype(jnp.bfloat16)
        attended = jnp.einsum(
            "hqk,khd->qhd", softmax_low, value_heads, preferred_element_type=jnp.float32
        )
        return (attended.reshape(QBLK, inner_dev), (peak + jnp.log(row_total))[..., 0])

    attended, log_norms = lax.map(forward_block, jnp.arange(block_count, dtype=jnp.int32))
    attended_low = attended.reshape(all_rows, inner_dev).astype(jnp.bfloat16)
    picked = attended_low
    middle = inputs + lax.psum_scatter(
        lax.dot_general(
            picked, out_weight, contract_cols, preferred_element_type=jnp.float32
        ).astype(jnp.bfloat16),
        "tensor",
        scatter_dimension=0,
        tiled=True,
    ).astype(jnp.float32)
    norm_second = normed(middle, second_gain).astype(jnp.bfloat16)
    second_all = lax.all_gather(norm_second, "tensor", axis=0, tiled=True)
    gate_pre = jnp.dot(second_all, gate_weight, preferred_element_type=jnp.float32)
    up_proj = jnp.dot(second_all, up_weight, preferred_element_type=jnp.float32)
    activated, gelu_back = jax.vjp(gelu_tanh, gate_pre)
    hidden_low = (activated * up_proj).astype(jnp.bfloat16)
    picked = hidden_low
    layer_out = middle + lax.psum_scatter(
        lax.dot_general(
            picked, down_weight, contract_cols, preferred_element_type=jnp.float32
        ).astype(jnp.bfloat16),
        "tensor",
        scatter_dimension=0,
        tiled=True,
    ).astype(jnp.float32)
    grad_all = lax.all_gather(cotangent, "tensor", axis=0, tiled=True)
    down_grad = lax.dot_general(
        grad_all, hidden_low, contract_rows, preferred_element_type=jnp.float32
    )
    grad_hidden = jnp.dot(grad_all, down_weight, preferred_element_type=jnp.float32)
    (grad_act,) = gelu_back(grad_hidden * up_proj)
    grad_gate_low = grad_act.astype(jnp.bfloat16)
    grad_up_low = (grad_hidden * activated).astype(jnp.bfloat16)
    gate_grad = lax.dot_general(
        second_all, grad_gate_low, contract_rows, preferred_element_type=jnp.float32
    )
    up_grad = lax.dot_general(
        second_all, grad_up_low, contract_rows, preferred_element_type=jnp.float32
    )
    summed_rows = lax.dot_general(
        grad_gate_low, gate_weight, contract_cols, preferred_element_type=jnp.float32
    )
    grad_second = lax.psum_scatter(
        (
            summed_rows
            + lax.dot_general(
                grad_up_low, up_weight, contract_cols, preferred_element_type=jnp.float32
            )
        ).astype(jnp.bfloat16),
        "tensor",
        scatter_dimension=0,
        tiled=True,
    ).astype(jnp.float32)
    _, second_back = jax.vjp(normed, middle, second_gain)
    middle_part, second_gain_grad = second_back(grad_second)
    grad_middle = cotangent.astype(jnp.float32) + middle_part
    middle_all = lax.all_gather(grad_middle.astype(jnp.bfloat16), "tensor", axis=0, tiled=True)
    out_grad = lax.dot_general(
        middle_all, attended_low, contract_rows, preferred_element_type=jnp.float32
    )
    grad_attended = jnp.dot(middle_all, out_weight, preferred_element_type=jnp.float32).astype(
        jnp.bfloat16
    )
    grad_attended = grad_attended.reshape(all_rows, head_count, head_dim)

    def backward_block(block_id, running):
        grad_query, grad_key, grad_value, grad_distance = running
        sequence, query_start, row_start = locate(block_id)
        query_block = lax.dynamic_slice_in_dim(query_heads, row_start, QBLK, 0)
        scores = block_scores(
            query_block, key_heads, distance_bias, piece_start[sequence], query_start
        )
        softmax_rows = jnp.exp(scores - log_norms[block_id][..., None])
        grad_block = lax.dynamic_slice_in_dim(grad_attended, row_start, QBLK, 0)
        grad_probs = jnp.einsum(
            "qhd,khd->hqk", grad_block, value_heads, preferred_element_type=jnp.float32
        )
        weighted = jnp.sum(softmax_rows * grad_probs, axis=-1, keepdims=True)
        grad_scores = (softmax_rows * (grad_probs - weighted)).astype(jnp.bfloat16)
        query_part = jnp.einsum(
            "hqk,khd->qhd", grad_scores, key_heads, preferred_element_type=jnp.float32
        )
        key_part = jnp.einsum(
            "hqk,qhd->khd", grad_scores, query_block, preferred_element_type=jnp.float32
        )
        value_part = jnp.einsum(
            "hqk,qhd->khd",
            softmax_rows.astype(jnp.bfloat16),
            grad_block,
            preferred_element_type=jnp.float32,
        )
        grad_query = lax.dynamic_update_slice_in_dim(grad_query, query_part, row_start, 0)
        grad_key = grad_key + key_part
        grad_value = grad_value + value_part
        diag_part = diagonal_sums(grad_scores.astype(jnp.float32))
        width = QBLK + LEN - 1
        diag_from = LEN - QBLK - query_start
        current = lax.dynamic_slice_in_dim(grad_distance, diag_from, width, 1)
        grad_distance = lax.dynamic_update_slice_in_dim(
            grad_distance, current + diag_part, diag_from, 1
        )
        return (grad_query, grad_key, grad_value, grad_distance)

    zero_heads = jnp.zeros((all_rows, head_count, head_dim), jnp.float32)
    zero_distance = jnp.zeros((head_count, 2 * LEN - 1), jnp.float32)
    grad_query, grad_key, grad_value, grad_distance = lax.fori_loop(
        0, block_count, backward_block, (zero_heads, zero_heads, zero_heads, zero_distance)
    )
    table_grad = jnp.dot(distance_hot.T, grad_distance.T, precision=HIGHEST)
    grad_query_low = grad_query.reshape(all_rows, inner_dev).astype(jnp.bfloat16)
    grad_key_low = grad_key.reshape(all_rows, inner_dev).astype(jnp.bfloat16)
    grad_value_low = grad_value.reshape(all_rows, inner_dev).astype(jnp.bfloat16)
    query_grad = lax.dot_general(
        first_all, grad_query_low, contract_rows, preferred_element_type=jnp.float32
    )
    key_grad = lax.dot_general(
        first_all, grad_key_low, contract_rows, preferred_element_type=jnp.float32
    )
    value_grad = lax.dot_general(
        first_all, grad_value_low, contract_rows, preferred_element_type=jnp.float32
    )
    summed_rows = jnp.zeros(
        (lax.axis_size("tensor") * own_rows, query_weight.shape[0]), jnp.float32
    )
    for grad_low, weight in (
        (grad_query_low, query_weight),
        (grad_key_low, key_weight),
        (grad_value_low, value_weight),
    ):
        picked = grad_low
        summed_rows = summed_rows + lax.dot_general(
            picked, weight, contract_cols, preferred_element_type=jnp.float32
        )
    grad_first = lax.psum_scatter(
        summed_rows.astype(jnp.bfloat16), "tensor", scatter_dimension=0, tiled=True
    ).astype(jnp.float32)
    _, first_back = jax.vjp(normed, inputs, first_gain)
    input_part, first_gain_grad = first_back(grad_first)
    input_grad = grad_middle + input_part
    query_grad, key_grad, value_grad, out_grad, gate_grad, up_grad, down_grad = (
        lax.psum_scatter(query_grad, "dp", scatter_dimension=0, tiled=True),
        lax.psum_scatter(key_grad, "dp", scatter_dimension=0, tiled=True),
        lax.psum_scatter(value_grad, "dp", scatter_dimension=0, tiled=True),
        lax.psum_scatter(out_grad, "dp", scatter_dimension=0, tiled=True),
        lax.psum_scatter(gate_grad, "dp", scatter_dimension=0, tiled=True),
        lax.psum_scatter(up_grad, "dp", scatter_dimension=0, tiled=True),
        lax.psum_scatter(down_grad, "dp", scatter_dimension=0, tiled=True),
    )
    table_grad = lax.psum(table_grad, "dp")
    first_gain_grad, second_gain_grad = lax.psum(
        (first_gain_grad, second_gain_grad), ("dp", "tensor")
    )
    return (
        layer_out.astype(jnp.bfloat16),
        input_grad.astype(jnp.bfloat16),
        first_gain_grad,
        query_grad,
        key_grad,
        value_grad,
        out_grad,
        table_grad,
        second_gain_grad,
        gate_grad,
        up_grad,
        down_grad,
    )


def solution(mesh):
    return jax.shard_map(
        per_device,
        mesh=mesh,
        in_specs=(
            P(("dp", "tensor"), None),
            P(),
            P(None, "tensor"),
            P(None, "tensor"),
            P(None, "tensor"),
            P(None, "tensor"),
            P(None, "tensor"),
            P(),
            P(None, "tensor"),
            P(None, "tensor"),
            P(None, "tensor"),
            P("dp", None),
            P(),
            P(("dp", "tensor"), None),
        ),
        out_specs=(
            P(("dp", "tensor"), None),
            P(("dp", "tensor"), None),
            P(),
            P("dp", "tensor"),
            P("dp", "tensor"),
            P("dp", "tensor"),
            P("dp", "tensor"),
            P(None, "tensor"),
            P(),
            P("dp", "tensor"),
            P("dp", "tensor"),
            P("dp", "tensor"),
        ),
        check_vma=False,
    )
```

profile of v0, /device:TPU:0, one launch (start us, length us, event | category | flops | bytes accessed | tf_op | source)
XLA Modules:
  0.0 1671.4 jit_solution(16654163404661405045)
XLA Ops:
  13.0 65.6 %all-gather.5.cloned.1.call-done = bf16[1024,1536]{1,0:T(8,128)(2,1)} async-done(((bf16[256,1536]{1,0:T(8,128)(2,1)}), bf16[1024,1536]{1,0:T(8,128)(2,1)}) %all-gather.5.cloned.1.call-update) | async-done | bytes 3145744 | tf_op jit(solution)/shard_map/all_gather | solution.py:105
  85.8 241.3 %while.38 = (s32[]{:T(128)}, bf16[2,512,192]{1,2,0:T(8,128)(2,1)}, f32[2,3,512]{2,1,0:T(4,128)}, s32[2]{0:T(128)S(1)}, s32[1,2]{1,0:T(1,128)}, /*index=5*/bf16[1...) while((s32[]{:T(128)}, bf16[2,512,192]{1,2,0:T(8,128)(2,1)}, ...), condition=%wide.region_6.7_spmd, body=%wide.region_1.6_spmd.sunk | while | flops 417348640 | bytes 142808624 | solution.py:134
  97.8 15.2 reshape.403
  148.9 48.5 %rev.35 = f32[3,512,1024]{2,1,0:T(8,128)} reverse(f32[3,512,1024]{2,1,0:T(8,128)} %slice.47), dimensions={1} | reverse | bytes 12582912 | tf_op jit(solution)/shard_map/while/body/eval_jaxpr/jit(_flip)/rev | solution.py:41
  218.1 15.2 reshape.403
  269.2 48.5 %rev.35 = f32[3,512,1024]{2,1,0:T(8,128)} reverse(f32[3,512,1024]{2,1,0:T(8,128)} %slice.47), dimensions={1} | reverse | bytes 12582912 | tf_op jit(solution)/shard_map/while/body/eval_jaxpr/jit(_flip)/rev | solution.py:41
  332.7 59.0 %reduce-scatter.14.cloned.1.call-done = bf16[256,1536]{1,0:T(8,128)(2,1)} async-done(((bf16[1024,1536]{1,0:T(8,128)(2,1)}), bf16[256,1536]{1,0:T(8,128)(2,1)}) %reduce-scatter.14.cloned.1.call-update) | async-done | bytes 786448 | tf_op jit(solution)/shard_map/reduce_scatter | solution.py:137
  396.6 63.1 %all-gather.7.cloned.1.call-done = bf16[1024,1536]{1,0:T(8,128)(2,1)} async-done(((bf16[256,1536]{1,0:T(8,128)(2,1)}), bf16[1024,1536]{1,0:T(8,128)(2,1)}) %all-gather.7.cloned.1.call-update) | async-done | bytes 3145744 | tf_op jit(solution)/shard_map/all_gather | solution.py:146
  472.9 50.4 %all-gather.9.cloned.1.call-done = bf16[1024,1536]{1,0:T(8,128)(2,1)} async-done(((bf16[256,1536]{1,0:T(8,128)(2,1)}), bf16[1024,1536]{1,0:T(8,128)(2,1)}) %all-gather.9.cloned.1.call-update) | async-done | bytes 3145744 | tf_op jit(solution)/shard_map/all_gather | solution.py:160
  542.5 59.0 %reduce-scatter.18.cloned.1.call-done = bf16[256,1536]{1,0:T(8,128)(2,1)} async-done(((bf16[1024,1536]{1,0:T(8,128)(2,1)}), bf16[256,1536]{1,0:T(8,128)(2,1)}) %reduce-scatter.18.cloned.1.call-update) | async-done | bytes 786448 | tf_op jit(solution)/shard_map/reduce_scatter | solution.py:177
  607.9 63.6 %all-gather.11.cloned.1.call-done = bf16[1024,1536]{1,0:T(8,128)(2,1)} async-done(((bf16[256,1536]{1,0:T(8,128)(2,1)}), bf16[1024,1536]{1,0:T(8,128)(2,1)}) %all-gather.11.cloned.1.call-update) | async-done | bytes 3145744 | tf_op jit(solution)/shard_map/all_gather | solution.py:191
  676.2 489.1 %while.39 = (s32[]{:T(128)}, bf16[1024,3,64]{0,2,1:T(8,128)(2,1)}, f32[1024,3,64]{0,2,1:T(8,128)}, f32[1024,3,64]{0,2,1:T(8,128)}, f32[3,2047]{1,0:T(4,128)S(1)}...) while((s32[]{:T(128)}, bf16[1024,3,64]{0,2,1:T(8,128)(2,1)}, ...), condition=%wide.region_17.18_spmd.clone, body=%wide.region_12.17_spmd.clone.sunk | while | flops 1026050048 | bytes 305763776 | solution.py:240
  690.6 15.2 reshape.404
  705.8 14.3 tile.47
  742.1 48.5 %rev.36 = f32[3,512,1024]{2,1,0:T(8,128)} reverse(f32[3,512,1024]{2,1,0:T(8,128)} %slice.49), dimensions={1} | reverse | bytes 12582912 | tf_op jit(solution)/shard_map/while/body/eval_jaxpr/jit(_flip)/rev | solution.py:41
  806.1 46.0 %rev.37 = f32[3,512,1024]{2,1,0:T(8,128)} reverse(bf16[3,512,1024]{2,1,0:T(8,128)(2,1)} %copy-done.1), dimensions={1} | reverse | bytes 9437184 | tf_op jit(solution)/shard_map/while/body/eval_jaxpr/jit(_flip)/rev | solution.py:47
  856.1 19.9 %copy.48 = f32[1,3,512,1536]{3,1,2,0:T(4,128)S(1)} copy(f32[1,3,512,1536]{3,2,1,0:T(8,128)S(1)} %pad_bitcast_fusion.2) | data formatting | bytes 18874368 | tf_op jit(solution)/shard_map/while
  895.2 16.3 reshape.406
  930.8 15.2 reshape.404
  982.1 48.5 %rev.36 = f32[3,512,1024]{2,1,0:T(8,128)} reverse(f32[3,512,1024]{2,1,0:T(8,128)} %slice.49), dimensions={1} | reverse | bytes 12582912 | tf_op jit(solution)/shard_map/while/body/eval_jaxpr/jit(_flip)/rev | solution.py:41
  1047.1 46.0 %rev.37 = f32[3,512,1024]{2,1,0:T(8,128)} reverse(bf16[3,512,1024]{2,1,0:T(8,128)(2,1)} %copy-done.1), dimensions={1} | reverse | bytes 9437184 | tf_op jit(solution)/shard_map/while/body/eval_jaxpr/jit(_flip)/rev | solution.py:47
  1097.2 19.9 %copy.48 = f32[1,3,512,1536]{3,1,2,0:T(4,128)S(1)} copy(f32[1,3,512,1536]{3,2,1,0:T(8,128)S(1)} %pad_bitcast_fusion.2) | data formatting | bytes 18874368 | tf_op jit(solution)/shard_map/while
  1136.3 16.5 reshape.406
  1232.0 14.3 psum.22
  1248.3 43.6 %all-reduce.2 = (f32[1536]{0:T(1024)}, f32[1536]{0:T(1024)}) all-reduce(f32[1536]{0:T(1024)S(1)} %get-tuple-element.593, f32[1536]{0:T(1024)S(1)} %copy-done.23), channel_id=1, replica_groups=mesh['dp'=8,'tensor'=4] {'dp','tensor'}, use_global_device_ids=true, to_apply=%region_21.22 | all-reduce | flops 3072 | bytes 24576 | tf_op jit(solution)/shard_map/psum | solution.py:284
  1301.4 61.1 %reduce-scatter.34.cloned.1.call-done = f32[192,992]{1,0:T(8,128)} async-done(((f32[1536,992]{1,0:T(8,128)}), f32[192,992]{1,0:T(8,128)}) %reduce-scatter.34.cloned.1.call-update) | async-done | bytes 761872
  1362.5 65.9 %reduce-scatter.32.cloned.1.call-done = f32[192,992]{1,0:T(8,128)} async-done(((f32[1536,992]{1,0:T(8,128)}), f32[192,992]{1,0:T(8,128)}) %reduce-scatter.32.cloned.1.call-update) | async-done | bytes 761872 | tf_op jit(solution)/shard_map/reduce_scatter | solution.py:280
  1428.4 65.7 %reduce-scatter.30.cloned.1.call-done = f32[192,992]{1,0:T(8,128)} async-done(((f32[1536,992]{1,0:T(8,128)}), f32[192,992]{1,0:T(8,128)}) %reduce-scatter.30.cloned.1.call-update) | async-done | bytes 761872 | tf_op jit(solution)/shard_map/reduce_scatter | solution.py:279
  1494.2 42.5 %reduce-scatter.28.cloned.1.call-done = f32[192,192]{1,0:T(8,128)} async-done(((f32[1536,192]{1,0:T(8,128)}), f32[192,192]{1,0:T(8,128)}) %reduce-scatter.28.cloned.1.call-update) | async-done | bytes 147472 | tf_op jit(solution)/shard_map/reduce_scatter | solution.py:278
  1536.7 42.7 %reduce-scatter.26.cloned.1.call-done = f32[192,192]{1,0:T(8,128)} async-done(((f32[1536,192]{1,0:T(8,128)}), f32[192,192]{1,0:T(8,128)}) %reduce-scatter.26.cloned.1.call-update) | async-done | bytes 147472 | tf_op jit(solution)/shard_map/reduce_scatter | solution.py:277
  1579.4 42.5 %reduce-scatter.22.cloned.1.call-done = f32[192,192]{1,0:T(8,128)} async-done(((f32[1536,192]{1,0:T(8,128)}), f32[192,192]{1,0:T(8,128)}) %reduce-scatter.22.cloned.1.call-update) | async-done | bytes 147472 | tf_op jit(solution)/shard_map/reduce_scatter | solution.py:275
  1621.9 42.5 %reduce-scatter.24.cloned.1.call-done = f32[192,192]{1,0:T(8,128)} async-done(((f32[1536,192]{1,0:T(8,128)}), f32[192,192]{1,0:T(8,128)}) %reduce-scatter.24.cloned.1.call-update) | async-done | bytes 147472 | tf_op jit(solution)/shard_map/reduce_scatter | solution.py:276
  (275 shorter events, 427.1 us)
Async XLA Ops:
  7.2 516.1 %copy-start = (bf16[1536,992]{0,1:T(8,128)(2,1)S(1)}, bf16[1536,992]{0,1:T(8,128)(2,1)}, u32[]{:S(2)}) copy-start(bf16[1536,992]{0,1:T(8,128)(2,1)} %param.28) | copy-start | bytes 9142276
  7.2 5.1 copy-start.37
  7.2 5.1 copy-start.39
  7.2 71.3 %all-gather.5.cloned.1.call-start = ((), (), s32[]{:S(2)}) async-start(), calls=%async_computation.11 | async-start | bytes 3932160 | tf_op jit(solution)/shard_map/all_gather | solution.py:105
  12.2 379.5 %reduce-scatter.14.cloned.1.call-start = ((), (), s32[]{:S(2)}) async-start(), calls=%async_computation.12 | async-start | bytes 3932160 | tf_op jit(solution)/shard_map/reduce_scatter | solution.py:137
  332.6 60.8 %copy-start.20 = (f32[1536]{0:T(1024)S(1)}, f32[1536]{0:T(1024)}, u32[]{:S(2)}) copy-start(f32[1536]{0:T(1024)} %param.25) | copy-start | bytes 18436
  332.6 127.0 %all-gather.7.cloned.1.call-start = ((), (), s32[]{:S(2)}) async-start(), calls=%async_computation.13 | async-start | bytes 3932160 | tf_op jit(solution)/shard_map/all_gather | solution.py:146
  393.4 211.0 %copy-start.24 = (f32[256]{0:T(256)}, f32[256]{0:T(256)S(1)}, u32[]{:S(2)}) copy-start(f32[256]{0:T(256)S(1)} %fusion.53) | copy-start | bytes 3076
  396.0 127.3 %all-gather.9.cloned.1.call-start = ((), (), s32[]{:S(2)}) async-start(), calls=%async_computation.15 | async-start | bytes 3932160 | tf_op jit(solution)/shard_map/all_gather | solution.py:160
  396.6 204.9 %reduce-scatter.18.cloned.1.call-start = ((), (), s32[]{:S(2)}) async-start(), calls=%async_computation.16 | async-start | bytes 3932160 | tf_op jit(solution)/shard_map/reduce_scatter | solution.py:177
  459.7 8.2 copy-start.33
  459.7 8.2 copy-start.34
  523.3 10.4 copy-start.35
  542.4 129.0 %all-gather.11.cloned.1.call-start = ((), (), s32[]{:S(2)}) async-start(), calls=%async_computation.17 | async-start | bytes 3932160 | tf_op jit(solution)/shard_map/all_gather | solution.py:191
  604.4 71.0 %copy-start.30 = (f32[256]{0:T(256)}, f32[256]{0:T(256)S(1)}, u32[]{:S(2)}) copy-start(f32[256]{0:T(256)S(1)} %multiply_multiply_fusion.4) | copy-start | bytes 3076
  607.8 638.4 %reduce-scatter.20.cloned.1.call-start = ((), (), s32[]{:S(2)}) async-start(), calls=%async_computation.18 | async-start | bytes 3932160 | tf_op jit(solution)/shard_map/reduce_scatter | solution.py:268
  1174.1 122.7 %reduce-scatter.16.cloned.1.call-start = ((), (), s32[]{:S(2)}) async-start(), calls=%async_computation.14 | async-start | bytes 3932160 | tf_op jit(solution)/shard_map/reduce_scatter | solution.py:152
  1180.7 181.8 %reduce-scatter.34.cloned.1.call-start = ((), (), s32[]{:S(2)}) async-start(), calls=%async_computation.25 | async-start | bytes 7077888
  1195.8 232.7 %reduce-scatter.32.cloned.1.call-start = ((), (), s32[]{:S(2)}) async-start(), calls=%async_computation.24 | async-start | bytes 7077888 | tf_op jit(solution)/shard_map/reduce_scatter | solution.py:280
  1204.5 289.7 %reduce-scatter.30.cloned.1.call-start = ((), (), s32[]{:S(2)}) async-start(), calls=%async_computation.23 | async-start | bytes 7077888 | tf_op jit(solution)/shard_map/reduce_scatter | solution.py:279
  1213.4 323.3 %reduce-scatter.28.cloned.1.call-start = ((), (), s32[]{:S(2)}) async-start(), calls=%async_computation.22 | async-start | bytes 1769472 | tf_op jit(solution)/shard_map/reduce_scatter | solution.py:278
  1218.5 4.4 copy-start.11
  1218.5 360.9 %reduce-scatter.26.cloned.1.call-start = ((), (), s32[]{:S(2)}) async-start(), calls=%async_computation.21 | async-start | bytes 1769472 | tf_op jit(solution)/shard_map/reduce_scatter | solution.py:277
  1222.8 399.1 %reduce-scatter.22.cloned.1.call-start = ((), (), s32[]{:S(2)}) async-start(), calls=%async_computation.19 | async-start | bytes 1769472 | tf_op jit(solution)/shard_map/reduce_scatter | solution.py:275
  1227.0 19.2 %copy-start.22 = (f32[1536]{0:T(1024)S(1)}, f32[1536]{0:T(1024)}, u32[]{:S(2)}) copy-start(f32[1536]{0:T(1024)} %param.19) | copy-start | bytes 18436
  1227.0 19.2 %copy-start.27 = (f32[256]{0:T(256)S(1)}, f32[256]{0:T(256)}, u32[]{:S(2)}) copy-start(f32[256]{0:T(256)} %copy-done.26) | copy-start | bytes 3076
  1227.0 437.4 %reduce-scatter.24.cloned.1.call-start = ((), (), s32[]{:S(2)}) async-start(), calls=%async_computation.20 | async-start | bytes 1769472 | tf_op jit(solution)/shard_map/reduce_scatter | solution.py:276
  1231.3 17.0 %copy-start.23 = (f32[1536]{0:T(1024)S(1)}, f32[1536]{0:T(1024)}, u32[]{:S(2)}) copy-start(f32[1536]{0:T(1024)} %get-tuple-element.591) | copy-start | bytes 18436
  1231.3 60.6 %copy-start.29 = (f32[256]{0:T(256)S(1)}, f32[256]{0:T(256)}, u32[]{:S(2)}) copy-start(f32[256]{0:T(256)} %copy-done.28) | copy-start | bytes 3076
  1231.3 65.5 %copy-start.21 = (f32[1536]{0:T(1024)S(1)}, f32[1536]{0:T(1024)}, u32[]{:S(2)}) copy-start(f32[1536]{0:T(1024)} %param.25) | copy-start | bytes 18436
  1231.3 65.5 %copy-start.25 = (f32[256]{0:T(256)S(1)}, f32[256]{0:T(256)}, u32[]{:S(2)}) copy-start(f32[256]{0:T(256)} %copy-done.24) | copy-start | bytes 3076
  1231.3 65.4 %copy-start.31 = (f32[256]{0:T(256)S(1)}, f32[256]{0:T(256)}, u32[]{:S(2)}) copy-start(f32[256]{0:T(256)} %copy-done.30) | copy-start | bytes 3076
  (35 other events, 80.1 us)
Sparse Core Ops, SparseCore 0:
  12.3 66.1 all-gather.4
  332.7 58.8 reduce-scatter.13
  396.1 63.5 all-gather.6
  461.1 62.1 all-gather.8
  542.6 58.8 reduce-scatter.17
  607.9 63.5 all-gather.10
  1174.2 58.8 reduce-scatter.19
  1235.4 61.3 reduce-scatter.15
  1300.7 61.7 reduce-scatter.33
  1366.7 61.7 reduce-scatter.31
  1432.4 61.7 reduce-scatter.29
  1498.3 38.4 reduce-scatter.27
  1540.9 38.4 reduce-scatter.25
  1583.5 38.4 reduce-scatter.21
  1626.0 38.4 reduce-scatter.23
where the time goes:
time: 1700 us; the launch traced here: 1670 us
  waiting for transfers between devices  729 us (43%)
  local copies, waits for them, and re-layouts  650 us (38%)
  matrix products  145 us (9%)
  other arithmetic  58.7 us (3%)
  blocking collectives  57.9 us (3%)
    rev x4, local copies, waits for them, and re-layouts, bias_rows(): return jnp.flip(skewed, axis=1)  194 us
    while x54, local copies, waits for them, and re-layouts  172 us
    rev x2, local copies, waits for them, and re-layouts, diagonal_sums(): flipped = jnp.flip(grad_block, axis=1)  92 us
    another operation x8, local copies, waits for them, and re-layouts, bias_rows(): tiled = jnp.tile(window, (1, QBLK + 1))[:, :QBLK * (width + 1)]  75.5 us
    reduce_scatter x1, waiting for transfers between devices, per_device(): lax.psum_scatter(up_grad, 'dp', scatter_dimension=0, tiled=True)  65.9 us
    reduce_scatter x1, waiting for transfers between devices, per_device(): lax.psum_scatter(gate_grad, 'dp', scatter_dimension=0, tiled=True)  65.7 us
    all_gather x1, waiting for transfers between devices, per_device(): first_all = lax.all_gather(norm_first, 'tensor', axis=0, tiled=True)  65.6 us
    all_gather x1, waiting for transfers between devices, per_device(): lax.all_gather(grad_middle.astype(jnp.bfloat16), 'tensor', axis=0, tiled=...  63.6 us
  transfers between devices with their start and end apart: 15, of which 14 were waited for; matrix products, arithmetic and copies ran while one was open for 5% of the time, Pallas kernels for 0%

commit v1 on v0

v1 whole, which is shorter than its diff:
```python
import functools

import jax
import jax.numpy as jnp
from jax import lax
from jax.experimental import pallas as pl
from jax.experimental.pallas import tpu as pltpu
from jax.sharding import PartitionSpec as P

NB = 32
LEN = 1024
QB = 256
PIECE = 256
NPIECE = 2
HALF = LEN // NPIECE
SPAN = 5 * QB
DIST = 2 * LEN

EPSILON = 1e-06
MASKED = -1000000000.0
VMEM_LIMIT = 60 * 1024 * 1024


def normed(row_block, gain_vec):
    inv_rms = lax.rsqrt(jnp.mean(row_block * row_block, axis=-1, keepdims=True) + EPSILON)
    return row_block * inv_rms * gain_vec


def gelu_tanh(values):
    return jax.nn.gelu(values, approximate=True)


def dot(a, b, dims):
    return lax.dot_general(a, b, (dims, ((), ())), preferred_element_type=jnp.float32)


def key_count(block):
    return HALF if (block + 1) * QB <= HALF else LEN


def toeplitz(bucket_row, table_ref, head):
    row = jnp.zeros(bucket_row.shape, jnp.float32)
    for bucket in range(NB):
        row = jnp.where(bucket_row == bucket, table_ref[bucket, head], row)
    rows = jnp.broadcast_to(row, (QB, DIST))
    return pltpu.roll(rows, DIST - (QB - 1), 1, stride=1, stride_axis=0)[:, :SPAN]


def label_of(position, starts):
    label = jnp.zeros(position.shape, jnp.int32)
    for piece, start in enumerate(starts):
        inside = (position >= start) & (position < start + PIECE)
        label = jnp.where(inside, piece + 1, label)
    return label


def allowed_block(block, starts):
    keys = key_count(block)
    query = block * QB + lax.broadcasted_iota(jnp.int32, (QB, 1), 0)
    key = lax.broadcasted_iota(jnp.int32, (1, keys), 1)
    query_label = label_of(query, starts)
    key_label = label_of(key, starts)
    return (key <= query) | ((query_label == key_label) & (query_label > 0))


def attend_kernel(heads, head_dim, q_ref, k_ref, v_ref, bucket_ref, table_ref, start_ref, att_ref, low_ref, high_ref, bias_ref):
    starts = [start_ref[0, piece] for piece in range(NPIECE)]
    for head in range(heads):
        bias_ref[head] = toeplitz(bucket_ref[...], table_ref, head)
    for block in range(LEN // QB):
        keys = key_count(block)
        allowed = allowed_block(block, starts)
        first = LEN - QB - block * QB
        rows = pl.ds(block * QB, QB)
        outs = []
        for head in range(heads):
            cols = pl.ds(head * head_dim, head_dim)
            raw = dot(q_ref[rows, cols], k_ref[pl.ds(0, keys), cols], ((1,), (1,)))
            scores = jnp.where(allowed, raw + bias_ref[head, :, pl.ds(first, keys)], MASKED)
            peak = jnp.max(scores, axis=-1, keepdims=True)
            powered = jnp.exp(scores - peak)
            total = jnp.sum(powered, axis=-1, keepdims=True)
            probs = (powered * (1.0 / total)).astype(jnp.bfloat16)
            if keys == HALF:
                low_ref[head, rows, :] = probs
            else:
                high_ref[head, pl.ds(block * QB - HALF, QB), :] = probs
            outs.append(dot(probs, v_ref[pl.ds(0, keys), cols], ((1,), (0,))))
        att_ref[rows, :] = jnp.concatenate(outs, axis=1).astype(jnp.bfloat16)


def fold_diagonals(grid):
    rows = QB // 2
    width = grid.shape[1]
    while rows >= 1:
        grid = grid[:rows] + pltpu.roll(grid[rows : 2 * rows], width - rows, 1)
        rows //= 2
    return grid


def attend_back_kernel(heads, head_dim, q_ref, k_ref, v_ref, do_ref, low_ref, high_ref, dq_ref, dk_ref, dv_ref, dist_ref, diag_ref, dk_acc, dv_acc):
    blocks = LEN // QB
    for head in range(heads):
        cols = pl.ds(head * head_dim, head_dim)
        diag_ref[...] = jnp.zeros_like(diag_ref)
        for block in reversed(range(blocks)):
            keys = key_count(block)
            rows = pl.ds(block * QB, QB)
            first = LEN - block * QB
            if keys == HALF:
                probs_low = low_ref[head, rows, :]
            else:
                probs_low = high_ref[head, pl.ds(block * QB - HALF, QB), :]
            probs = probs_low.astype(jnp.float32)
            do = do_ref[rows, cols]
            grad_probs = dot(do, v_ref[pl.ds(0, keys), cols], ((1,), (1,)))
            weighted = jnp.sum(probs * grad_probs, axis=-1, keepdims=True)
            grad_low = (probs * (grad_probs - weighted)).astype(jnp.bfloat16)
            span = pl.ds(first, keys)
            diag_ref[:, span] = diag_ref[:, span] + grad_low.astype(jnp.float32)
            dq_ref[rows, cols] = dot(grad_low, k_ref[pl.ds(0, keys), cols], ((1,), (0,))).astype(
                jnp.bfloat16
            )
            key_part = dot(grad_low, q_ref[rows, cols], ((0,), (0,)))
            value_part = dot(probs_low, do, ((0,), (0,)))
            if block == blocks - 1:
                dk_acc[...] = key_part
                dv_acc[...] = value_part
            else:
                dk_acc[pl.ds(0, keys), :] += key_part
                dv_acc[pl.ds(0, keys), :] += value_part
        dk_ref[:, cols] = dk_acc[...].astype(jnp.bfloat16)
        dv_ref[:, cols] = dv_acc[...].astype(jnp.bfloat16)
        dist_ref[pl.ds(head, 1), :] = fold_diagonals(diag_ref[...])


def whole_vmem(count):
    return [pl.BlockSpec(memory_space=pltpu.VMEM)] * count


def attend(query, key, value, bucket_row, table, starts):
    heads = table.shape[1]
    inner = query.shape[1]
    smem = pl.BlockSpec(memory_space=pltpu.SMEM)
    return pl.pallas_call(
        functools.partial(attend_kernel, heads, inner // heads),
        out_shape=(
            jax.ShapeDtypeStruct(query.shape, jnp.bfloat16),
            jax.ShapeDtypeStruct((heads, HALF, HALF), jnp.bfloat16),
            jax.ShapeDtypeStruct((heads, HALF, LEN), jnp.bfloat16),
        ),
        in_specs=whole_vmem(4) + [smem, smem],
        out_specs=tuple(whole_vmem(3)),
        scratch_shapes=[pltpu.VMEM((heads, QB, SPAN), jnp.float32)],
        compiler_params=pltpu.CompilerParams(vmem_limit_bytes=VMEM_LIMIT),
        name="attend",
    )(query, key, value, bucket_row, table, starts)


def attend_back(query, key, value, grad_attended, low, high):
    heads = low.shape[0]
    inner = query.shape[1]
    shape = jax.ShapeDtypeStruct(query.shape, jnp.bfloat16)
    return pl.pallas_call(
        functools.partial(attend_back_kernel, heads, inner // heads),
        out_shape=(shape, shape, shape, jax.ShapeDtypeStruct((heads, SPAN + QB), jnp.float32)),
        in_specs=whole_vmem(6),
        out_specs=tuple(whole_vmem(4)),
        scratch_shapes=[
            pltpu.VMEM((QB, SPAN + QB), jnp.float32),
            pltpu.VMEM((LEN, inner // heads), jnp.float32),
            pltpu.VMEM((LEN, inner // heads), jnp.float32),
        ],
        compiler_params=pltpu.CompilerParams(vmem_limit_bytes=VMEM_LIMIT),
        name="attend_back",
    )(query, key, value, grad_attended, low, high)


def per_device(
    tokens,
    first_gain,
    query_weight,
    key_weight,
    value_weight,
    out_weight,
    bucket_table,
    second_gain,
    gate_weight,
    up_weight,
    down_weight,
    piece_start,
    bucket_index,
    cotangent,
):
    own_rows = tokens.shape[0]
    contract_cols = (((1,), (1,)), ((), ()))
    contract_rows = (((0,), (0,)), ((), ()))
    bucket_row = jnp.pad(bucket_index, (0, 1))[None, :]
    inputs = tokens.astype(jnp.float32)
    norm_first = normed(inputs, first_gain).astype(jnp.bfloat16)
    first_all = lax.all_gather(norm_first, "tensor", axis=0, tiled=True)
    query_low = jnp.dot(first_all, query_weight, preferred_element_type=jnp.float32).astype(
        jnp.bfloat16
    )
    key_low = jnp.dot(first_all, key_weight, preferred_element_type=jnp.float32).astype(
        jnp.bfloat16
    )
    value_low = jnp.dot(first_all, value_weight, preferred_element_type=jnp.float32).astype(
        jnp.bfloat16
    )
    attended_low, probs_low, probs_high = attend(
        query_low, key_low, value_low, bucket_row, bucket_table, piece_start
    )
    picked = attended_low
    middle = inputs + lax.psum_scatter(
        lax.dot_general(
            picked, out_weight, contract_cols, preferred_element_type=jnp.float32
        ).astype(jnp.bfloat16),
        "tensor",
        scatter_dimension=0,
        tiled=True,
    ).astype(jnp.float32)
    norm_second = normed(middle, second_gain).astype(jnp.bfloat16)
    second_all = lax.all_gather(norm_second, "tensor", axis=0, tiled=True)
    gate_pre = jnp.dot(second_all, gate_weight, preferred_element_type=jnp.float32)
    up_proj = jnp.dot(second_all, up_weight, preferred_element_type=jnp.float32)
    activated, gelu_back = jax.vjp(gelu_tanh, gate_pre)
    hidden_low = (activated * up_proj).astype(jnp.bfloat16)
    picked = hidden_low
    layer_out = middle + lax.psum_scatter(
        lax.dot_general(
            picked, down_weight, contract_cols, preferred_element_type=jnp.float32
        ).astype(jnp.bfloat16),
        "tensor",
        scatter_dimension=0,
        tiled=True,
    ).astype(jnp.float32)
    grad_all = lax.all_gather(cotangent, "tensor", axis=0, tiled=True)
    down_grad = lax.dot_general(
        grad_all, hidden_low, contract_rows, preferred_element_type=jnp.float32
    )
    grad_hidden = jnp.dot(grad_all, down_weight, preferred_element_type=jnp.float32)
    (grad_act,) = gelu_back(grad_hidden * up_proj)
    grad_gate_low = grad_act.astype(jnp.bfloat16)
    grad_up_low = (grad_hidden * activated).astype(jnp.bfloat16)
    gate_grad = lax.dot_general(
        second_all, grad_gate_low, contract_rows, preferred_element_type=jnp.float32
    )
    up_grad = lax.dot_general(
        second_all, grad_up_low, contract_rows, preferred_element_type=jnp.float32
    )
    summed_rows = lax.dot_general(
        grad_gate_low, gate_weight, contract_cols, preferred_element_type=jnp.float32
    )
    grad_second = lax.psum_scatter(
        (
            summed_rows
            + lax.dot_general(
                grad_up_low, up_weight, contract_cols, preferred_element_type=jnp.float32
            )
        ).astype(jnp.bfloat16),
        "tensor",
        scatter_dimension=0,
        tiled=True,
    ).astype(jnp.float32)
    _, second_back = jax.vjp(normed, middle, second_gain)
    middle_part, second_gain_grad = second_back(grad_second)
    grad_middle = cotangent.astype(jnp.float32) + middle_part
    middle_all = lax.all_gather(grad_middle.astype(jnp.bfloat16), "tensor", axis=0, tiled=True)
    out_grad = lax.dot_general(
        middle_all, attended_low, contract_rows, preferred_element_type=jnp.float32
    )
    grad_attended = jnp.dot(middle_all, out_weight, preferred_element_type=jnp.float32).astype(
        jnp.bfloat16
    )
    grad_query_low, grad_key_low, grad_value_low, distance_sums = attend_back(
        query_low, key_low, value_low, grad_attended, probs_low, probs_high
    )
    width = min(distance_sums.shape[1] - 1, bucket_index.shape[0])
    table_hot = bucket_index[None, :width] == jnp.arange(NB, dtype=jnp.int32)[:, None]
    table_grad = jnp.sum(
        jnp.where(table_hot[:, None, :], distance_sums[None, :, 1 : width + 1], 0.0), axis=2
    )
    query_grad = lax.dot_general(
        first_all, grad_query_low, contract_rows, preferred_element_type=jnp.float32
    )
    key_grad = lax.dot_general(
        first_all, grad_key_low, contract_rows, preferred_element_type=jnp.float32
    )
    value_grad = lax.dot_general(
        first_all, grad_value_low, contract_rows, preferred_element_type=jnp.float32
    )
    summed_rows = jnp.zeros(
        (lax.axis_size("tensor") * own_rows, query_weight.shape[0]), jnp.float32
    )
    for grad_low, weight in (
        (grad_query_low, query_weight),
        (grad_key_low, key_weight),
        (grad_value_low, value_weight),
    ):
        picked = grad_low
        summed_rows = summed_rows + lax.dot_general(
            picked, weight, contract_cols, preferred_element_type=jnp.float32
        )
    grad_first = lax.psum_scatter(
        summed_rows.astype(jnp.bfloat16), "tensor", scatter_dimension=0, tiled=True
    ).astype(jnp.float32)
    _, first_back = jax.vjp(normed, inputs, first_gain)
    input_part, first_gain_grad = first_back(grad_first)
    input_grad = grad_middle + input_part
    grads = (query_grad, key_grad, value_grad, out_grad, gate_grad, up_grad, down_grad)
    joined = jnp.concatenate([grad.astype(jnp.bfloat16) for grad in grads], axis=1)
    summed = lax.psum_scatter(joined, "dp", scatter_dimension=0, tiled=True).astype(jnp.float32)
    edges = []
    for grad in grads[:-1]:
        edges.append((edges[-1] if edges else 0) + grad.shape[1])
    query_grad, key_grad, value_grad, out_grad, gate_grad, up_grad, down_grad = jnp.split(
        summed, edges, axis=1
    )
    table_grad = lax.psum(table_grad, "dp")
    first_gain_grad, second_gain_grad = lax.psum(
        (first_gain_grad, second_gain_grad), ("dp", "tensor")
    )
    return (
        layer_out.astype(jnp.bfloat16),
        input_grad.astype(jnp.bfloat16),
        first_gain_grad,
        query_grad,
        key_grad,
        value_grad,
        out_grad,
        table_grad,
        second_gain_grad,
        gate_grad,
        up_grad,
        down_grad,
    )


def solution(mesh):
    return jax.shard_map(
        per_device,
        mesh=mesh,
        in_specs=(
            P(("dp", "tensor"), None),
            P(),
            P(None, "tensor"),
            P(None, "tensor"),
            P(None, "tensor"),
            P(None, "tensor"),
            P(None, "tensor"),
            P(),
            P(None, "tensor"),
            P(None, "tensor"),
            P(None, "tensor"),
            P("dp", None),
            P(),
            P(("dp", "tensor"), None),
        ),
        out_specs=(
            P(("dp", "tensor"), None),
            P(("dp", "tensor"), None),
            P(),
            P("dp", "tensor"),
            P("dp", "tensor"),
            P("dp", "tensor"),
            P("dp", "tensor"),
            P(None, "tensor"),
            P(),
            P("dp", "tensor"),
            P("dp", "tensor"),
            P("dp", "tensor"),
        ),
        check_vma=False,
    )
```

time: 1700 us -> 710 us (0.42); the launches traced: 1670 us -> 701 us
  local copies, waits for them, and re-layouts: 650 us -> 38.3 us
  waiting for transfers between devices: 729 us -> 461 us
  matrix products: 145 us -> 81.5 us
  other arithmetic: 58.7 us -> 19.6 us
  Pallas kernels: 0 us -> 25.7 us
    reduce_scatter x6 -> x0, waiting for transfers between devices: 302 us -> none  [the longest x1 65.9 us: per_device(): lax.psum_scatter(up_grad, 'dp', scatter_dimension=0, tiled=True)]
    rev x6 -> x0, local copies, waits for them, and re-layouts: 286 us -> none  [the longest x4 194 us: bias_rows(): return jnp.flip(skewed, axis=1)]
    while x54 -> x0, local copies, waits for them, and re-layouts: 172 us -> none
    another operation x8 -> x0, local copies, waits for them, and re-layouts: 75.5 us -> none  [bias_rows(): tiled = jnp.tile(window, (1, QBLK + 1))[:, :QBLK * (width + 1)]]
    slice x8 -> x1, local copies, waits for them, and re-layouts: 58 us -> 0.07 us  [per_device(): distance_sums[None, :, 1:width + 1]]
    dot_general x16 -> x0, matrix products: 43.3 us -> none  [the longest x4 21 us: block_scores(): jnp.einsum('qhd,khd->hqk', query_block, key_seq, preferred_element_type=j...]
    reshape x2 -> x0, local copies, waits for them, and re-layouts: 32.9 us -> none  [diagonal_sums(): return jnp.sum(flat.reshape(heads, QBLK + 1, width), axis=1)]
    unnamed x16 -> x10, waiting for transfers between devices: 61.8 us -> 88.5 us
  transfers between devices with their start and end apart: 15 -> 9, of which waited for: 14 -> 8; matrix products, arithmetic and copies ran while one was open for 5% -> 9% of each run, Pallas kernels for 0% -> 0%
where the time goes in v1:
time: 710 us; the launch traced here: 701 us
  waiting for transfers between devices  461 us (65%)
  matrix products  81.5 us (11%)
  blocking collectives  58.7 us (8%)
  local copies, waits for them, and re-layouts  38.3 us (5%)
  Pallas kernels  25.7 us (4%)
  other arithmetic  19.6 us (3%)
  between operations  14.5 us (2%)
    unnamed x10, waiting for transfers between devices  88.5 us
    all_gather x1, waiting for transfers between devices, per_device(): first_all = lax.all_gather(norm_first, 'tensor', axis=0, tiled=True)  65 us
    all_gather x1, waiting for transfers between devices, per_device(): lax.all_gather(grad_middle.astype(jnp.bfloat16), 'tensor', axis=0, tiled=...  63.5 us
    all_gather x1, waiting for transfers between devices, per_device(): second_all = lax.all_gather(norm_second, 'tensor', axis=0, tiled=True)  62.6 us
    reduce_scatter x1, waiting for transfers between devices, per_device(): lax.psum_scatter(lax.dot_general(picked, out_weight, contract_cols, prefe...  59 us
    reduce_scatter x1, waiting for transfers between devices, per_device(): lax.psum_scatter((summed_rows + lax.dot_general(grad_up_low, up_weight, c...  59 us
    all_gather x1, waiting for transfers between devices, per_device(): grad_all = lax.all_gather(cotangent, 'tensor', axis=0, tiled=True)  50.5 us
    psum x1, blocking collectives, per_device(): lax.psum((first_gain_grad, second_gain_grad), ('dp', 'tensor'))  44.6 us
  transfers between devices with their start and end apart: 9, of which 8 were waited for; matrix products, arithmetic and copies ran while one was open for 9% of the time, Pallas kernels for 0%

profile of v1, /device:TPU:0, one launch (start us, length us, event | category | flops | bytes accessed | tf_op | source)
XLA Modules:
  0.0 701.0 jit_solution(18384529516528612866)
XLA Ops:
  12.4 65.0 %all-gather.5.cloned.1.call-done = bf16[1024,1536]{1,0:T(8,128)(2,1)} async-done(((bf16[256,1536]{1,0:T(8,128)(2,1)}), bf16[1024,1536]{1,0:T(8,128)(2,1)}) %all-gather.5.cloned.1.call-update) | async-done | bytes 3145744 | tf_op jit(solution)/shard_map/all_gather | solution.py:201
  77.4 3.9 convolution_convert_fusion.9.v_ref
  85.0 12.2 %attend.1 = (bf16[1024,192]{1,0:T(8,128)(2,1)}, bf16[3,512,512]{2,1,0:T(8,128)(2,1)}, bf16[3,512,1024]{2,1,0:T(8,128)(2,1)}) custom-call(bf16[1024,192]{1,0:T(8,128)(2,1)} %convolution_convert_fusion.11.q_ref, bf16[1024,192]{1,0:T(8,128)(2,1)} %convolution_convert_fusion.10.k_ref, bf16[1024,192]{1,0:T(8,128)(2,1)} %convolution_convert_fusion.9.v_ref, ...), custom_call_target="tpu_custom_call" | custom-call | tf_op jit(solution)/shard_map/attend/pallas_call | solution.py:145
  97.2 3.6 convolution_convert_fusion
  100.9 59.0 %reduce-scatter.8.cloned.1.call-done = bf16[256,1536]{1,0:T(8,128)(2,1)} async-done(((bf16[1024,1536]{1,0:T(8,128)(2,1)}), bf16[256,1536]{1,0:T(8,128)(2,1)}) %reduce-scatter.8.cloned.1.call-update) | async-done | bytes 786448 | tf_op jit(solution)/shard_map/reduce_scatter | solution.py:215
  161.7 2.5 multiply_convert_fusion.2
  165.3 62.6 %all-gather.7.cloned.1.call-done = bf16[1024,1536]{1,0:T(8,128)(2,1)} async-done(((bf16[256,1536]{1,0:T(8,128)(2,1)}), bf16[1024,1536]{1,0:T(8,128)(2,1)}) %all-gather.7.cloned.1.call-update) | async-done | bytes 3145744 | tf_op jit(solution)/shard_map/all_gather | solution.py:224
  227.9 8.2 %fusion.34 = f32[1024,992]{0,1:T(8,128)} fusion(bf16[1024,1536]{1,0:T(8,128)(2,1)} %all-gather.7.cloned.1.call-done, bf16[1536,992]{0,1:T(8,128)(2,1)} %param.23), kind=kOutput, calls=%fused_computation.74 | convolution fusion | flops 3120562176 | bytes 10256384 | tf_op jit(solution)/shard_map/dot_general | solution.py:226
  236.2 4.8 fusion.33
  241.0 50.5 %all-gather.9.cloned.1.call-done = bf16[1024,1536]{1,0:T(8,128)(2,1)} async-done(((bf16[256,1536]{1,0:T(8,128)(2,1)}), bf16[1024,1536]{1,0:T(8,128)(2,1)}) %all-gather.9.cloned.1.call-update) | async-done | bytes 3145744 | tf_op jit(solution)/shard_map/all_gather | solution.py:238
  291.5 10.4 %multiply_convert_fusion = (bf16[1024,992]{0,1:T(8,128)(2,1)S(1)}, bf16[1024,992]{0,1:T(8,128)(2,1)S(1)}, bf16[1024,992]{0,1:T(8,128)(2,1)}) fusion(f32[1024,992]{0,1:T(8,128)} %fusion.33, f32[1024,992]{0,1:T(8,128)} %fusion.34, bf16[1024,1536]{1,0:T(8,128)(2,1)} %all-gather.9.cloned.1.call-done, bf16[1536,992]{0,1:T(8,128)(2,1)S(1)} %copy-done), kind=kOutput, calls=%fused_computation.11 | convolution fusion | flops 3146973184 | bytes 20414464 | tf_op jit(solution)/shard_map/dot_general | solution.py:242
  302.0 3.5 fusion.35
  305.5 5.2 add_convert_fusion.1
  310.8 59.0 %reduce-scatter.12.cloned.1.call-done = bf16[256,1536]{1,0:T(8,128)(2,1)} async-done(((bf16[1024,1536]{1,0:T(8,128)(2,1)}), bf16[256,1536]{1,0:T(8,128)(2,1)}) %reduce-scatter.12.cloned.1.call-update) | async-done | bytes 786448 | tf_op jit(solution)/shard_map/reduce_scatter | solution.py:255
  372.1 3.3 fusion.30
  375.7 63.5 %all-gather.11.cloned.1.call-done = bf16[1024,1536]{1,0:T(8,128)(2,1)} async-done(((bf16[256,1536]{1,0:T(8,128)(2,1)}), bf16[1024,1536]{1,0:T(8,128)(2,1)}) %all-gather.11.cloned.1.call-update) | async-done | bytes 3145744 | tf_op jit(solution)/shard_map/all_gather | solution.py:269
  439.1 3.2 convolution_convert_fusion.12
  443.3 13.5 %attend_back.1 = (bf16[1024,192]{1,0:T(8,128)(2,1)}, bf16[1024,192]{1,0:T(8,128)(2,1)}, bf16[1024,192]{1,0:T(8,128)(2,1)}, f32[3,1536]{1,0:T(4,128)}) custom-call(bf16[1024,192]{1,0:T(8,128)(2,1)} %convolution_convert_fusion.11.q_ref, bf16[1024,192]{1,0:T(8,128)(2,1)} %convolution_convert_fusion.10.k_ref, bf16[1024,192]{1,0:T(8,128)(2,1)} %convolution_convert_fusion.9.v_ref, ...), custom_call_target="tpu_custom_call" | custom-call | tf_op jit(solution)/shard_map/attend_back/pallas_call | solution.py:164
  460.2 2.6 add_convert_fusion
  463.1 6.5 convolution_convert_fusion.1
  470.7 3.7 fusion.11
  481.1 4.7 fusion.8
  485.8 4.8 fusion.7
  490.6 4.7 fusion.10
  495.3 15.4 %copy.77 = bf16[1536,3744]{1,0:T(8,128)(2,1)} copy(bf16[1536,3744]{0,1:T(8,128)(2,1)} %fusion.10) | data formatting | bytes 23003136
  511.6 14.2 %psum.22 = f32[32,3]{0,1:T(4,128)} all-reduce(f32[32,3]{0,1:T(4,128)S(1)} %select_reduce_fusion), channel_id=1, replica_groups=mesh['dp'=8,'tensor'=4] {'dp'}, use_global_device_ids=true, to_apply=%region_12.13 | all-reduce | flops 96 | bytes 768 | tf_op jit(solution)/shard_map/psum | solution.py:320
  527.6 44.6 %all-reduce.1 = (f32[1536]{0:T(1024)}, f32[1536]{0:T(1024)}) all-reduce(f32[1536]{0:T(1024)S(1)} %get-tuple-element.76, f32[1536]{0:T(1024)S(1)} %get-tuple-element.74), channel_id=1, replica_groups=mesh['dp'=8,'tensor'=4] {'dp','tensor'}, use_global_device_ids=true, to_apply=%region_9.10 | all-reduce | flops 3072 | bytes 24576 | tf_op jit(solution)/shard_map/psum | solution.py:321
  572.2 13.3 %reduce-scatter.10.cloned.1.call-done = bf16[256,1536]{1,0:T(8,128)(2,1)} async-done(((bf16[1024,1536]{1,0:T(8,128)(2,1)}), bf16[256,1536]{1,0:T(8,128)(2,1)}) %reduce-scatter.10.cloned.1.call-update) | async-done | bytes 786448 | tf_op jit(solution)/shard_map/reduce_scatter | solution.py:230
  585.5 3.9 fusion.25
  589.4 87.8 %reduce-scatter.16.cloned.1.call-done = bf16[192,3744]{1,0:T(8,128)(2,1)} async-done(((bf16[1536,3744]{1,0:T(8,128)(2,1)}), bf16[192,3744]{1,0:T(8,128)(2,1)}) %reduce-scatter.16.cloned.1.call-update) | async-done | bytes 1437712
  677.2 2.9 copy.78
  686.8 2.4 copy.73
  (121 shorter events, 41.0 us)
Async XLA Ops:
  7.2 284.4 %copy-start = (bf16[1536,992]{0,1:T(8,128)(2,1)S(1)}, bf16[1536,992]{0,1:T(8,128)(2,1)}, u32[]{:S(2)}) copy-start(bf16[1536,992]{0,1:T(8,128)(2,1)} %param.24) | copy-start | bytes 9142276
  7.2 3.9 copy-start.21
  7.2 4.6 copy-start.19
  7.2 70.2 %all-gather.5.cloned.1.call-start = ((), (), s32[]{:S(2)}) async-start(), calls=%async_computation.5 | async-start | bytes 3932160 | tf_op jit(solution)/shard_map/all_gather | solution.py:201
  11.1 148.9 %reduce-scatter.8.cloned.1.call-start = ((), (), s32[]{:S(2)}) async-start(), calls=%async_computation.6 | async-start | bytes 3932160 | tf_op jit(solution)/shard_map/reduce_scatter | solution.py:215
  77.4 3.9 copy-start.13
  77.4 3.9 copy-start.22
  83.2 14.0 %copy-start.10 = (bf16[1536,192]{0,1:T(8,128)(2,1)S(1)}, bf16[1536,192]{0,1:T(8,128)(2,1)}, u32[]{:S(2)}) copy-start(bf16[1536,192]{0,1:T(8,128)(2,1)} %param.19) | copy-start | bytes 1769476
  100.8 60.8 %copy-start.17 = (f32[1536]{0:T(1024)S(1)}, f32[1536]{0:T(1024)}, u32[]{:S(2)}) copy-start(f32[1536]{0:T(1024)} %param.21) | copy-start | bytes 18436
  100.8 127.1 %all-gather.7.cloned.1.call-start = ((), (), s32[]{:S(2)}) async-start(), calls=%async_computation.7 | async-start | bytes 3932160 | tf_op jit(solution)/shard_map/all_gather | solution.py:224
  164.2 127.3 %all-gather.9.cloned.1.call-start = ((), (), s32[]{:S(2)}) async-start(), calls=%async_computation.9 | async-start | bytes 3932160 | tf_op jit(solution)/shard_map/all_gather | solution.py:238
  164.8 205.0 %reduce-scatter.12.cloned.1.call-start = ((), (), s32[]{:S(2)}) async-start(), calls=%async_computation.10 | async-start | bytes 3932160 | tf_op jit(solution)/shard_map/reduce_scatter | solution.py:255
  227.9 8.2 %copy-start.24 = (bf16[1024,1536]{1,0:T(8,128)(2,1)S(1)}, bf16[1024,1536]{1,0:T(8,128)(2,1)}, u32[]{:S(2)}) copy-start(bf16[1024,1536]{1,0:T(8,128)(2,1)} %all-gather.7.cloned.1.call-done) | copy-start | bytes 9437188
  227.9 8.2 %copy-start.28 = (bf16[1536,992]{0,1:T(8,128)(2,1)S(1)}, bf16[1536,992]{0,1:T(8,128)(2,1)}, u32[]{:S(2)}) copy-start(bf16[1536,992]{0,1:T(8,128)(2,1)} %param.22) | copy-start | bytes 9142276
  291.5 10.4 %copy-start.29 = (bf16[1536,992]{0,1:T(8,128)(2,1)S(1)}, bf16[1536,992]{0,1:T(8,128)(2,1)}, u32[]{:S(2)}) copy-start(bf16[1536,992]{0,1:T(8,128)(2,1)} %param.22) | copy-start | bytes 9142276
  301.9 3.5 copy-start.33
  301.9 3.5 copy-start.30
  310.7 128.4 %all-gather.11.cloned.1.call-start = ((), (), s32[]{:S(2)}) async-start(), calls=%async_computation.11 | async-start | bytes 3932160 | tf_op jit(solution)/shard_map/all_gather | solution.py:269
  375.4 150.3 %reduce-scatter.14.cloned.1.call-start = ((), (), s32[]{:S(2)}) async-start(), calls=%async_computation.12 | async-start | bytes 3932160 | tf_op jit(solution)/shard_map/reduce_scatter | solution.py:305
  443.3 13.5 %copy-start.12 = (bf16[1536,192]{0,1:T(8,128)(2,1)S(1)}, bf16[1536,192]{0,1:T(8,128)(2,1)}, u32[]{:S(2)}) copy-start(bf16[1536,192]{0,1:T(8,128)(2,1)} %param.16) | copy-start | bytes 1769476
  462.8 122.7 %reduce-scatter.10.cloned.1.call-start = ((), (), s32[]{:S(2)}) async-start(), calls=%async_computation.8 | async-start | bytes 3932160 | tf_op jit(solution)/shard_map/reduce_scatter | solution.py:230
  469.6 4.7 copy-start.7
  469.6 207.6 %reduce-scatter.16.cloned.1.call-start = ((), (), s32[]{:S(2)}) async-start(), calls=%async_computation.13 | async-start | bytes 13271040
  470.7 3.7 copy-start.23
  481.1 4.7 copy-start.34
  485.8 4.8 copy-start.26
  485.8 4.8 copy-start.35
  510.6 15.1 %copy-start.2 = (bf16[256,1536]{1,0:T(8,128)(2,1)S(1)}, bf16[256,1536]{1,0:T(8,128)(2,1)}, u32[]{:S(2)}) copy-start(bf16[256,1536]{1,0:T(8,128)(2,1)} %param.14) | copy-start | bytes 2359300
  510.6 15.1 %copy-start.18 = (f32[1536]{0:T(1024)S(1)}, f32[1536]{0:T(1024)}, u32[]{:S(2)}) copy-start(f32[1536]{0:T(1024)} %param.15) | copy-start | bytes 18436
  510.6 74.9 %copy-start.3 = (bf16[256,1536]{1,0:T(8,128)(2,1)S(1)}, bf16[256,1536]{1,0:T(8,128)(2,1)}, u32[]{:S(2)}) copy-start(bf16[256,1536]{1,0:T(8,128)(2,1)} %reduce-scatter.8.cloned.1.call-done) | copy-start | bytes 2359300
  510.6 74.9 %copy-start.4 = (bf16[256,1536]{1,0:T(8,128)(2,1)S(1)}, bf16[256,1536]{1,0:T(8,128)(2,1)}, u32[]{:S(2)}) copy-start(bf16[256,1536]{1,0:T(8,128)(2,1)} %param.27) | copy-start | bytes 2359300
  683.4 10.7 %copy-start.1 = (bf16[1536,992]{0,1:T(8,128)(2,1)S(1)}, bf16[1536,992]{0,1:T(8,128)(2,1)}, u32[]{:S(2)}) copy-start(bf16[1536,992]{0,1:T(8,128)(2,1)} %param.24) | copy-start | bytes 9142276
  (13 other events, 24.2 us)
Sparse Core Ops, SparseCore 0:
  11.2 66.1 all-gather.4
  101.0 58.9 reduce-scatter.7
  164.3 63.5 all-gather.6
  229.3 62.1 all-gather.8
  310.8 58.8 reduce-scatter.11
  375.6 63.5 all-gather.10
  463.0 58.8 reduce-scatter.13
  524.2 61.2 reduce-scatter.9
  589.0 88.1 reduce-scatter.15

commit v2 on v1

--- a/solution.py
+++ b/solution.py
@@ -19,6 +19,7 @@
 EPSILON = 1e-06
 MASKED = -1000000000.0
 VMEM_LIMIT = 60 * 1024 * 1024
+MESH = pl.DeviceIdType.MESH
 
 
 def normed(row_block, gain_vec):
@@ -63,30 +64,224 @@
     return (key <= query) | ((query_label == key_label) & (query_label > 0))
 
 
-def attend_kernel(heads, head_dim, q_ref, k_ref, v_ref, bucket_ref, table_ref, start_ref, att_ref, low_ref, high_ref, bias_ref):
+def attend_block(block, head_dim, allowed, qkv_ref, bias_ref, low_ref, high_ref):
+    keys = key_count(block)
+    first = LEN - QB - block * QB
+    rows = pl.ds(block * QB, QB)
+    outs = []
+    for head in range(bias_ref.shape[0]):
+        cols = pl.ds(head * head_dim, head_dim)
+        raw = dot(qkv_ref[0, rows, cols], qkv_ref[1, pl.ds(0, keys), cols], ((1,), (1,)))
+        scores = jnp.where(allowed, raw + bias_ref[head, :, pl.ds(first, keys)], MASKED)
+        peak = jnp.max(scores, axis=-1, keepdims=True)
+        powered = jnp.exp(scores - peak)
+        total = jnp.sum(powered, axis=-1, keepdims=True)
+        probs = (powered * (1.0 / total)).astype(jnp.bfloat16)
+        if keys == HALF:
+            low_ref[head, rows, :] = probs
+        else:
+            high_ref[head, pl.ds(block * QB - HALF, QB), :] = probs
+        outs.append(dot(probs, qkv_ref[2, pl.ds(0, keys), cols], ((1,), (0,))))
+    return jnp.concatenate(outs, axis=1).astype(jnp.bfloat16)
+
+
+def greet(t, nt):
+    barrier = pltpu.get_barrier_semaphore()
+    for k in range(1, nt):
+        pl.semaphore_signal(
+            barrier, inc=1, device_id={"tensor": lax.rem(t + k, nt)}, device_id_type=MESH
+        )
+    return barrier
+
+
+def line_copy(t, nt, way, step, buf, piece, pieces, send_sem, recv_sem):
+    sign = 1 if way == 0 else -1
+    origin = jnp.clip(t - sign * step, 0, nt - 1)
+    rows = buf.shape[1] // pieces
+    part = buf.at[origin, pl.ds(piece * rows, rows)]
+    return pltpu.make_async_remote_copy(
+        src_ref=part,
+        dst_ref=part,
+        send_sem=send_sem,
+        recv_sem=recv_sem,
+        device_id={"tensor": jnp.clip(t + sign, 0, nt - 1)},
+        device_id_type=MESH,
+    )
+
+
+def gather_attend_kernel(
+    nt, pieces, heads, head_dim,
+    x_ref, cot_ref, gain_ref, wq_ref, wk_ref, wv_ref, bucket_ref, table_ref, start_ref,
+    first_out, cot_out, qkv_out, low_out, high_out, own_out, att_out,
+    first, qkv, low, high, bias, att,
+    send_sem, recv_sem, swap_send, swap_recv, local_sem,
+):
+    t = lax.axis_index("tensor")
+    barrier = greet(t, nt)
+    own_cot = pltpu.make_async_copy(cot_ref, cot_out.at[t], local_sem.at[0])
+    own_cot.start()
+    first[t] = normed(x_ref[...].astype(jnp.float32), gain_ref[...]).astype(jnp.bfloat16)
+    pl.semaphore_wait(barrier, nt - 1)
+
+    def copy(way, stage, step, piece):
+        buf = first if stage == 0 else cot_out
+        return line_copy(
+            t, nt, way, step, buf, piece, pieces,
+            send_sem.at[way, stage, step, piece], recv_sem.at[way, stage, step, piece],
+        )
+
+    def landed(way, stage, step, piece):
+        sign = 1 if way == 0 else -1
+        buf = first if stage == 0 else cot_out
+        rows = buf.shape[1] // pieces
+        part = buf.at[jnp.clip(t - sign * step, 0, nt - 1), pl.ds(piece * rows, rows)]
+        pltpu.make_async_remote_copy(
+            src_ref=part, dst_ref=part,
+            send_sem=send_sem.at[way, stage, step - 1, piece],
+            recv_sem=recv_sem.at[way, stage, step - 1, piece],
+            device_id={"tensor": jnp.clip(t + sign, 0, nt - 1)}, device_id_type=MESH,
+        ).wait_recv()
+
+    ways = ((0, t, t < nt - 1), (1, nt - 1 - t, t > 0))
+
+    def tick(k):
+        for piece in range(pieces):
+            for way, last, onward in ways:
+                if k < nt:
+                    @pl.when(k <= last)
+                    def _():
+                        if k > 0:
+                            landed(way, 0, k, piece)
+
+                        @pl.when(onward)
+                        def _():
+                            copy(way, 0, k, piece).start()
+
+                if k > 0:
+                    step = k - last - 1
+
+                    @pl.when((step >= 1) & (step <= last))
+                    def _():
+                        landed(way, 1, step, piece)
+
+                        @pl.when(onward)
+                        def _():
+                            copy(way, 1, step, piece).start()
+
+                    @pl.when((step == 0) & onward)
+                    def _():
+                        copy(way, 0, last, piece).wait_send()
+                        copy(way, 1, 0, piece).start()
+
+    def project(origin):
+        rows = pl.ds(pl.multiple_of(origin * QB, QB), QB)
+        for place, weight in enumerate((wq_ref, wk_ref, wv_ref)):
+            qkv[place, rows, :] = dot(first[origin], weight[...], ((1,), (0,))).astype(jnp.bfloat16)
+
+    tick(0)
+    project(t)
+    for head in range(heads):
+        bias[head] = toeplitz(bucket_ref[...], table_ref, head)
+    own_cot.wait()
+    for k in range(1, nt):
+        tick(k)
+
+        @pl.when(t - k >= 0)
+        def _():
+            project(t - k)
+
+        @pl.when(t + k < nt)
+        def _():
+            project(t + k)
+
     starts = [start_ref[0, piece] for piece in range(NPIECE)]
-    for head in range(heads):
-        bias_ref[head] = toeplitz(bucket_ref[...], table_ref, head)
+    keep = [pltpu.make_async_copy(first, first_out, local_sem.at[1]), pltpu.make_async_copy(qkv, qkv_out, local_sem.at[2])]
+    for one in keep:
+        one.start()
+
+    def swap(block):
+        return pltpu.make_async_remote_copy(
+            src_ref=att.at[block], dst_ref=own_out.at[t],
+            send_sem=swap_send.at[block], recv_sem=swap_recv.at[t],
+            device_id={"tensor": block}, device_id_type=MESH,
+        )
+
+    own_att = pltpu.make_async_copy(att.at[t], own_out.at[t], local_sem.at[3])
     for block in range(LEN // QB):
-        keys = key_count(block)
-        allowed = allowed_block(block, starts)
-        first = LEN - QB - block * QB
-        rows = pl.ds(block * QB, QB)
-        outs = []
-        for head in range(heads):
-            cols = pl.ds(head * head_dim, head_dim)
-            raw = dot(q_ref[rows, cols], k_ref[pl.ds(0, keys), cols], ((1,), (1,)))
-            scores = jnp.where(allowed, raw + bias_ref[head, :, pl.ds(first, keys)], MASKED)
-            peak = jnp.max(scores, axis=-1, keepdims=True)
-            powered = jnp.exp(scores - peak)
-            total = jnp.sum(powered, axis=-1, keepdims=True)
-            probs = (powered * (1.0 / total)).astype(jnp.bfloat16)
-            if keys == HALF:
-                low_ref[head, rows, :] = probs
-            else:
-                high_ref[head, pl.ds(block * QB - HALF, QB), :] = probs
-            outs.append(dot(probs, v_ref[pl.ds(0, keys), cols], ((1,), (0,))))
-        att_ref[rows, :] = jnp.concatenate(outs, axis=1).astype(jnp.bfloat16)
+        att[block] = attend_block(block, head_dim, allowed_block(block, starts), qkv, bias, low, high)
+
+        @pl.when(t != block)
+        def _():
+            swap(block).start()
+
+        @pl.when(t == block)
+        def _():
+            own_att.start()
+
+    late = [
+        pltpu.make_async_copy(low, low_out, local_sem.at[4]),
+        pltpu.make_async_copy(high, high_out, local_sem.at[5]),
+        pltpu.make_async_copy(att, att_out, local_sem.at[6]),
+    ]
+    for one in late:
+        one.start()
+    for k in range(nt, 2 * nt):
+        tick(k)
+    for block in range(nt):
+        @pl.when(t != block)
+        def _():
+            swap(block).wait_send()
+            pltpu.make_async_remote_copy(
+                src_ref=att.at[block], dst_ref=own_out.at[block],
+                send_sem=swap_send.at[block], recv_sem=swap_recv.at[block],
+                device_id={"tensor": block}, device_id_type=MESH,
+            ).wait_recv()
+
+    own_att.wait()
+    for one in keep + late:
+        one.wait()
+    for piece in range(pieces):
+        for way, last, onward in ways:
+            for stage in range(2):
+                for step in range(nt):
+                    @pl.when(onward & ((step < last) if stage == 0 else (step <= last)))
+                    def _():
+                        copy(way, stage, step, piece).wait_send()
+
+
+def gather_attend(nt, tokens, cotangent, gain, weights, bucket_row, table, starts):
+    heads = table.shape[1]
+    inner = weights[0].shape[1]
+    rows, width = tokens.shape
+    low = jnp.bfloat16
+    pieces = 2
+    smem = pl.BlockSpec(memory_space=pltpu.SMEM)
+    hbm = pl.BlockSpec(memory_space=pl.ANY)
+    vmem = pl.BlockSpec(memory_space=pltpu.VMEM)
+    shapes = (
+        (nt, rows, width), (nt, rows, width), (3, LEN, inner), (heads, HALF, HALF), (heads, HALF, LEN),
+        (nt, rows, inner), (nt, rows, inner),
+    )
+    dma = pltpu.SemaphoreType.DMA
+    return pl.pallas_call(
+        functools.partial(gather_attend_kernel, nt, pieces, heads, inner // heads),
+        out_shape=tuple(jax.ShapeDtypeStruct(shape, low) for shape in shapes),
+        in_specs=[vmem, hbm] + [vmem] * 5 + [smem, smem],
+        out_specs=(hbm,) * 7,
+        scratch_shapes=[
+            pltpu.VMEM((nt, rows, width), low),
+            pltpu.VMEM((3, LEN, inner), low),
+            pltpu.VMEM((heads, HALF, HALF), low),
+            pltpu.VMEM((heads, HALF, LEN), low),
+            pltpu.VMEM((heads, QB, SPAN), jnp.float32),
+            pltpu.VMEM((nt, rows, inner), low),
+            dma((2, 2, nt, pieces)), dma((2, 2, nt, pieces)), dma((nt,)), dma((nt,)), dma((7,)),
+        ],
+        compiler_params=pltpu.CompilerParams(
+            vmem_limit_bytes=VMEM_LIMIT, collective_id=0, has_side_effects=True
+        ),
+        name="gather_attend",
+    )(tokens, cotangent, gain[None, :], *weights, bucket_row, table, starts)
 
 
 def fold_diagonals(grid):
@@ -138,25 +333,6 @@
     return [pl.BlockSpec(memory_space=pltpu.VMEM)] * count
 
 
-def attend(query, key, value, bucket_row, table, starts):
-    heads = table.shape[1]
-    inner = query.shape[1]
-    smem = pl.BlockSpec(memory_space=pltpu.SMEM)
-    return pl.pallas_call(
-        functools.partial(attend_kernel, heads, inner // heads),
-        out_shape=(
-            jax.ShapeDtypeStruct(query.shape, jnp.bfloat16),
-            jax.ShapeDtypeStruct((heads, HALF, HALF), jnp.bfloat16),
-            jax.ShapeDtypeStruct((heads, HALF, LEN), jnp.bfloat16),
-        ),
-        in_specs=whole_vmem(4) + [smem, smem],
-        out_specs=tuple(whole_vmem(3)),
-        scratch_shapes=[pltpu.VMEM((heads, QB, SPAN), jnp.float32)],
-        compiler_params=pltpu.CompilerParams(vmem_limit_bytes=VMEM_LIMIT),
-        name="attend",
-    )(query, key, value, bucket_row, table, starts)
-
-
 def attend_back(query, key, value, grad_attended, low, high):
     heads = low.shape[0]
     inner = query.shape[1]
@@ -197,29 +373,23 @@
     contract_rows = (((0,), (0,)), ((), ()))
     bucket_row = jnp.pad(bucket_index, (0, 1))[None, :]
     inputs = tokens.astype(jnp.float32)
-    norm_first = normed(inputs, first_gain).astype(jnp.bfloat16)
-    first_all = lax.all_gather(norm_first, "tensor", axis=0, tiled=True)
-    query_low = jnp.dot(first_all, query_weight, preferred_element_type=jnp.float32).astype(
-        jnp.bfloat16
-    )
-    key_low = jnp.dot(first_all, key_weight, preferred_element_type=jnp.float32).astype(
-        jnp.bfloat16
-    )
-    value_low = jnp.dot(first_all, value_weight, preferred_element_type=jnp.float32).astype(
-        jnp.bfloat16
-    )
-    attended_low, probs_low, probs_high = attend(
-        query_low, key_low, value_low, bucket_row, bucket_table, piece_start
-    )
-    picked = attended_low
-    middle = inputs + lax.psum_scatter(
-        lax.dot_general(
-            picked, out_weight, contract_cols, preferred_element_type=jnp.float32
-        ).astype(jnp.bfloat16),
-        "tensor",
-        scatter_dimension=0,
-        tiled=True,
-    ).astype(jnp.float32)
+    nt = lax.axis_size("tensor")
+    first_all, grad_all, qkv, probs_low, probs_high, attended_own, attended_heads = gather_attend(
+        nt, tokens, cotangent, first_gain, (query_weight, key_weight, value_weight),
+        bucket_row, bucket_table, piece_start,
+    )
+    first_all = first_all.reshape(-1, tokens.shape[1])
+    grad_all = grad_all.reshape(-1, tokens.shape[1])
+    attended_low = attended_heads.reshape(-1, query_weight.shape[1])
+    query_low, key_low, value_low = qkv[0], qkv[1], qkv[2]
+    own_part = out_weight.shape[0] // lax.axis_size("dp")
+    out_all = lax.all_gather(
+        lax.dynamic_slice_in_dim(out_weight, lax.axis_index("dp") * own_part, own_part, 0),
+        ("tensor", "dp"), axis=0, tiled=True,
+    ).reshape(nt, *out_weight.shape)
+    middle = inputs + jnp.einsum(
+        "tri,tdi->rd", attended_own, out_all, preferred_element_type=jnp.float32
+    )
     norm_second = normed(middle, second_gain).astype(jnp.bfloat16)
     second_all = lax.all_gather(norm_second, "tensor", axis=0, tiled=True)
     gate_pre = jnp.dot(second_all, gate_weight, preferred_element_type=jnp.float32)
@@ -235,7 +405,6 @@
         scatter_dimension=0,
         tiled=True,
     ).astype(jnp.float32)
-    grad_all = lax.all_gather(cotangent, "tensor", axis=0, tiled=True)
     down_grad = lax.dot_general(
         grad_all, hidden_low, contract_rows, preferred_element_type=jnp.float32
     )

time: 710 us -> 644 us (0.907)
  waiting for transfers between devices: 461 us -> 288 us
  Pallas kernels: 25.7 us -> 147 us
  local copies, waits for them, and re-layouts: 38.3 us -> 52.6 us
  matrix products: 81.5 us -> 67.6 us
  other arithmetic: 19.6 us -> 12.2 us
    pallas_call x1, Pallas kernels: 12.2 us -> 133 us  [gather_attend(): pl.pallas_call(functools.partial(gather_attend_kernel, nt, pieces, heads,...]
    all_gather x2 -> x1, waiting for transfers between devices: 116 us -> 0.02 us  [per_device(): lax.all_gather(lax.dynamic_slice_in_dim(out_weight, lax.axis_index('dp')...]
    reduce_scatter x1 -> x0, waiting for transfers between devices: 59 us -> none  [per_device(): lax.psum_scatter(lax.dot_general(picked, out_weight, contract_cols, prefe...]
    unnamed x82 -> x78, local copies, waits for them, and re-layouts: 34.2 us -> 42.8 us
    dot_general x4 -> x1, matrix products: 11.1 us -> 3.36 us  [per_device(): jnp.einsum('tri,tdi->rd', attended_own, out_all, preferred_element_type=j...]
    unnamed x10 -> x8, waiting for transfers between devices: 88.5 us -> 88.1 us
  transfers between devices with their start and end apart: 9 -> 7, of which waited for: 8 -> 5; matrix products, arithmetic and copies ran while one was open for 9% -> 10% of each run, Pallas kernels for 0% -> 21%
where the time goes in v2:
time: 644 us; the launch traced here: 638 us
  waiting for transfers between devices  288 us (45%)
  Pallas kernels  147 us (23%)
  matrix products  67.6 us (10%)
  blocking collectives  55.7 us (9%)
  local copies, waits for them, and re-layouts  52.6 us (8%)
  between operations  14.6 us (2%)
  other arithmetic  12.2 us (2%)
    pallas_call x1, Pallas kernels, gather_attend(): pl.pallas_call(functools.partial(gather_attend_kernel, nt, pieces, heads,...  133 us
    unnamed x8, waiting for transfers between devices  88.1 us
    all_gather x1, waiting for transfers between devices, per_device(): second_all = lax.all_gather(norm_second, 'tensor', axis=0, tiled=True)  63.2 us
    all_gather x1, waiting for transfers between devices, per_device(): lax.all_gather(grad_middle.astype(jnp.bfloat16), 'tensor', axis=0, tiled=...  60.9 us
    reduce_scatter x1, waiting for transfers between devices, per_device(): lax.psum_scatter((summed_rows + lax.dot_general(grad_up_low, up_weight, c...  59 us
    unnamed x78, local copies, waits for them, and re-layouts  42.8 us
    psum x1, blocking collectives, per_device(): lax.psum((first_gain_grad, second_gain_grad), ('dp', 'tensor'))  41.1 us
    reduce_scatter x1, waiting for transfers between devices, per_device(): lax.psum_scatter(lax.dot_general(picked, down_weight, contract_cols, pref...  16.7 us
  transfers between devices with their start and end apart: 7, of which 5 were waited for; matrix products, arithmetic and copies ran while one was open for 10% of the time, Pallas kernels for 21%

profile of v2, /device:TPU:0, one launch (start us, length us, event | category | flops | bytes accessed | tf_op | source)
XLA Modules:
  0.0 638.0 jit_solution(15459977741349959038)
XLA Ops:
  17.6 2.2 copy.87.wv_ref
  19.8 133.3 %gather_attend.1 = (bf16[4,256,1536]{2,1,0:T(8,128)(2,1)}, bf16[4,256,1536]{2,1,0:T(8,128)(2,1)}, bf16[3,1024,192]{2,1,0:T(8,128)(2,1)}, bf16[3,512,512]{2,1,0:T...) custom-call(bf16[256,1536]{1,0:T(8,128)(2,1)} %x_ref.1, ...), custom_call_target="tpu_custom_call" | custom-call | tf_op jit(solution)/shard_map/gather_attend/pallas_call | solution.py:266
  153.2 3.4 multiply_reduce_fusion
  159.0 63.2 %all-gather.6.cloned.1.call-done = bf16[1024,1536]{1,0:T(8,128)(2,1)} async-done(((bf16[256,1536]{1,0:T(8,128)(2,1)}), bf16[1024,1536]{1,0:T(8,128)(2,1)}) %all-gather.6.cloned.1.call-update) | async-done | bytes 3145744 | tf_op jit(solution)/shard_map/all_gather | solution.py:394
  222.2 6.3 fusion.31
  228.5 3.3 fusion.30
  231.9 7.3 %multiply_convert_fusion = (bf16[1024,992]{0,1:T(8,128)(2,1)S(1)}, bf16[1024,992]{0,1:T(8,128)(2,1)S(1)}, bf16[1024,992]{0,1:T(8,128)(2,1)}) fusion(f32[1024,992]{0,1:T(8,128)S(1)} %fusion.30, f32[1024,992]{0,1:T(8,128)S(1)} %fusion.31, bf16[1024,1536]{1,0:T(8,128)(2,1)S(1)} %bitcast.56, bf16[1536,992]{0,1:T(8,128)(2,1)S(1)} %copy-done), kind=kOutput, calls=%fused_computation.11 | convolution fusion | flops 3146973184 | bytes 20414464 | tf_op jit(solution)/shard_map/dot_general | solution.py:411
  239.2 3.5 fusion.32
  242.7 5.2 add_convert_fusion.1
  247.9 59.0 %reduce-scatter.9.cloned.1.call-done = bf16[256,1536]{1,0:T(8,128)(2,1)} async-done(((bf16[1024,1536]{1,0:T(8,128)(2,1)}), bf16[256,1536]{1,0:T(8,128)(2,1)}) %reduce-scatter.9.cloned.1.call-update) | async-done | bytes 786448 | tf_op jit(solution)/shard_map/reduce_scatter | solution.py:424
  307.0 2.2 fusion.18
  309.2 2.8 fusion.27
  312.3 2.5 slice_bitcast_fusion
  314.8 60.9 %all-gather.8.cloned.1.call-done = bf16[1024,1536]{1,0:T(8,128)(2,1)} async-done(((bf16[256,1536]{1,0:T(8,128)(2,1)}), bf16[1024,1536]{1,0:T(8,128)(2,1)}) %all-gather.8.cloned.1.call-update) | async-done | bytes 3145744 | tf_op jit(solution)/shard_map/all_gather | solution.py:438
  375.7 3.2 convolution_convert_fusion.8
  379.9 13.5 %attend_back.1 = (bf16[1024,192]{1,0:T(8,128)(2,1)}, bf16[1024,192]{1,0:T(8,128)(2,1)}, bf16[1024,192]{1,0:T(8,128)(2,1)}, f32[3,1536]{1,0:T(4,128)}) custom-call(bf16[1024,192]{1,0:T(8,128)(2,1)} %get-tuple-element.114.q_ref, bf16[1024,192]{1,0:T(8,128)(2,1)} %get-tuple-element.113.k_ref, bf16[1024,192]{1,0:T(8,128)(2,1)} %get-tuple-element.112.v_ref, ...), custom_call_target="tpu_custom_call" | custom-call | tf_op jit(solution)/shard_map/attend_back/pallas_call | solution.py:340
  396.8 3.1 add_convert_fusion
  400.0 6.6 %convolution_convert_fusion = bf16[1024,1536]{1,0:T(8,128)(2,1)} fusion(bf16[1024,992]{0,1:T(8,128)(2,1)} %get-tuple-element.102, bf16[1536,992]{0,1:T(8,128)(2,1)S(1)} %copy-done), kind=kOutput, calls=%fused_computation.14 | convolution fusion | flops 3122135040 | bytes 8224768 | tf_op jit(solution)/shard_map/dot_general | solution.py:401
  407.6 3.7 fusion.10
  417.5 4.6 fusion.9
  422.1 4.7 fusion.8
  426.8 4.8 fusion.7
  431.6 14.9 %copy.104 = bf16[1536,3744]{1,0:T(8,128)(2,1)} copy(bf16[1536,3744]{0,1:T(8,128)(2,1)} %fusion.7) | data formatting | bytes 23003136
  448.2 14.6 %psum.22 = f32[32,3]{0,1:T(4,128)} all-reduce(f32[32,3]{0,1:T(4,128)S(1)} %select_reduce_fusion), channel_id=1, replica_groups=mesh['dp'=8,'tensor'=4] {'dp'}, use_global_device_ids=true, to_apply=%region_11.12 | all-reduce | flops 96 | bytes 768 | tf_op jit(solution)/shard_map/psum | solution.py:489
  464.6 41.1 %all-reduce.1 = (f32[1536]{0:T(1024)}, f32[1536]{0:T(1024)}) all-reduce(f32[1536]{0:T(1024)S(1)} %get-tuple-element.96, f32[1536]{0:T(1024)S(1)} %get-tuple-element.94), channel_id=1, replica_groups=mesh['dp'=8,'tensor'=4] {'dp','tensor'}, use_global_device_ids=true, to_apply=%region_8.9 | all-reduce | flops 3072 | bytes 24576 | tf_op jit(solution)/shard_map/psum | solution.py:490
  505.7 16.7 %reduce-scatter.7.cloned.1.call-done = bf16[256,1536]{1,0:T(8,128)(2,1)} async-done(((bf16[1024,1536]{1,0:T(8,128)(2,1)}), bf16[256,1536]{1,0:T(8,128)(2,1)}) %reduce-scatter.7.cloned.1.call-update) | async-done | bytes 786448 | tf_op jit(solution)/shard_map/reduce_scatter | solution.py:400
  522.4 3.8 fusion.22
  526.2 87.9 %reduce-scatter.13.cloned.1.call-done = bf16[192,3744]{1,0:T(8,128)(2,1)} async-done(((bf16[1536,3744]{1,0:T(8,128)(2,1)}), bf16[192,3744]{1,0:T(8,128)(2,1)}) %reduce-scatter.13.cloned.1.call-update) | async-done | bytes 1437712
  614.2 2.9 copy.105
  623.8 2.4 copy.100
  626.2 2.4 copy.99
  628.6 2.4 copy.98
  (109 shorter events, 35.0 us)
Async XLA Ops:
  7.2 224.7 %copy-start = (bf16[1536,992]{0,1:T(8,128)(2,1)S(1)}, bf16[1536,992]{0,1:T(8,128)(2,1)}, u32[]{:S(2)}) copy-start(bf16[1536,992]{0,1:T(8,128)(2,1)} %param.24) | copy-start | bytes 9142276
  7.2 146.0 %all-gather.4.cloned.1.call-start = ((), (), s32[]{:S(2)}) async-start(), calls=%async_computation.4 | async-start | bytes 3244032 | tf_op jit(solution)/shard_map/all_gather | solution.py:386
  9.2 213.0 %all-gather.6.cloned.1.call-start = ((), (), s32[]{:S(2)}) async-start(), calls=%async_computation.5 | async-start | bytes 3932160 | tf_op jit(solution)/shard_map/all_gather | solution.py:394
  153.1 4.6 copy-start.14
  158.8 148.1 %reduce-scatter.9.cloned.1.call-start = ((), (), s32[]{:S(2)}) async-start(), calls=%async_computation.7 | async-start | bytes 3932160 | tf_op jit(solution)/shard_map/reduce_scatter | solution.py:424
  222.2 6.3 copy-start.21
  222.2 6.3 copy-start.24
  228.5 3.4 copy-start.18
  239.2 3.5 copy-start.27
  239.2 3.5 copy-start.29
  239.2 3.5 copy-start.25
  247.9 127.8 %all-gather.8.cloned.1.call-start = ((), (), s32[]{:S(2)}) async-start(), calls=%async_computation.8 | async-start | bytes 3932160 | tf_op jit(solution)/shard_map/all_gather | solution.py:438
  307.0 2.3 copy-start.3
  312.0 150.8 %reduce-scatter.11.cloned.1.call-start = ((), (), s32[]{:S(2)}) async-start(), calls=%async_computation.9 | async-start | bytes 3932160 | tf_op jit(solution)/shard_map/reduce_scatter | solution.py:474
  379.9 13.6 %copy-start.7 = (bf16[1536,192]{0,1:T(8,128)(2,1)S(1)}, bf16[1536,192]{0,1:T(8,128)(2,1)}, u32[]{:S(2)}) copy-start(bf16[1536,192]{0,1:T(8,128)(2,1)} %param.16) | copy-start | bytes 1769476
  393.4 2.1 copy-start.8
  393.4 2.1 copy-start.9
  399.9 122.5 %reduce-scatter.7.cloned.1.call-start = ((), (), s32[]{:S(2)}) async-start(), calls=%async_computation.6 | async-start | bytes 3932160 | tf_op jit(solution)/shard_map/reduce_scatter | solution.py:400
  406.6 207.6 %reduce-scatter.13.cloned.1.call-start = ((), (), s32[]{:S(2)}) async-start(), calls=%async_computation.10 | async-start | bytes 13271040
  407.6 3.7 copy-start.10
  407.6 3.7 copy-start.20
  411.3 1.7 copy-start.13
  412.9 2.1 copy-start.23
  413.0 2.2 copy-start.26
  414.6 2.2 copy-start.22
  414.6 2.8 copy-start.28
  417.5 4.6 copy-start.30
  422.1 4.7 copy-start.19
  422.1 4.7 copy-start.31
  446.5 16.3 %copy-start.15 = (f32[1536]{0:T(1024)S(1)}, f32[1536]{0:T(1024)}, u32[]{:S(2)}) copy-start(f32[1536]{0:T(1024)} %param.15) | copy-start | bytes 18436
  447.7 74.7 %copy-start.4 = (f32[256,1536]{1,0:T(8,128)S(1)}, f32[256,1536]{1,0:T(8,128)}, u32[]{:S(2)}) copy-start(f32[256,1536]{1,0:T(8,128)} %copy-done.2) | copy-start | bytes 4718596
  620.3 10.7 %copy-start.1 = (bf16[1536,992]{0,1:T(8,128)(2,1)S(1)}, bf16[1536,992]{0,1:T(8,128)(2,1)}, u32[]{:S(2)}) copy-start(bf16[1536,992]{0,1:T(8,128)(2,1)} %param.24) | copy-start | bytes 9142276
  (7 other events, 8.4 us)
Sparse Core Ops, SparseCore 0:
  11.5 66.0 all-gather.3
  158.9 63.2 all-gather.5
  248.0 58.8 reduce-scatter.8
  312.2 63.5 all-gather.7
  400.0 58.8 reduce-scatter.10
  461.1 61.2 reduce-scatter.6
  525.9 88.2 reduce-scatter.12

commit v3 on v2

--- a/solution.py
+++ b/solution.py
@@ -25,10 +25,6 @@
 def normed(row_block, gain_vec):
     inv_rms = lax.rsqrt(jnp.mean(row_block * row_block, axis=-1, keepdims=True) + EPSILON)
     return row_block * inv_rms * gain_vec
-
-
-def gelu_tanh(values):
-    return jax.nn.gelu(values, approximate=True)
 
 
 def dot(a, b, dims):
@@ -176,7 +172,7 @@
     def project(origin):
         rows = pl.ds(pl.multiple_of(origin * QB, QB), QB)
         for place, weight in enumerate((wq_ref, wk_ref, wv_ref)):
-            qkv[place, rows, :] = dot(first[origin], weight[...], ((1,), (0,))).astype(jnp.bfloat16)
+            qkv[place, rows, :] = dot(first[origin], weight[...], ((1,), (1,))).astype(jnp.bfloat16)
 
     tick(0)
     project(t)
@@ -251,7 +247,7 @@
 
 def gather_attend(nt, tokens, cotangent, gain, weights, bucket_row, table, starts):
     heads = table.shape[1]
-    inner = weights[0].shape[1]
+    inner = weights[0].shape[0]
     rows, width = tokens.shape
     low = jnp.bfloat16
     pieces = 2
@@ -291,6 +287,276 @@
         grid = grid[:rows] + pltpu.roll(grid[rows : 2 * rows], width - rows, 1)
         rows //= 2
     return grid
+
+
+def gelu_parts(v):
+    root, cubic = 0.7978845608028654, 0.044715
+    square = v * v
+    bend = jnp.tanh(root * v * (1.0 + cubic * square))
+    half = 0.5 * (1.0 + bend)
+    slope = half + 0.5 * v * (1.0 - bend * bend) * root * (1.0 + 3.0 * cubic * square)
+    return v * half, slope
+
+
+def feed_kernel(
+    nt, pieces,
+    x_ref, own_ref, wo_ref, gain_ref, cot_own_ref, cot_hbm, wg_hbm, wu_hbm, wd_hbm,
+    middle_out, gm_out, gain_out, ga_out, lo_out, grads_out,
+    buf, cot, wg, wu, wd, hid, gg, gu, gs, lo, mate_in, acc_in, far_in, middle, grads,
+    send_sem, recv_sem, rs_send, rs_recv, local_sem,
+):
+    t = lax.axis_index("tensor")
+    barrier = greet(t, nt)
+    loads = [
+        pltpu.make_async_copy(a, b, local_sem.at[i])
+        for i, (a, b) in enumerate(((wg_hbm, wg), (wu_hbm, wu), (wd_hbm, wd), (cot_hbm, cot)))
+    ]
+    for one in loads:
+        one.start()
+    row_count = x_ref.shape[0]
+    size = row_count // pieces
+    total = x_ref[...].astype(jnp.float32)
+    for j in range(nt):
+        total = total + dot(own_ref[j], wo_ref[j], ((1,), (0,)))
+    middle[...] = total
+    buf[t] = normed(total, gain_ref[...]).astype(jnp.bfloat16)
+    keep = [pltpu.make_async_copy(middle, middle_out, local_sem.at[4])]
+    keep[0].start()
+    pl.semaphore_wait(barrier, nt - 1)
+    mate = t + 1 - 2 * lax.rem(t, 2)
+    is_end = (t == 0) | (t == nt - 1)
+    ways = ((0, t, t < nt - 1), (1, nt - 1 - t, t > 0))
+
+    def copy(way, step, piece):
+        return line_copy(
+            t, nt, way, step, buf, piece, pieces,
+            send_sem.at[way, step, piece], recv_sem.at[way, step, piece],
+        )
+
+    def landed(way, step, piece):
+        sign = 1 if way == 0 else -1
+        part = buf.at[jnp.clip(t - sign * step, 0, nt - 1), pl.ds(piece * size, size)]
+        pltpu.make_async_remote_copy(
+            src_ref=part, dst_ref=part,
+            send_sem=send_sem.at[way, step - 1, piece], recv_sem=recv_sem.at[way, step - 1, piece],
+            device_id={"tensor": jnp.clip(t + sign, 0, nt - 1)}, device_id_type=MESH,
+        ).wait_recv()
+
+    def remote(src, dst, target, send, recv):
+        return pltpu.make_async_remote_copy(
+            src_ref=src, dst_ref=dst, send_sem=send, recv_sem=recv,
+            device_id={"tensor": target}, device_id_type=MESH,
+        )
+
+    def to_mate(piece):
+        rows = pl.ds(piece * size, size)
+        return remote(gs.at[mate, rows], mate_in.at[rows], mate, rs_send.at[0, piece], rs_recv.at[0, piece])
+
+    def to_acc(origin, piece):
+        rows = pl.ds(piece * size, size)
+        j = lax.rem(origin, 2)
+        return remote(
+            gs.at[origin, rows], acc_in.at[j, rows], mate, rs_send.at[1 + j, piece], rs_recv.at[1 + j, piece]
+        )
+
+    def to_far(origin, piece):
+        rows = pl.ds(piece * size, size)
+        j = lax.rem(origin, 2)
+        return remote(
+            gs.at[origin, rows], far_in.at[rows], origin, rs_send.at[3 + j, piece], rs_recv.at[3, piece]
+        )
+
+    def feed(origin, piece):
+        rows = pl.ds(pl.multiple_of(piece * size, size), size)
+        flat = pl.ds(pl.multiple_of(origin * row_count + piece * size, size), size)
+        normal = buf[origin, rows]
+        gate = dot(normal, wg[...], ((1,), (1,)))
+        up = dot(normal, wu[...], ((1,), (1,)))
+        grad_hidden = dot(cot[origin, rows], wd[...], ((1,), (1,)))
+        act, slope = gelu_parts(gate)
+        hid[flat, :] = (act * up).astype(jnp.bfloat16)
+        grad_gate = (grad_hidden * up * slope).astype(jnp.bfloat16)
+        grad_up = (grad_hidden * act).astype(jnp.bfloat16)
+        gg[flat, :] = grad_gate
+        gu[flat, :] = grad_up
+        gs[origin, rows] = (
+            dot(grad_gate, wg[...], ((1,), (0,))) + dot(grad_up, wu[...], ((1,), (0,)))
+        ).astype(jnp.bfloat16)
+
+    for piece in range(pieces):
+        for way, last, onward in ways:
+            @pl.when(onward)
+            def _():
+                copy(way, 0, piece).start()
+
+    for one in loads:
+        one.wait()
+
+    def unit(u, carry):
+        step = u // pieces
+        piece = lax.rem(u, pieces)
+
+        @pl.when(step > 0)
+        def _():
+            for way, last, onward in ways:
+                @pl.when(step <= last)
+                def _():
+                    landed(way, step, piece)
+
+                    @pl.when(onward)
+                    def _():
+                        copy(way, step, piece).start()
+
+        def side(way, carry):
+            origin = t - (1 - 2 * way) * step
+            there = (origin >= 0) & (origin < nt) & ((step > 0) | (way == 0))
+
+            @pl.when(there)
+            def _():
+                feed(origin, piece)
+
+                @pl.when(origin == mate)
+                def _():
+                    to_mate(piece).start()
+
+                @pl.when((origin != mate) & (origin != t) & is_end)
+                def _():
+                    to_acc(origin, piece).start()
+
+            return carry
+
+        return lax.fori_loop(0, 2, side, carry)
+
+    lax.fori_loop(0, nt * pieces, unit, 0)
+
+    near = jnp.where(t < nt // 2, nt // 2, nt // 2 - 1)
+    far = jnp.where(t < nt // 2, nt - 1, 0)
+
+    def pass_on(origin, piece):
+        @pl.when(jnp.logical_not(is_end))
+        def _():
+            to_acc(origin, piece).wait_recv()
+            rows = pl.ds(piece * size, size)
+            j = lax.rem(origin, 2)
+            gs[origin, rows] = (
+                gs[origin, rows].astype(jnp.float32) + acc_in[j, rows].astype(jnp.float32)
+            ).astype(jnp.bfloat16)
+            to_far(origin, piece).start()
+
+    span = 256
+    flat_rows = nt * row_count
+    spans = buf.shape[2] // span
+
+    def columns(ref, i):
+        cols = pl.ds(pl.multiple_of(i * span, span), span)
+        return ref[:, :, cols].reshape(flat_rows, span)
+
+    def down_cols(i, carry):
+        rows = pl.ds(pl.multiple_of(i * span, span), span)
+        grads[2, rows, :] = dot(columns(cot, i), hid[...], ((0,), (0,))).astype(jnp.bfloat16)
+        return carry
+
+    def gate_up_cols(i, carry):
+        rows = pl.ds(pl.multiple_of(i * span, span), span)
+        left = columns(buf, i)
+        grads[0, rows, :] = dot(left, gg[...], ((0,), (0,))).astype(jnp.bfloat16)
+        grads[1, rows, :] = dot(left, gu[...], ((0,), (0,))).astype(jnp.bfloat16)
+        return carry
+
+    def down_rows(i, carry):
+        rows = pl.ds(pl.multiple_of(i * row_count, row_count), row_count)
+        lo[i] = dot(hid[rows, :], wd[...], ((1,), (0,))).astype(jnp.bfloat16)
+        return carry
+
+    pass_on(near, 0)
+    lax.fori_loop(0, spans, down_cols, 0)
+    pass_on(near, 1)
+    lax.fori_loop(0, nt, down_rows, 0)
+    keep.append(pltpu.make_async_copy(lo, lo_out, local_sem.at[5]))
+    keep[-1].start()
+    pass_on(far, 0)
+    lax.fori_loop(0, spans // 2, gate_up_cols, 0)
+    pass_on(far, 1)
+    lax.fori_loop(spans // 2, spans, gate_up_cols, 0)
+    keep.append(pltpu.make_async_copy(grads, grads_out, local_sem.at[6]))
+    keep[-1].start()
+
+    for piece in range(pieces):
+        rows = pl.ds(piece * size, size)
+        to_mate(piece).wait_recv()
+        remote(gs.at[t, rows], far_in.at[rows], mate, rs_send.at[3, piece], rs_recv.at[3, piece]).wait_recv()
+        grad_second = (
+            gs[t, rows].astype(jnp.float32)
+            + mate_in[rows].astype(jnp.float32)
+            + far_in[rows].astype(jnp.float32)
+        )
+        mid = middle[rows]
+        inv = lax.rsqrt(jnp.mean(mid * mid, axis=-1, keepdims=True) + EPSILON)
+        scaled = gain_ref[...] * grad_second
+        along = jnp.mean(scaled * mid, axis=-1, keepdims=True)
+        grad_middle = cot_own_ref[rows].astype(jnp.float32) + inv * scaled - mid * (inv * inv * inv * along)
+        gm_out[rows] = grad_middle
+        part = jnp.sum(grad_second * mid * inv, axis=0, keepdims=True)
+        if piece == 0:
+            gain_out[...] = part
+        else:
+            gain_out[...] += part
+        grad_low = grad_middle.astype(jnp.bfloat16)
+        for j in range(nt):
+            ga_out[j, rows] = dot(grad_low, wo_ref[j], ((1,), (1,))).astype(jnp.bfloat16)
+
+    for one in keep:
+        one.wait()
+    for piece in range(pieces):
+        for way, last, onward in ways:
+            for step in range(nt):
+                @pl.when(onward & (step <= last))
+                def _():
+                    copy(way, step, piece).wait_send()
+
+        to_mate(piece).wait_send()
+        for origin in (near, far):
+            @pl.when(is_end)
+            def _():
+                to_acc(origin, piece).wait_send()
+
+            @pl.when(jnp.logical_not(is_end))
+            def _():
+                to_far(origin, piece).wait_send()
+
+
+def feed(nt, tokens, attended, out_all, gain, cotangent, cot_all, gate_weight, up_weight, down_weight):
+    rows, width = tokens.shape
+    hidden = gate_weight.shape[0]
+    low, full = jnp.bfloat16, jnp.float32
+    pieces = 2
+    hbm = pl.BlockSpec(memory_space=pl.ANY)
+    vmem = pl.BlockSpec(memory_space=pltpu.VMEM)
+    inner = attended.shape[2]
+    dma = pltpu.SemaphoreType.DMA
+    shape = jax.ShapeDtypeStruct
+    return pl.pallas_call(
+        functools.partial(feed_kernel, nt, pieces),
+        out_shape=(
+            shape((rows, width), full), shape((rows, width), full), shape((1, width), full),
+            shape((nt, rows, inner), low), shape((nt, rows, width), low), shape((3, width, hidden), low),
+        ),
+        in_specs=[vmem] * 5 + [hbm] * 4,
+        out_specs=(hbm, vmem, vmem, vmem, hbm, hbm),
+        scratch_shapes=[
+            pltpu.VMEM((nt, rows, width), low), pltpu.VMEM((nt, rows, width), low),
+            pltpu.VMEM((hidden, width), low), pltpu.VMEM((hidden, width), low), pltpu.VMEM((hidden, width), low),
+            pltpu.VMEM((nt * rows, hidden), low), pltpu.VMEM((nt * rows, hidden), low), pltpu.VMEM((nt * rows, hidden), low),
+            pltpu.VMEM((nt, rows, width), low), pltpu.VMEM((nt, rows, width), low),
+            pltpu.VMEM((rows, width), low), pltpu.VMEM((2, rows, width), low), pltpu.VMEM((rows, width), low),
+            pltpu.VMEM((rows, width), full), pltpu.VMEM((3, width, hidden), low),
+            dma((2, nt, pieces)), dma((2, nt, pieces)), dma((5, pieces)), dma((4, pieces)), dma((7,)),
+        ],
+        compiler_params=pltpu.CompilerParams(
+            vmem_limit_bytes=VMEM_LIMIT, collective_id=1, has_side_effects=True
+        ),
+        name="feed",
+    )(tokens, attended, out_all, gain[None, :], cotangent, cot_all, gate_weight, up_weight, down_weight)
 
 
 def attend_back_kernel(heads, head_dim, q_ref, k_ref, v_ref, do_ref, low_ref, high_ref, dq_ref, dk_ref, dv_ref, dist_ref, diag_ref, dk_acc, dv_acc):
@@ -375,73 +641,34 @@
     inputs = tokens.astype(jnp.float32)
     nt = lax.axis_size("tensor")
     first_all, grad_all, qkv, probs_low, probs_high, attended_own, attended_heads = gather_attend(
-        nt, tokens, cotangent, first_gain, (query_weight, key_weight, value_weight),
+        nt, tokens, cotangent, first_gain, (query_weight.T, key_weight.T, value_weight.T),
         bucket_row, bucket_table, piece_start,
     )
     first_all = first_all.reshape(-1, tokens.shape[1])
-    grad_all = grad_all.reshape(-1, tokens.shape[1])
     attended_low = attended_heads.reshape(-1, query_weight.shape[1])
     query_low, key_low, value_low = qkv[0], qkv[1], qkv[2]
-    own_part = out_weight.shape[0] // lax.axis_size("dp")
+    out_cols = out_weight.T
+    own_part = out_cols.shape[0] // lax.axis_size("dp")
     out_all = lax.all_gather(
-        lax.dynamic_slice_in_dim(out_weight, lax.axis_index("dp") * own_part, own_part, 0),
+        lax.dynamic_slice_in_dim(out_cols, lax.axis_index("dp") * own_part, own_part, 0),
         ("tensor", "dp"), axis=0, tiled=True,
-    ).reshape(nt, *out_weight.shape)
-    middle = inputs + jnp.einsum(
-        "tri,tdi->rd", attended_own, out_all, preferred_element_type=jnp.float32
-    )
-    norm_second = normed(middle, second_gain).astype(jnp.bfloat16)
-    second_all = lax.all_gather(norm_second, "tensor", axis=0, tiled=True)
-    gate_pre = jnp.dot(second_all, gate_weight, preferred_element_type=jnp.float32)
-    up_proj = jnp.dot(second_all, up_weight, preferred_element_type=jnp.float32)
-    activated, gelu_back = jax.vjp(gelu_tanh, gate_pre)
-    hidden_low = (activated * up_proj).astype(jnp.bfloat16)
-    picked = hidden_low
+    ).reshape(nt, *out_cols.shape)
+    middle, grad_middle, second_gain_grad, grad_attended_own, layer_parts, feed_grads = feed(
+        nt, tokens, attended_own, out_all, second_gain, cotangent, grad_all,
+        gate_weight.T, up_weight.T, down_weight.T,
+    )
+    second_gain_grad = second_gain_grad[0]
     layer_out = middle + lax.psum_scatter(
-        lax.dot_general(
-            picked, down_weight, contract_cols, preferred_element_type=jnp.float32
-        ).astype(jnp.bfloat16),
-        "tensor",
-        scatter_dimension=0,
-        tiled=True,
+        layer_parts.reshape(-1, tokens.shape[1]), "tensor", scatter_dimension=0, tiled=True
     ).astype(jnp.float32)
-    down_grad = lax.dot_general(
-        grad_all, hidden_low, contract_rows, preferred_element_type=jnp.float32
-    )
-    grad_hidden = jnp.dot(grad_all, down_weight, preferred_element_type=jnp.float32)
-    (grad_act,) = gelu_back(grad_hidden * up_proj)
-    grad_gate_low = grad_act.astype(jnp.bfloat16)
-    grad_up_low = (grad_hidden * activated).astype(jnp.bfloat16)
-    gate_grad = lax.dot_general(
-        second_all, grad_gate_low, contract_rows, preferred_element_type=jnp.float32
-    )
-    up_grad = lax.dot_general(
-        second_all, grad_up_low, contract_rows, preferred_element_type=jnp.float32
-    )
-    summed_rows = lax.dot_general(
-        grad_gate_low, gate_weight, contract_cols, preferred_element_type=jnp.float32
-    )
-    grad_second = lax.psum_scatter(
-        (
-            summed_rows
-            + lax.dot_general(
-                grad_up_low, up_weight, contract_cols, preferred_element_type=jnp.float32
-            )
-        ).astype(jnp.bfloat16),
-        "tensor",
-        scatter_dimension=0,
-        tiled=True,
-    ).astype(jnp.float32)
-    _, second_back = jax.vjp(normed, middle, second_gain)
-    middle_part, second_gain_grad = second_back(grad_second)
-    grad_middle = cotangent.astype(jnp.float32) + middle_part
+    gate_grad, up_grad, down_grad = feed_grads[0], feed_grads[1], feed_grads[2]
     middle_all = lax.all_gather(grad_middle.astype(jnp.bfloat16), "tensor", axis=0, tiled=True)
     out_grad = lax.dot_general(
         middle_all, attended_low, contract_rows, preferred_element_type=jnp.float32
     )
-    grad_attended = jnp.dot(middle_all, out_weight, preferred_element_type=jnp.float32).astype(
-        jnp.bfloat16
-    )
+    grad_attended = lax.all_to_all(
+        grad_attended_own, "tensor", split_axis=0, concat_axis=0, tiled=True
+    ).reshape(-1, query_weight.shape[1])
     grad_query_low, grad_key_low, grad_value_low, distance_sums = attend_back(
         query_low, key_low, value_low, grad_attended, probs_low, probs_high
     )

time: 644 us -> 584 us (0.907)
  waiting for transfers between devices: 288 us -> 179 us
  Pallas kernels: 147 us -> 244 us
  matrix products: 67.6 us -> 18.2 us
    pallas_call x0 -> x1, Pallas kernels: none -> 98.5 us  [feed(): pl.pallas_call(functools.partial(feed_kernel, nt, pieces), out_shape=(sha...]
    unnamed x8 -> x5, waiting for transfers between devices: 88.1 us -> 0.59 us
    all_gather x2 -> x1, waiting for transfers between devices: 63.2 us -> 0.02 us  [per_device(): lax.all_gather(lax.dynamic_slice_in_dim(out_cols, lax.axis_index('dp') *...]
    reduce_scatter x1, waiting for transfers between devices: 0.01 us -> 58.4 us  [per_device(): lax.psum_scatter(summed_rows.astype(jnp.bfloat16), 'tensor', scatter_dime...]
    dot_general x11 -> x0, matrix products: 52.8 us -> none  [the longest x1 7.28 us: per_device(): jnp.dot(grad_all, down_weight, preferred_element_type=jnp.float32)]
    unnamed x78 -> x37, local copies, waits for them, and re-layouts: 42.8 us -> 4.55 us
    all_gather x1, waiting for transfers between devices: 60.9 us -> 40.8 us  [per_device(): lax.all_gather(grad_middle.astype(jnp.bfloat16), 'tensor', axis=0, tiled=...]
    concatenate x0 -> x1, local copies, waits for them, and re-layouts: none -> 19.6 us  [per_device(): jnp.concatenate([grad.astype(jnp.bfloat16) for grad in grads], axis=1)]
  transfers between devices with their start and end apart: 7 -> 6, of which waited for: 5 -> 5; matrix products, arithmetic and copies ran while one was open for 10% -> 10% of each run, Pallas kernels for 21% -> 23%
where the time goes in v3:
time: 584 us; the launch traced here: 574 us
  Pallas kernels  244 us (42%)
  waiting for transfers between devices  179 us (31%)
  blocking collectives  55.2 us (9%)
  local copies, waits for them, and re-layouts  51.9 us (9%)
  matrix products  18.2 us (3%)
  between operations  14.4 us (2%)
  other arithmetic  7.29 us (1%)
    pallas_call x1, Pallas kernels, gather_attend(): pl.pallas_call(functools.partial(gather_attend_kernel, nt, pieces, heads,...  132 us
    pallas_call x1, Pallas kernels, feed(): pl.pallas_call(functools.partial(feed_kernel, nt, pieces), out_shape=(sha...  98.5 us
    reduce_scatter x1, waiting for transfers between devices, per_device(): lax.psum_scatter(summed_rows.astype(jnp.bfloat16), 'tensor', scatter_dime...  58.4 us
    reduce_scatter x1, waiting for transfers between devices, per_device(): lax.psum_scatter(joined, 'dp', scatter_dimension=0, tiled=True)  49.4 us
    all_gather x1, waiting for transfers between devices, per_device(): lax.all_gather(grad_middle.astype(jnp.bfloat16), 'tensor', axis=0, tiled=...  40.8 us
    psum x1, blocking collectives, per_device(): lax.psum((first_gain_grad, second_gain_grad), ('dp', 'tensor'))  40.7 us
    reduce_scatter x1, waiting for transfers between devices, per_device(): lax.psum_scatter(layer_parts.reshape(-1, tokens.shape[1]), 'tensor', scat...  20.1 us
    concatenate x1, local copies, waits for them, and re-layouts, per_device(): jnp.concatenate([grad.astype(jnp.bfloat16) for grad in grads], axis=1)  19.6 us
  transfers between devices with their start and end apart: 6, of which 5 were waited for; matrix products, arithmetic and copies ran while one was open for 10% of the time, Pallas kernels for 23%

profile of v3, /device:TPU:0, one launch (start us, length us, event | category | flops | bytes accessed | tf_op | source)
XLA Modules:
  0.0 574.1 jit_solution(3741752492081166169)
XLA Ops:
  8.9 1.3 broadcast_in_dim.40.gain_ref
  11.5 1.3 pad.4
  12.8 1.4 copy.45.table_ref
  14.2 132.4 %gather_attend.1 = (bf16[4,256,1536]{2,1,0:T(8,128)(2,1)}, bf16[4,256,1536]{2,1,0:T(8,128)(2,1)}, bf16[3,1024,192]{2,1,0:T(8,128)(2,1)}, bf16[3,512,512]{2,1,0:T...) custom-call(bf16[256,1536]{1,0:T(8,128)(2,1)} %x_ref.3, ...), custom_call_target="tpu_custom_call" | custom-call | tf_op jit(solution)/shard_map/gather_attend/pallas_call | solution.py:262
  146.6 98.5 %feed.1 = (f32[256,1536]{1,0:T(8,128)}, f32[256,1536]{1,0:T(8,128)}, f32[1,1536]{1,0:T(1,128)}, bf16[4,256,192]{2,1,0:T(8,128)(2,1)}, bf16[4,256,1536]{2,1,0:T(8,128)(2,1)}, /*index=5*/bf16[3,1536,992]{2,1,0:T(8,128)(2,1)}) custom-call(bf16[256,1536]{1,0:T(8,128)(2,1)} %x_ref.3, bf16[4,256,192]{2,1,0:T(8,128)(2,1)} %get-tuple-element.29.own_ref, ...), custom_call_target="tpu_custom_call" | custom-call | tf_op jit(solution)/shard_map/feed/pallas_call | solution.py:538
  245.1 2.0 copy.46
  247.1 3.5 all-to-all-start
  251.8 9.4 %all-to-all-done = bf16[4,256,192]{1,2,0:T(8,128)(2,1)S(1)} async-done(((bf16[4,256,192]{1,2,0:T(8,128)(2,1)}), bf16[4,256,192]{1,2,0:T(8,128)(2,1)S(1)}, u32[]{:S(2)}, u32[]{:S(2)}) %all-to-all-start) | async-done | bytes 393248 | tf_op jit(solution)/shard_map/all_to_all | solution.py:669
  262.2 13.5 %attend_back.1 = (bf16[1024,192]{1,0:T(8,128)(2,1)}, bf16[1024,192]{1,0:T(8,128)(2,1)}, bf16[1024,192]{1,0:T(8,128)(2,1)}, f32[3,1536]{1,0:T(4,128)}) custom-call(bf16[1024,192]{1,0:T(8,128)(2,1)} %get-tuple-element.57.q_ref, bf16[1024,192]{1,0:T(8,128)(2,1)} %get-tuple-element.56.k_ref, bf16[1024,192]{1,0:T(8,128)(2,1)} %get-tuple-element.55.v_ref, ...), custom_call_target="tpu_custom_call" | custom-call | tf_op jit(solution)/shard_map/attend_back/pallas_call | solution.py:606
  275.8 2.1 fusion.11
  279.1 2.6 add_convert_fusion
  283.1 58.4 %reduce-scatter.6.cloned.1.call-done = bf16[256,1536]{1,0:T(8,128)(2,1)} async-done(((bf16[1024,1536]{1,0:T(8,128)(2,1)}), bf16[256,1536]{1,0:T(8,128)(2,1)}) %reduce-scatter.6.cloned.1.call-update) | async-done | bytes 786448 | tf_op jit(solution)/shard_map/reduce_scatter | solution.py:701
  341.5 1.8 fusion.1
  343.4 2.8 fusion.7
  346.9 6.2 %slice_bitcast_fusion = (bf16[1536,992]{1,0:T(8,128)(2,1)S(1)}, bf16[1536,992]{1,0:T(8,128)(2,1)}, bf16[1536,992]{1,0:T(8,128)(2,1)}) fusion(bf16[3,1536,992]{2,1,0:T(8,128)(2,1)} %get-tuple-element.43), kind=kLoop, calls=%fused_computation.1 | loop fusion | bytes 18284544 | tf_op jit(solution)/shard_map/squeeze | solution.py:664
  353.5 1.6 convolution_convert_fusion.3
  355.1 2.3 copy.48
  357.4 3.6 convolution_convert_fusion.1
  361.0 2.2 copy.50
  363.2 3.6 convolution_convert_fusion.2
  366.9 2.2 copy.49
  369.1 40.8 %all-gather.5.cloned.1.call-done = bf16[1024,1536]{1,0:T(8,128)(2,1)} async-done(((bf16[256,1536]{1,0:T(8,128)(2,1)}), bf16[1024,1536]{1,0:T(8,128)(2,1)}) %all-gather.5.cloned.1.call-update) | async-done | bytes 3145744 | tf_op jit(solution)/shard_map/all_gather | solution.py:665
  409.9 3.7 convolution_convert_fusion
  413.6 2.2 copy.51
  415.8 19.6 %concatenate.3 = bf16[1536,3744]{1,0:T(8,128)(2,1)} concatenate(bf16[1536,192]{1,0:T(8,128)(2,1)} %copy.48, bf16[1536,192]{1,0:T(8,128)(2,1)} %copy.49, bf16[1536,192]{1,0:T(8,128)(2,1)} %copy.50, bf16[1536,192]{1,0:T(8,128)(2,1)} %copy.51, bf16[1536,992]{1,0:T(8,128)(2,1)} %get-tuple-element.52, bf16[1536,992]{1,0:T(8,128)(2,1)} %get-tuple-element.51, ...), dimensions={1} | concatenate | bytes 23003136 | tf_op jit(solution)/shard_map/concatenate | solution.py:708
  436.3 14.5 %psum.22 = f32[32,3]{0,1:T(4,128)} all-reduce(f32[32,3]{0,1:T(4,128)S(1)} %select_reduce_fusion), channel_id=1, replica_groups=mesh['dp'=8,'tensor'=4] {'dp'}, use_global_device_ids=true, to_apply=%region_8.9 | all-reduce | flops 96 | bytes 768 | tf_op jit(solution)/shard_map/psum | solution.py:716
  450.9 20.1 %reduce-scatter.4.cloned.1.call-done = bf16[256,1536]{1,0:T(8,128)(2,1)} async-done(((bf16[1024,1536]{1,0:T(8,128)(2,1)}), bf16[256,1536]{1,0:T(8,128)(2,1)}) %reduce-scatter.4.cloned.1.call-update) | async-done | bytes 786448 | tf_op jit(solution)/shard_map/reduce_scatter | solution.py:661
  471.0 2.2 add_convert_fusion.1
  473.2 40.7 %all-reduce.1 = (f32[1536]{0:T(1024)}, f32[1536]{0:T(1024)}) all-reduce(f32[1536]{0:T(1024)S(1)} %get-tuple-element.46, f32[1536]{0:T(1024)S(1)} %reduce), channel_id=1, replica_groups=mesh['dp'=8,'tensor'=4] {'dp','tensor'}, use_global_device_ids=true, to_apply=%region_5.6 | all-reduce | flops 3072 | bytes 24576 | tf_op jit(solution)/shard_map/psum | solution.py:717
  513.9 49.4 %reduce-scatter.8.cloned.1.call-done = bf16[192,3744]{1,0:T(8,128)(2,1)} async-done(((bf16[1536,3744]{1,0:T(8,128)(2,1)}), bf16[192,3744]{1,0:T(8,128)(2,1)}) %reduce-scatter.8.cloned.1.call-update) | async-done | bytes 1437712 | tf_op jit(solution)/shard_map/reduce_scatter | solution.py:709
  563.2 2.1 fusion.9
  565.4 1.8 fusion.8
  (59 shorter events, 9.9 us)
Async XLA Ops:
  7.2 1.1 copy-start
  7.2 139.4 %all-gather.3.cloned.1.call-start = ((), (), s32[]{:S(2)}) async-start(), calls=%async_computation.4 | async-start | bytes 2433024 | tf_op jit(solution)/shard_map/all_gather | solution.py:652
  146.6 104.0 %copy-start.8 = (bf16[3,1024,192]{2,1,0:T(8,128)(2,1)S(1)}, bf16[3,1024,192]{2,1,0:T(8,128)(2,1)}, u32[]{:S(2)}) copy-start(bf16[3,1024,192]{2,1,0:T(8,128)(2,1)} %get-tuple-element.34) | copy-start | bytes 3538948
  247.1 14.1 %all-to-all-start = ((bf16[4,256,192]{1,2,0:T(8,128)(2,1)}), bf16[4,256,192]{1,2,0:T(8,128)(2,1)S(1)}, u32[]{:S(2)}, u32[]{:S(2)}) async-start(bf16[4,256,192]{1,2,0:T(8,128)(2,1)} %copy.46), calls=%async_computation.1 | async-start | bytes 786432 | tf_op jit(solution)/shard_map/all_to_all | solution.py:669
  250.5 91.0 %reduce-scatter.6.cloned.1.call-start = ((), (), s32[]{:S(2)}) async-start(), calls=%async_computation.6 | async-start | bytes 3932160 | tf_op jit(solution)/shard_map/reduce_scatter | solution.py:701
  262.2 13.6 %copy-start.5 = (bf16[1536,192]{0,1:T(8,128)(2,1)S(1)}, bf16[1536,192]{0,1:T(8,128)(2,1)}, u32[]{:S(2)}) copy-start(bf16[1536,192]{0,1:T(8,128)(2,1)} %param.17) | copy-start | bytes 1769476
  275.7 2.1 copy-start.6
  275.7 2.1 copy-start.10
  277.9 1.1 copy-start.4
  277.9 1.2 copy-start.12
  281.7 1.1 copy-start.2
  281.7 59.8 %copy-start.13 = (f32[1536]{0:T(1024)S(1)}, f32[1536]{0:T(1024)}, u32[]{:S(2)}) copy-start(f32[1536]{0:T(1024)} %param.15) | copy-start | bytes 18436
  281.7 61.7 %copy-start.9 = (f32[256,1536]{1,0:T(8,128)S(1)}, f32[256,1536]{1,0:T(8,128)}, u32[]{:S(2)}) copy-start(f32[256,1536]{1,0:T(8,128)} %get-tuple-element.33) | copy-start | bytes 4718596
  281.7 128.2 %all-gather.5.cloned.1.call-start = ((), (), s32[]{:S(2)}) async-start(), calls=%async_computation.7 | async-start | bytes 3932160 | tf_op jit(solution)/shard_map/all_gather | solution.py:665
  346.2 124.8 %reduce-scatter.4.cloned.1.call-start = ((), (), s32[]{:S(2)}) async-start(), calls=%async_computation.5 | async-start | bytes 3932160 | tf_op jit(solution)/shard_map/reduce_scatter | solution.py:661
  346.8 216.4 %reduce-scatter.8.cloned.1.call-start = ((), (), s32[]{:S(2)}) async-start(), calls=%async_computation.8 | async-start | bytes 13271040 | tf_op jit(solution)/shard_map/reduce_scatter | solution.py:709
  346.8 6.2 %copy-start.11 = (bf16[1024,192]{1,0:T(8,128)(2,1)S(1)}, bf16[1024,192]{1,0:T(8,128)(2,1)}, u32[]{:S(2)}) copy-start(bf16[1024,192]{1,0:T(8,128)(2,1)} %get-tuple-element.38) | copy-start | bytes 1179652
  346.8 6.6 %copy-start.17 = (bf16[4,256,1536]{2,1,0:T(8,128)(2,1)S(1)}, bf16[4,256,1536]{2,1,0:T(8,128)(2,1)}, u32[]{:S(2)}) copy-start(bf16[4,256,1536]{2,1,0:T(8,128)(2,1)} %get-tuple-element.41) | copy-start | bytes 9437188
  435.3 0.7 copy-start.14
  435.4 0.7 copy-start.16
  435.4 0.8 copy-start.15
  435.4 35.6 %copy-start.7 = (f32[256,1536]{1,0:T(8,128)S(1)}, f32[256,1536]{1,0:T(8,128)}, u32[]{:S(2)}) copy-start(f32[256,1536]{1,0:T(8,128)} %get-tuple-element.31) | copy-start | bytes 4718596
  473.2 93.9 %copy-start.1 = (bf16[1536,192]{0,1:T(8,128)(2,1)S(1)}, bf16[1536,192]{0,1:T(8,128)(2,1)}, u32[]{:S(2)}) copy-start(bf16[1536,192]{0,1:T(8,128)(2,1)} %param.19) | copy-start | bytes 1769476
  563.2 2.1 copy-start.3
Sparse Core Ops, SparseCore 0:
  11.5 62.2 all-gather.2
  281.8 59.6 reduce-scatter.5
  346.3 63.5 all-gather.4
  412.1 58.8 reduce-scatter.3
  474.4 88.7 reduce-scatter.7

commit v4 on v3

--- a/solution.py
+++ b/solution.py
@@ -18,6 +18,7 @@
 
 EPSILON = 1e-06
 MASKED = -1000000000.0
+HIGHEST = lax.Precision.HIGHEST
 VMEM_LIMIT = 60 * 1024 * 1024
 MESH = pl.DeviceIdType.MESH
 
@@ -108,7 +109,7 @@
 def gather_attend_kernel(
     nt, pieces, heads, head_dim,
     x_ref, cot_ref, gain_ref, wq_ref, wk_ref, wv_ref, bucket_ref, table_ref, start_ref,
-    first_out, cot_out, qkv_out, low_out, high_out, own_out, att_out,
+    first_out, cot_out, qkv_out, low_out, high_out, own_out,
     first, qkv, low, high, bias, att,
     send_sem, recv_sem, swap_send, swap_recv, local_sem,
 ):
@@ -217,7 +218,6 @@
     late = [
         pltpu.make_async_copy(low, low_out, local_sem.at[4]),
         pltpu.make_async_copy(high, high_out, local_sem.at[5]),
-        pltpu.make_async_copy(att, att_out, local_sem.at[6]),
     ]
     for one in late:
         one.start()
@@ -256,14 +256,14 @@
     vmem = pl.BlockSpec(memory_space=pltpu.VMEM)
     shapes = (
         (nt, rows, width), (nt, rows, width), (3, LEN, inner), (heads, HALF, HALF), (heads, HALF, LEN),
-        (nt, rows, inner), (nt, rows, inner),
+        (nt, rows, inner),
     )
     dma = pltpu.SemaphoreType.DMA
     return pl.pallas_call(
         functools.partial(gather_attend_kernel, nt, pieces, heads, inner // heads),
         out_shape=tuple(jax.ShapeDtypeStruct(shape, low) for shape in shapes),
         in_specs=[vmem, hbm] + [vmem] * 5 + [smem, smem],
-        out_specs=(hbm,) * 7,
+        out_specs=(hbm,) * 6,
         scratch_shapes=[
             pltpu.VMEM((nt, rows, width), low),
             pltpu.VMEM((3, LEN, inner), low),
@@ -271,7 +271,7 @@
             pltpu.VMEM((heads, HALF, LEN), low),
             pltpu.VMEM((heads, QB, SPAN), jnp.float32),
             pltpu.VMEM((nt, rows, inner), low),
-            dma((2, 2, nt, pieces)), dma((2, 2, nt, pieces)), dma((nt,)), dma((nt,)), dma((7,)),
+            dma((2, 2, nt, pieces)), dma((2, 2, nt, pieces)), dma((nt,)), dma((nt,)), dma((6,)),
         ],
         compiler_params=pltpu.CompilerParams(
             vmem_limit_bytes=VMEM_LIMIT, collective_id=0, has_side_effects=True
@@ -301,9 +301,9 @@
 def feed_kernel(
     nt, pieces,
     x_ref, own_ref, wo_ref, gain_ref, cot_own_ref, cot_hbm, wg_hbm, wu_hbm, wd_hbm,
-    middle_out, gm_out, gain_out, ga_out, lo_out, grads_out,
-    buf, cot, wg, wu, wd, hid, gg, gu, gs, lo, mate_in, acc_in, far_in, middle, grads,
-    send_sem, recv_sem, rs_send, rs_recv, local_sem,
+    base_out, gm_out, gain_out, ga_out, lo_out, grads_out,
+    buf, cot, wg, wu, wd, hid, gg, gu, gs, lo, mate_in, acc_in, far_in, middle, grads, mate_lo,
+    send_sem, recv_sem, rs_send, rs_recv, lo_sem, local_sem,
 ):
     t = lax.axis_index("tensor")
     barrier = greet(t, nt)
@@ -320,8 +320,7 @@
         total = total + dot(own_ref[j], wo_ref[j], ((1,), (0,)))
     middle[...] = total
     buf[t] = normed(total, gain_ref[...]).astype(jnp.bfloat16)
-    keep = [pltpu.make_async_copy(middle, middle_out, local_sem.at[4])]
-    keep[0].start()
+    keep = []
     pl.semaphore_wait(barrier, nt - 1)
     mate = t + 1 - 2 * lax.rem(t, 2)
     is_end = (t == 0) | (t == nt - 1)
@@ -474,6 +473,8 @@
     lax.fori_loop(0, nt, down_rows, 0)
     keep.append(pltpu.make_async_copy(lo, lo_out, local_sem.at[5]))
     keep[-1].start()
+    lo_swap = remote(lo.at[mate], mate_lo, mate, lo_sem.at[0], lo_sem.at[1])
+    lo_swap.start()
     pass_on(far, 0)
     lax.fori_loop(0, spans // 2, gate_up_cols, 0)
     pass_on(far, 1)
@@ -505,6 +506,8 @@
         for j in range(nt):
             ga_out[j, rows] = dot(grad_low, wo_ref[j], ((1,), (1,))).astype(jnp.bfloat16)
 
+    lo_swap.wait()
+    base_out[...] = middle[...] + lo[t].astype(jnp.float32) + mate_lo[...].astype(jnp.float32)
     for one in keep:
         one.wait()
     for piece in range(pieces):
@@ -542,15 +545,15 @@
             shape((nt, rows, inner), low), shape((nt, rows, width), low), shape((3, width, hidden), low),
         ),
         in_specs=[vmem] * 5 + [hbm] * 4,
-        out_specs=(hbm, vmem, vmem, vmem, hbm, hbm),
+        out_specs=(vmem, vmem, vmem, vmem, hbm, hbm),
         scratch_shapes=[
             pltpu.VMEM((nt, rows, width), low), pltpu.VMEM((nt, rows, width), low),
             pltpu.VMEM((hidden, width), low), pltpu.VMEM((hidden, width), low), pltpu.VMEM((hidden, width), low),
             pltpu.VMEM((nt * rows, hidden), low), pltpu.VMEM((nt * rows, hidden), low), pltpu.VMEM((nt * rows, hidden), low),
             pltpu.VMEM((nt, rows, width), low), pltpu.VMEM((nt, rows, width), low),
             pltpu.VMEM((rows, width), low), pltpu.VMEM((2, rows, width), low), pltpu.VMEM((rows, width), low),
-            pltpu.VMEM((rows, width), full), pltpu.VMEM((3, width, hidden), low),
-            dma((2, nt, pieces)), dma((2, nt, pieces)), dma((5, pieces)), dma((4, pieces)), dma((7,)),
+            pltpu.VMEM((rows, width), full), pltpu.VMEM((3, width, hidden), low), pltpu.VMEM((rows, width), low),
+            dma((2, nt, pieces)), dma((2, nt, pieces)), dma((5, pieces)), dma((4, pieces)), dma((2,)), dma((7,)),
         ],
         compiler_params=pltpu.CompilerParams(
             vmem_limit_bytes=VMEM_LIMIT, collective_id=1, has_side_effects=True
@@ -559,63 +562,366 @@
     )(tokens, attended, out_all, gain[None, :], cotangent, cot_all, gate_weight, up_weight, down_weight)
 
 
-def attend_back_kernel(heads, head_dim, q_ref, k_ref, v_ref, do_ref, low_ref, high_ref, dq_ref, dk_ref, dv_ref, dist_ref, diag_ref, dk_acc, dv_acc):
+def back_kernel(
+    nt, ndp, pieces, heads, head_dim, grad_type,
+    ga_ref, gm_ref, base_ref, x_ref, gain_ref, gain2_ref, own_ref, bucket_ref,
+    qkv_hbm, low_hbm, high_hbm, first_hbm, weight_hbm, lo_hbm,
+    layer_out, input_out, gain_out, gain2_out, table_out, q_out, k_out, v_out, o_out,
+    ga_in, qkv, low, high, first, weight, lo, acc_in, far_in,
+    gq, gq_in, diag, dk_acc, dv_acc,
+    og, og_sum, og_chip, og_line, og_line_in, pg, pg_sum, pg_chip,
+    gains_line, gains_in, dist_in,
+    swap_send, swap_recv, back_send, back_recv, lo_send, lo_recv,
+    pair_send, pair_recv, chip_send, chip_recv, line_send, line_recv,
+    gl_send, gl_recv, gd_send, gd_recv, dist_send, dist_recv, local_sem,
+):
+    t = lax.axis_index("tensor")
+    d = lax.axis_index("dp")
+    core = lax.rem(d, 2)
+    chip = d // 2
+    chips = ndp // 2
+    barrier = greet(t, nt)
+    for k in range(1, ndp):
+        pl.semaphore_signal(
+            barrier, inc=1, device_id={"dp": lax.rem(d + k, ndp)}, device_id_type=MESH
+        )
+    mate = t + 1 - 2 * lax.rem(t, 2)
+    is_end = (t == 0) | (t == nt - 1)
+    near = jnp.where(t < nt // 2, nt // 2, nt // 2 - 1)
+    far = jnp.where(t < nt // 2, nt - 1, 0)
+    loads = [
+        pltpu.make_async_copy(a, b, local_sem.at[i])
+        for i, (a, b) in enumerate(
+            ((qkv_hbm, qkv), (low_hbm, low), (high_hbm, high), (first_hbm, first), (weight_hbm, weight),
+             (lo_hbm.at[near], lo.at[lax.rem(near, 2)]), (lo_hbm.at[far], lo.at[lax.rem(far, 2)]))
+        )
+    ]
+    for one in loads:
+        one.start()
+    others = (far, near, mate)
+    row_count, width = x_ref.shape
+    inner = heads * head_dim
+    size = row_count // pieces
+    share = width // ndp
+    full = jnp.float32
+
+    def remote(src, dst, send, recv, **target):
+        return pltpu.make_async_remote_copy(
+            src_ref=src, dst_ref=dst, send_sem=send, recv_sem=recv,
+            device_id=target, device_id_type=MESH,
+        )
+
+    def swap(peer):
+        return remote(ga_ref.at[peer], ga_in.at[t], swap_send.at[peer], swap_recv.at[t], tensor=peer)
+
+    def swap_in(peer):
+        return remote(ga_ref.at[peer], ga_in.at[peer], swap_send.at[peer], swap_recv.at[peer], tensor=peer)
+
+    def lo_acc(origin, piece):
+        rows = pl.ds(piece * size, size)
+        j = lax.rem(origin, 2)
+        return remote(
+            lo.at[j, rows], acc_in.at[j, rows], lo_send.at[j, piece], lo_recv.at[j, piece], tensor=mate
+        )
+
+    def lo_far(origin, piece):
+        rows = pl.ds(piece * size, size)
+        j = lax.rem(origin, 2)
+        return remote(
+            lo.at[j, rows], far_in.at[rows], lo_send.at[j, piece], lo_recv.at[2, piece], tensor=origin
+        )
+
+    def pass_on(origin, piece):
+        @pl.when(jnp.logical_not(is_end))
+        def _():
+            lo_acc(origin, piece).wait_recv()
+            rows = pl.ds(piece * size, size)
+            j = lax.rem(origin, 2)
+            lo[j, rows] = (lo[j, rows].astype(full) + acc_in[j, rows].astype(full)).astype(jnp.bfloat16)
+            lo_far(origin, piece).start()
+
+    pl.semaphore_wait(barrier, nt - 1 + ndp - 1)
+    for peer in others:
+        swap(peer).start()
+    ga_in[t] = ga_ref[t]
+    loads[5].wait()
+    loads[6].wait()
+
+    @pl.when(is_end)
+    def _():
+        for origin in (far, near):
+            for piece in range(pieces):
+                lo_acc(origin, piece).start()
+
+    def block_rows(index):
+        return pl.ds(pl.multiple_of(index * share, share), share)
+
+    def pair(kind, c):
+        grads, landing = ((og, og_sum), (pg, pg_sum))[kind]
+        return remote(
+            grads.at[block_rows(2 * c + 1 - core)], landing.at[c],
+            pair_send.at[kind, c], pair_recv.at[kind, c], dp=d + 1 - 2 * core,
+        )
+
+    def chip_copy(kind, k):
+        sums, landing = ((og_sum, og_chip), (pg_sum, pg_chip))[kind]
+        to = lax.rem(chip + k, chips)
+        return remote(
+            sums.at[to], landing.at[k - 1], chip_send.at[kind, k - 1], chip_recv.at[kind, k - 1], dp=2 * to + core
+        )
+
+    def pair_sum(kind):
+        grads, sums = ((og, og_sum), (pg, pg_sum))[kind]
+        for c in range(chips):
+            pair(kind, c).wait_recv()
+            sums[c] = (grads[block_rows(2 * c + core)].astype(full) + sums[c].astype(full)).astype(grad_type)
+        for k in range(1, chips):
+            chip_copy(kind, k).start()
+
+    def chip_sum(kind):
+        sums, landing = ((og_sum, og_chip), (pg_sum, pg_chip))[kind]
+        total = sums[chip].astype(full)
+        for k in range(1, chips):
+            chip_copy(kind, k).wait_recv()
+            total = total + landing[k - 1].astype(full)
+        return total
+
+    span = 256
+    spans = width // span
+    own = jnp.concatenate([own_ref[j] for j in range(nt)], axis=1)
+    for i in range(spans):
+        left = gm_ref[:, pl.ds(i * span, span)].astype(jnp.bfloat16)
+        og[pl.ds(i * span, span), :] = dot(left, own, ((0,), (0,))).astype(grad_type)
+    for c in range(chips):
+        pair(0, c).start()
+
+    for i in range(3):
+        loads[i].wait()
     blocks = LEN // QB
-    for head in range(heads):
-        cols = pl.ds(head * head_dim, head_dim)
-        diag_ref[...] = jnp.zeros_like(diag_ref)
-        for block in reversed(range(blocks)):
-            keys = key_count(block)
-            rows = pl.ds(block * QB, QB)
-            first = LEN - block * QB
+    diag[...] = jnp.zeros_like(diag)
+    for block in reversed(range(blocks)):
+        keys = key_count(block)
+        rows = pl.ds(block * QB, QB)
+        first_col = LEN - block * QB
+
+        @pl.when(t != block)
+        def _():
+            swap_in(block).wait_recv()
+
+        parts = []
+        for head in range(heads):
+            cols = pl.ds(head * head_dim, head_dim)
             if keys == HALF:
-                probs_low = low_ref[head, rows, :]
+                probs_low = low[head, rows, :]
             else:
-                probs_low = high_ref[head, pl.ds(block * QB - HALF, QB), :]
-            probs = probs_low.astype(jnp.float32)
-            do = do_ref[rows, cols]
-            grad_probs = dot(do, v_ref[pl.ds(0, keys), cols], ((1,), (1,)))
+                probs_low = high[head, pl.ds(block * QB - HALF, QB), :]
+            probs = probs_low.astype(full)
+            do = ga_in[block, :, cols]
+            grad_probs = dot(do, qkv[2, pl.ds(0, keys), cols], ((1,), (1,)))
             weighted = jnp.sum(probs * grad_probs, axis=-1, keepdims=True)
             grad_low = (probs * (grad_probs - weighted)).astype(jnp.bfloat16)
-            span = pl.ds(first, keys)
-            diag_ref[:, span] = diag_ref[:, span] + grad_low.astype(jnp.float32)
-            dq_ref[rows, cols] = dot(grad_low, k_ref[pl.ds(0, keys), cols], ((1,), (0,))).astype(
-                jnp.bfloat16
-            )
-            key_part = dot(grad_low, q_ref[rows, cols], ((0,), (0,)))
+            reach = pl.ds(first_col, keys)
+            diag[head, :, reach] = diag[head, :, reach] + grad_low.astype(full)
+            parts.append(dot(grad_low, qkv[1, pl.ds(0, keys), cols], ((1,), (0,))))
+            key_part = dot(grad_low, qkv[0, rows, cols], ((0,), (0,)))
             value_part = dot(probs_low, do, ((0,), (0,)))
             if block == blocks - 1:
-                dk_acc[...] = key_part
-                dv_acc[...] = value_part
+                dk_acc[head] = key_part
+                dv_acc[head] = value_part
             else:
-                dk_acc[pl.ds(0, keys), :] += key_part
-                dv_acc[pl.ds(0, keys), :] += value_part
-        dk_ref[:, cols] = dk_acc[...].astype(jnp.bfloat16)
-        dv_ref[:, cols] = dv_acc[...].astype(jnp.bfloat16)
-        dist_ref[pl.ds(head, 1), :] = fold_diagonals(diag_ref[...])
-
-
-def whole_vmem(count):
-    return [pl.BlockSpec(memory_space=pltpu.VMEM)] * count
-
-
-def attend_back(query, key, value, grad_attended, low, high):
-    heads = low.shape[0]
-    inner = query.shape[1]
-    shape = jax.ShapeDtypeStruct(query.shape, jnp.bfloat16)
+                dk_acc[head, pl.ds(0, keys), :] += key_part
+                dv_acc[head, pl.ds(0, keys), :] += value_part
+        gq[rows, pl.ds(0, inner)] = jnp.concatenate(parts, axis=1).astype(jnp.bfloat16)
+        if block == 1:
+            pair_sum(0)
+    for block in range(blocks):
+        rows = pl.ds(block * QB, QB)
+        sides = [acc[head, rows, :] for acc in (dk_acc, dv_acc) for head in range(heads)]
+        gq[rows, pl.ds(inner, 2 * inner)] = jnp.concatenate(sides, axis=1).astype(jnp.bfloat16)
+
+    def token_rows(peer):
+        return pl.ds(pl.multiple_of(peer * row_count, row_count), row_count)
+
+    def give(peer):
+        return remote(
+            gq.at[token_rows(peer)], gq_in.at[t], back_send.at[peer], back_recv.at[t], tensor=peer
+        )
+
+    def taken(peer):
+        return remote(
+            gq.at[token_rows(peer)], gq_in.at[peer], back_send.at[peer], back_recv.at[peer], tensor=peer
+        )
+
+    for peer in others:
+        give(peer).start()
+    for head in range(heads):
+        dist_in[d, pl.ds(head, 1), :] = fold_diagonals(diag[head])
+
+    def dist_copy(k):
+        return remote(
+            dist_in.at[d], dist_in.at[d], dist_send.at[k - 1], dist_recv.at[d], dp=lax.rem(d + k, ndp)
+        )
+
+    for k in range(1, ndp):
+        dist_copy(k).start()
+    pass_on(far, 0)
+    loads[3].wait()
+    for i in range(spans):
+        cols = pl.ds(i * span, span)
+        left = first[:, :, cols].reshape(nt * row_count, span)
+        pg[cols, :] = dot(left, gq[...], ((0,), (0,))).astype(grad_type)
+    for c in range(chips):
+        pair(1, c).start()
+    pass_on(far, 1)
+    total = chip_sum(0)
+    for j in range(nt):
+        og_line[j] = total[:, j * inner : (j + 1) * inner].astype(grad_type)
+
+    def line_copy_out(peer):
+        return remote(og_line.at[peer], og_line_in.at[t], line_send.at[peer], line_recv.at[t], tensor=peer)
+
+    def line_in(peer):
+        return remote(og_line.at[peer], og_line_in.at[peer], line_send.at[peer], line_recv.at[peer], tensor=peer)
+
+    for peer in others:
+        line_copy_out(peer).start()
+    pair_sum(1)
+    pass_on(near, 0)
+    pass_on(near, 1)
+    loads[4].wait()
+    inputs = x_ref[...].astype(full)
+    inv = lax.rsqrt(jnp.mean(inputs * inputs, axis=-1, keepdims=True) + EPSILON)
+    grad_first = dot(gq[token_rows(t)], weight[t], ((1,), (0,)))
+    for peer in (mate, near, far):
+        taken(peer).wait_recv()
+        grad_first = grad_first + dot(gq_in[peer], weight[peer], ((1,), (0,)))
+    scaled = gain_ref[...] * grad_first
+    along = jnp.mean(scaled * inputs, axis=-1, keepdims=True)
+    gains_line[t, pl.ds(0, 1), :] = jnp.sum(grad_first * inputs * inv, axis=0, keepdims=True)
+    gains_line[t, pl.ds(1, 1), :] = gain2_ref[...]
+
+    def gain_copy(peer):
+        return remote(gains_line.at[t], gains_line.at[t], gl_send.at[peer], gl_recv.at[t], tensor=peer)
+
+    def gain_landed(peer):
+        return remote(gains_line.at[peer], gains_line.at[peer], gl_send.at[peer], gl_recv.at[peer], tensor=peer)
+
+    for peer in others:
+        gain_copy(peer).start()
+    input_out[...] = (gm_ref[...] + inv * scaled - inputs * (inv * inv * inv * along)).astype(jnp.bfloat16)
+    for peer in others:
+        gain_landed(peer).wait_recv()
+    gains_in[d] = gains_line[0] + gains_line[1] + gains_line[2] + gains_line[3]
+
+    def gains_copy(k):
+        return remote(
+            gains_in.at[d], gains_in.at[d], gd_send.at[k - 1], gd_recv.at[d], dp=lax.rem(d + k, ndp)
+        )
+
+    for k in range(1, ndp):
+        gains_copy(k).start()
+    total = chip_sum(1)
+    q_out[...] = total[:, :inner]
+    k_out[...] = total[:, inner : 2 * inner]
+    v_out[...] = total[:, 2 * inner :]
+    total = og_line[t].astype(full)
+    for peer in others:
+        line_in(peer).wait_recv()
+        total = total + og_line_in[peer].astype(full)
+    o_out[...] = total
+
+    def others_of(landing, send, recv):
+        for k in range(1, ndp):
+            peer = lax.rem(d + k, ndp)
+            remote(landing.at[peer], landing.at[peer], send.at[k - 1], recv.at[peer], dp=peer).wait_recv()
+
+    others_of(dist_in, dist_send, dist_recv)
+    dist = dist_in[0]
+    for k in range(1, ndp):
+        dist = dist + dist_in[k]
+    reach = dist.shape[1]
+    bucket = pltpu.roll(bucket_ref[...], 1, 1)[:, :reach]
+    hot = (lax.broadcasted_iota(jnp.int32, (NB, reach), 0) == bucket).astype(full)
+    table_out[...] = lax.dot_general(
+        dist, hot, (((1,), (1,)), ((), ())), precision=HIGHEST, preferred_element_type=full
+    )
+    for piece in range(pieces):
+        rows = pl.ds(piece * size, size)
+        remote(lo.at[0, rows], far_in.at[rows], lo_send.at[0, piece], lo_recv.at[2, piece], tensor=mate).wait_recv()
+        layer_out[rows] = (base_ref[rows] + far_in[rows].astype(full)).astype(jnp.bfloat16)
+    others_of(gains_in, gd_send, gd_recv)
+    total = gains_in[0]
+    for k in range(1, ndp):
+        total = total + gains_in[k]
+    gain_out[...] = total[0:1]
+    gain2_out[...] = total[1:2]
+
+    for peer in others:
+        swap(peer).wait_send()
+        give(peer).wait_send()
+        line_copy_out(peer).wait_send()
+        gain_copy(peer).wait_send()
+    for origin in (near, far):
+        for piece in range(pieces):
+            lo_acc(origin, piece).wait_send()
+    for kind in range(2):
+        for c in range(chips):
+            pair(kind, c).wait_send()
+        for k in range(1, chips):
+            chip_copy(kind, k).wait_send()
+    for k in range(1, ndp):
+        dist_copy(k).wait_send()
+        gains_copy(k).wait_send()
+
+
+def back(nt, ndp, grad_attended, grad_middle, base, tokens, gain, gain2_part, attended, bucket_row, qkv, probs_low, probs_high, first_all, weights, layer_parts):
+    rows, width = tokens.shape
+    heads = probs_low.shape[0]
+    inner = qkv.shape[2]
+    head_dim = inner // heads
+    low, full = jnp.bfloat16, jnp.float32
+    pieces = 2
+    share, chips = width // ndp, ndp // 2
+    grad_type = low if share % 16 == 0 else full
+    hbm = pl.BlockSpec(memory_space=pl.ANY)
+    vmem = pl.BlockSpec(memory_space=pltpu.VMEM)
+    dma = pltpu.SemaphoreType.DMA
+    shape = jax.ShapeDtypeStruct
+    reach = SPAN + QB
+    scratch = lambda *dims, kind=low: pltpu.VMEM(dims, kind)
+    part = shape((share, inner), full)
     return pl.pallas_call(
-        functools.partial(attend_back_kernel, heads, inner // heads),
-        out_shape=(shape, shape, shape, jax.ShapeDtypeStruct((heads, SPAN + QB), jnp.float32)),
-        in_specs=whole_vmem(6),
-        out_specs=tuple(whole_vmem(4)),
+        functools.partial(back_kernel, nt, ndp, pieces, heads, head_dim, grad_type),
+        out_shape=(
+            shape((rows, width), low), shape((rows, width), low), shape((1, width), full), shape((1, width), full),
+            shape((heads, NB), full), part, part, part, part,
+        ),
+        in_specs=[vmem] * 8 + [hbm] * 6,
+        out_specs=(vmem,) * 9,
         scratch_shapes=[
-            pltpu.VMEM((QB, SPAN + QB), jnp.float32),
-            pltpu.VMEM((LEN, inner // heads), jnp.float32),
-            pltpu.VMEM((LEN, inner // heads), jnp.float32),
+            scratch(nt, rows, inner), scratch(3, LEN, inner), scratch(heads, HALF, HALF), scratch(heads, HALF, LEN),
+            scratch(nt, rows, width), scratch(nt, 3 * inner, width), scratch(2, rows, width),
+            scratch(2, rows, width), scratch(rows, width),
+            scratch(nt * rows, 3 * inner), scratch(nt, rows, 3 * inner), scratch(heads, QB, reach, kind=full),
+            scratch(heads, LEN, head_dim, kind=full), scratch(heads, LEN, head_dim, kind=full),
+            scratch(width, nt * inner, kind=grad_type), scratch(chips, share, nt * inner, kind=grad_type), scratch(chips - 1, share, nt * inner, kind=grad_type),
+            scratch(nt, share, inner, kind=grad_type), scratch(nt, share, inner, kind=grad_type),
+            scratch(width, 3 * inner, kind=grad_type), scratch(chips, share, 3 * inner, kind=grad_type), scratch(chips - 1, share, 3 * inner, kind=grad_type),
+            scratch(nt, 2, width, kind=full), scratch(ndp, 2, width, kind=full),
+            scratch(ndp, heads, reach, kind=full),
+            dma((nt,)), dma((nt,)), dma((nt,)), dma((nt,)), dma((2, pieces)), dma((3, pieces)),
+            dma((2, chips)), dma((2, chips)), dma((2, chips - 1)), dma((2, chips - 1)), dma((nt,)), dma((nt,)),
+            dma((nt,)), dma((nt,)), dma((ndp - 1,)), dma((ndp,)), dma((ndp - 1,)), dma((ndp,)), dma((7,)),
         ],
-        compiler_params=pltpu.CompilerParams(vmem_limit_bytes=VMEM_LIMIT),
-        name="attend_back",
-    )(query, key, value, grad_attended, low, high)
+        compiler_params=pltpu.CompilerParams(
+            vmem_limit_bytes=VMEM_LIMIT, collective_id=2, has_side_effects=True
+        ),
+        cost_estimate=pl.CostEstimate(flops=60 * 10**9, bytes_accessed=200 * 10**6, transcendentals=0),
+        name="back",
+    )(
+        grad_attended, grad_middle, base, tokens, gain[None, :], gain2_part, attended, bucket_row,
+        qkv, probs_low, probs_high, first_all, weights, layer_parts,
+    )
 
 
 def per_device(
@@ -634,102 +940,46 @@
     bucket_index,
     cotangent,
 ):
-    own_rows = tokens.shape[0]
-    contract_cols = (((1,), (1,)), ((), ()))
-    contract_rows = (((0,), (0,)), ((), ()))
+    nt, ndp = lax.axis_size("tensor"), lax.axis_size("dp")
     bucket_row = jnp.pad(bucket_index, (0, 1))[None, :]
-    inputs = tokens.astype(jnp.float32)
-    nt = lax.axis_size("tensor")
-    first_all, grad_all, qkv, probs_low, probs_high, attended_own, attended_heads = gather_attend(
-        nt, tokens, cotangent, first_gain, (query_weight.T, key_weight.T, value_weight.T),
-        bucket_row, bucket_table, piece_start,
+    first_weights = (query_weight.T, key_weight.T, value_weight.T)
+
+    def whole(rows):
+        part = rows.shape[0] // ndp
+        mine = lax.dynamic_slice_in_dim(rows, lax.axis_index("dp") * part, part, 0)
+        return lax.all_gather(mine, ("tensor", "dp"), axis=0, tiled=True).reshape(nt, *rows.shape)
+
+    out_all = whole(out_weight.T)
+    first_all, cot_all, qkv, probs_low, probs_high, attended = gather_attend(
+        nt, tokens, cotangent, first_gain, first_weights, bucket_row, bucket_table, piece_start
     )
-    first_all = first_all.reshape(-1, tokens.shape[1])
-    attended_low = attended_heads.reshape(-1, query_weight.shape[1])
-    query_low, key_low, value_low = qkv[0], qkv[1], qkv[2]
-    out_cols = out_weight.T
-    own_part = out_cols.shape[0] // lax.axis_size("dp")
-    out_all = lax.all_gather(
-        lax.dynamic_slice_in_dim(out_cols, lax.axis_index("dp") * own_part, own_part, 0),
-        ("tensor", "dp"), axis=0, tiled=True,
-    ).reshape(nt, *out_cols.shape)
-    middle, grad_middle, second_gain_grad, grad_attended_own, layer_parts, feed_grads = feed(
-        nt, tokens, attended_own, out_all, second_gain, cotangent, grad_all,
+    joined, attended = lax.optimization_barrier((jnp.concatenate(first_weights, axis=0), attended))
+    weights_all = whole(joined)
+    base, grad_middle, second_part, grad_attended, layer_parts, feed_grads = feed(
+        nt, tokens, attended, out_all, second_gain, cotangent, cot_all,
         gate_weight.T, up_weight.T, down_weight.T,
     )
-    second_gain_grad = second_gain_grad[0]
-    layer_out = middle + lax.psum_scatter(
-        layer_parts.reshape(-1, tokens.shape[1]), "tensor", scatter_dimension=0, tiled=True
-    ).astype(jnp.float32)
-    gate_grad, up_grad, down_grad = feed_grads[0], feed_grads[1], feed_grads[2]
-    middle_all = lax.all_gather(grad_middle.astype(jnp.bfloat16), "tensor", axis=0, tiled=True)
-    out_grad = lax.dot_general(
-        middle_all, attended_low, contract_rows, preferred_element_type=jnp.float32
-    )
-    grad_attended = lax.all_to_all(
-        grad_attended_own, "tensor", split_axis=0, concat_axis=0, tiled=True
-    ).reshape(-1, query_weight.shape[1])
-    grad_query_low, grad_key_low, grad_value_low, distance_sums = attend_back(
-        query_low, key_low, value_low, grad_attended, probs_low, probs_high
-    )
-    width = min(distance_sums.shape[1] - 1, bucket_index.shape[0])
-    table_hot = bucket_index[None, :width] == jnp.arange(NB, dtype=jnp.int32)[:, None]
-    table_grad = jnp.sum(
-        jnp.where(table_hot[:, None, :], distance_sums[None, :, 1 : width + 1], 0.0), axis=2
-    )
-    query_grad = lax.dot_general(
-        first_all, grad_query_low, contract_rows, preferred_element_type=jnp.float32
-    )
-    key_grad = lax.dot_general(
-        first_all, grad_key_low, contract_rows, preferred_element_type=jnp.float32
-    )
-    value_grad = lax.dot_general(
-        first_all, grad_value_low, contract_rows, preferred_element_type=jnp.float32
-    )
-    summed_rows = jnp.zeros(
-        (lax.axis_size("tensor") * own_rows, query_weight.shape[0]), jnp.float32
-    )
-    for grad_low, weight in (
-        (grad_query_low, query_weight),
-        (grad_key_low, key_weight),
-        (grad_value_low, value_weight),
-    ):
-        picked = grad_low
-        summed_rows = summed_rows + lax.dot_general(
-            picked, weight, contract_cols, preferred_element_type=jnp.float32
-        )
-    grad_first = lax.psum_scatter(
-        summed_rows.astype(jnp.bfloat16), "tensor", scatter_dimension=0, tiled=True
-    ).astype(jnp.float32)
-    _, first_back = jax.vjp(normed, inputs, first_gain)
-    input_part, first_gain_grad = first_back(grad_first)
-    input_grad = grad_middle + input_part
-    grads = (query_grad, key_grad, value_grad, out_grad, gate_grad, up_grad, down_grad)
-    joined = jnp.concatenate([grad.astype(jnp.bfloat16) for grad in grads], axis=1)
-    summed = lax.psum_scatter(joined, "dp", scatter_dimension=0, tiled=True).astype(jnp.float32)
-    edges = []
-    for grad in grads[:-1]:
-        edges.append((edges[-1] if edges else 0) + grad.shape[1])
-    query_grad, key_grad, value_grad, out_grad, gate_grad, up_grad, down_grad = jnp.split(
-        summed, edges, axis=1
-    )
-    table_grad = lax.psum(table_grad, "dp")
-    first_gain_grad, second_gain_grad = lax.psum(
-        (first_gain_grad, second_gain_grad), ("dp", "tensor")
+    feed_sums = lax.psum_scatter(feed_grads, "dp", scatter_dimension=1, tiled=True).astype(jnp.float32)
+    (
+        layer_out, input_grad, first_gain_grad, second_gain_grad, table_grad,
+        query_grad, key_grad, value_grad, out_grad,
+    ) = back(
+        nt, ndp, grad_attended, grad_middle, base, tokens, first_gain, second_part, attended, bucket_row,
+        qkv, probs_low, probs_high, first_all, weights_all, layer_parts,
     )
     return (
-        layer_out.astype(jnp.bfloat16),
-        input_grad.astype(jnp.bfloat16),
-        first_gain_grad,
+        layer_out,
+        input_grad,
+        first_gain_grad[0],
         query_grad,
         key_grad,
         value_grad,
         out_grad,
-        table_grad,
-        second_gain_grad,
-        gate_grad,
-        up_grad,
-        down_grad,
+        table_grad.T,
+        second_gain_grad[0],
+        feed_sums[0],
+        feed_sums[1],
+        feed_sums[2],
     )
 
 

time: 584 us -> 419 us (0.72)
  waiting for transfers between devices: 179 us -> 0.07 us
  Pallas kernels: 244 us -> 376 us
  blocking collectives: 55.2 us -> 0 us
  local copies, waits for them, and re-layouts: 51.9 us -> 14.4 us
  matrix products: 18.2 us -> 0 us
    reduce_scatter x3 -> x1, waiting for transfers between devices: 128 us -> 0.01 us  [per_device(): lax.psum_scatter(feed_grads, 'dp', scatter_dimension=1, tiled=True)]
    pallas_call x1, Pallas kernels: 13.5 us -> 102 us  [back(): pl.pallas_call(functools.partial(back_kernel, nt, ndp, pieces, heads, hea...]
    psum x2 -> x0, blocking collectives: 55.2 us -> none  [the longest x1 40.7 us: per_device(): lax.psum((first_gain_grad, second_gain_grad), ('dp', 'tensor'))]
    pallas_call x1, Pallas kernels: 98.5 us -> 142 us  [feed(): pl.pallas_call(functools.partial(feed_kernel, nt, pieces), out_shape=(sha...]
    all_gather x2, waiting for transfers between devices: 40.8 us -> 0.02 us  [whole(): lax.all_gather(mine, ('tensor', 'dp'), axis=0, tiled=True)]
    concatenate x1 -> x0, local copies, waits for them, and re-layouts: 19.6 us -> none  [per_device(): jnp.concatenate([grad.astype(jnp.bfloat16) for grad in grads], axis=1)]
    dot_general x7 -> x0, matrix products: 18.2 us -> none  [the longest x3 5.66 us: per_device(): lax.dot_general(picked, weight, contract_cols, preferred_element_type=jnp...]
    all_to_all x1 -> x0, waiting for transfers between devices: 9.41 us -> none  [per_device(): lax.all_to_all(grad_attended_own, 'tensor', split_axis=0, concat_axis=0,...]
  transfers between devices with their start and end apart: 6 -> 3, of which waited for: 5 -> 0; matrix products, arithmetic and copies ran while one was open for 10% -> 2% of each run, Pallas kernels for 23% -> 92%
where the time goes in v4:
time: 419 us; the launch traced here: 411 us
  Pallas kernels  376 us (90%)
  local copies, waits for them, and re-layouts  14.4 us (3%)
  between operations  14.4 us (3%)
  other arithmetic  5.5 us (1%)
    pallas_call x1, Pallas kernels, feed(): pl.pallas_call(functools.partial(feed_kernel, nt, pieces), out_shape=(sha...  142 us
    pallas_call x1, Pallas kernels, gather_attend(): pl.pallas_call(functools.partial(gather_attend_kernel, nt, pieces, heads,...  132 us
    pallas_call x1, Pallas kernels, back(): pl.pallas_call(functools.partial(back_kernel, nt, ndp, pieces, heads, hea...  102 us
  transfers between devices with their start and end apart: 3, of which 0 were waited for; matrix products, arithmetic and copies ran while one was open for 2% of the time, Pallas kernels for 92%

profile of v4, /device:TPU:0, one launch (start us, length us, event | category | flops | bytes accessed | tf_op | source)
XLA Modules:
  0.0 411.0 jit_solution(9294970388857381651)
XLA Ops:
  7.2 0.0 copy-start
  7.2 0.0 copy-start.1
  7.2 0.0 copy-start.2
  7.2 0.0 all-gather.3.cloned.1.call-start
  7.3 1.0 copy-done
  8.2 0.6 dynamic-slice_bitcast_fusion
  8.9 0.0 all-gather.3.cloned.1.call-update
  8.9 0.0 all-gather.5.cloned.1.call-start
  9.0 1.3 pad.4
  10.3 1.3 broadcast_in_dim.10.gain_ref
  11.6 1.4 copy.26.table_ref
  12.9 132.4 %gather_attend.1 = (bf16[4,256,1536]{2,1,0:T(8,128)(2,1)}, bf16[4,256,1536]{2,1,0:T(8,128)(2,1)}, bf16[3,1024,192]{2,1,0:T(8,128)(2,1)}, bf16[3,512,512]{2,1,0:T...) custom-call(bf16[256,1536]{1,0:T(8,128)(2,1)} %x_ref.5, bf16[256,1536]{1,0:T(8,128)(2,1)} %cot_own_ref.1, ...), custom_call_target="tpu_custom_call" | custom-call | tf_op jit(solution)/shard_map/gather_attend/pallas_call | solution.py:262
  145.4 1.3 pad_maximum_fusion
  146.7 1.6 constant_dynamic-slice_fusion
  148.4 0.0 all-gather.5.cloned.1.call-update
  148.4 0.2 reduce-scatter.2.cloned.1.call-start
  148.6 0.6 broadcast_in_dim.12.gain_ref
  149.2 142.1 %feed.1 = (f32[256,1536]{1,0:T(8,128)}, f32[256,1536]{1,0:T(8,128)}, f32[1,1536]{1,0:T(1,128)}, bf16[4,256,192]{2,1,0:T(8,128)(2,1)}, bf16[4,256,1536]{2,1,0:T(8,128)(2,1)}, /*index=5*/bf16[3,1536,992]{2,1,0:T(8,128)(2,1)}) custom-call(bf16[256,1536]{1,0:T(8,128)(2,1)} %x_ref.5, bf16[4,256,192]{2,1,0:T(8,128)(2,1)} %get-tuple-element.36.own_ref, ...), custom_call_target="tpu_custom_call" | custom-call | tf_op jit(solution)/shard_map/feed/pallas_call | solution.py:541
  291.3 0.0 reduce-scatter.2.cloned.1.call-update
  291.3 0.0 all-gather.5.cloned.1.call-done
  291.4 101.9 %back.1 = (bf16[256,1536]{1,0:T(8,128)(2,1)}, bf16[256,1536]{1,0:T(8,128)(2,1)}, f32[1,1536]{1,0:T(1,128)}, f32[1,1536]{1,0:T(1,128)}, f32[3,32]{1,0:T(4,128)}, ...) custom-call(bf16[4,256,192]{2,1,0:T(8,128)(2,1)} %get-tuple-element.38.ga_ref, ...), custom_call_target="tpu_custom_call" | custom-call | flops 60000002048 | bytes 200000000 | tf_op jit(solution)/shard_map/back/pallas_call | solution.py:893
  393.3 1.3 reduce
  394.6 1.3 reduce.1
  395.9 1.6 convert_element_type.3
  397.5 1.5 slice_bitcast_fusion
  399.0 0.9 copy.34
  399.9 0.9 copy.35
  400.8 0.7 copy.36
  401.4 0.7 copy.37
  402.1 0.7 copy.38
  402.8 0.7 copy.39
  403.5 0.6 copy.40
  (22 shorter events, 0.0 us)
Async XLA Ops:
  7.2 1.1 copy-start
  7.2 138.2 %copy-start.1 = (bf16[1536,192]{0,1:T(8,128)(2,1)S(1)}, bf16[1536,192]{0,1:T(8,128)(2,1)}, u32[]{:S(2)}) copy-start(bf16[1536,192]{0,1:T(8,128)(2,1)} %param.16) | copy-start | bytes 1769476
  7.2 138.2 %copy-start.2 = (bf16[1536,192]{0,1:T(8,128)(2,1)S(1)}, bf16[1536,192]{0,1:T(8,128)(2,1)}, u32[]{:S(2)}) copy-start(bf16[1536,192]{0,1:T(8,128)(2,1)} %param.17) | copy-start | bytes 1769476
  7.2 138.2 %copy-start.3 = (bf16[1536,192]{0,1:T(8,128)(2,1)S(1)}, bf16[1536,192]{0,1:T(8,128)(2,1)}, u32[]{:S(2)}) copy-start(bf16[1536,192]{0,1:T(8,128)(2,1)} %param.18) | copy-start | bytes 1769476
  7.2 142.0 %all-gather.3.cloned.1.call-start = ((), (), s32[]{:S(2)}) async-start(), calls=%async_computation.1 | async-start | bytes 2433024 | tf_op jit(solution)/shard_map/all_gather | solution.py:950
  8.9 282.4 %all-gather.5.cloned.1.call-start = ((), (), s32[]{:S(2)}) async-start(), calls=%async_computation.2 | async-start | bytes 7299072 | tf_op jit(solution)/shard_map/all_gather | solution.py:950
  12.9 135.7 %copy-start.10 = (f32[1536]{0:T(1024)S(1)}, f32[1536]{0:T(1024)}, u32[]{:S(2)}) copy-start(f32[1536]{0:T(1024)} %param.21) | copy-start | bytes 18436
  148.4 247.5 %reduce-scatter.2.cloned.1.call-start = ((), (), s32[]{:S(2)}) async-start(), calls=%async_computation.3 | async-start | bytes 10616832 | tf_op jit(solution)/shard_map/reduce_scatter | solution.py:962
  397.5 1.5 copy-start.5
  397.5 2.4 copy-start.4
  397.5 3.3 copy-start.9
  397.5 3.9 copy-start.8
  399.0 3.1 copy-start.7
  399.0 3.8 copy-start.6
  399.0 4.5 %copy-start.11 = (f32[3,32]{1,0:T(4,128)S(1)}, f32[3,32]{1,0:T(4,128)}, u32[]{:S(2)}) copy-start(f32[3,32]{1,0:T(4,128)} %get-tuple-element.55) | copy-start | bytes 1156
Sparse Core Ops, SparseCore 0:
  11.5 61.9 all-gather.2
  148.5 87.8 all-gather.4
  291.4 95.0 reduce-scatter.1

commit v5 on v4

--- a/solution.py
+++ b/solution.py
@@ -39,7 +39,7 @@
 def toeplitz(bucket_row, table_ref, head):
     row = jnp.zeros(bucket_row.shape, jnp.float32)
     for bucket in range(NB):
-        row = jnp.where(bucket_row == bucket, table_ref[bucket, head], row)
+        row = jnp.where(bucket_row == bucket, table_ref[head, bucket], row)
     rows = jnp.broadcast_to(row, (QB, DIST))
     return pltpu.roll(rows, DIST - (QB - 1), 1, stride=1, stride_axis=0)[:, :SPAN]
 
@@ -107,18 +107,81 @@
 
 
 def gather_attend_kernel(
-    nt, pieces, heads, head_dim,
-    x_ref, cot_ref, gain_ref, wq_ref, wk_ref, wv_ref, bucket_ref, table_ref, start_ref,
-    first_out, cot_out, qkv_out, low_out, high_out, own_out,
-    first, qkv, low, high, bias, att,
-    send_sem, recv_sem, swap_send, swap_recv, local_sem,
+    nt, ndp, pieces, heads, head_dim, exchange,
+    x_ref, cot_ref, gain_ref, gain2_ref, bucket_ref, table_ref, start_ref, *rest,
 ):
+    weight_refs, rest = rest[: 4 if exchange else 1], rest[4 if exchange else 1 :]
+    (
+        first_out, cot_out, qkv_out, low_out, high_out, own_out, whole_out, middle_out, second_out,
+        first, qkv, low, high, bias, att, own, whole,
+        send_sem, recv_sem, swap_send, swap_recv, line_send, line_recv, chip_send, chip_recv, core_send, core_recv,
+        local_sem,
+    ) = rest
     t = lax.axis_index("tensor")
+    d = lax.axis_index("dp")
+    core = lax.rem(d, 2)
+    chip = d // 2
+    chips = ndp // 2
     barrier = greet(t, nt)
+    greeted = nt - 1
+    if exchange:
+        for k in range(chips):
+            peer = 2 * lax.rem(chip + k, chips) + core if k else d + 1 - 2 * core
+            pl.semaphore_signal(barrier, inc=1, device_id={"dp": peer}, device_id_type=MESH)
+        greeted += chips
+    inner = heads * head_dim
+    share = whole.shape[1] // ndp
     own_cot = pltpu.make_async_copy(cot_ref, cot_out.at[t], local_sem.at[0])
     own_cot.start()
+    if exchange:
+        loads = [
+            pltpu.make_async_copy(weight, whole.at[t, pl.ds(i * inner, inner)], local_sem.at[1 + i])
+            for i, weight in enumerate(weight_refs)
+        ]
+    else:
+        loads = [pltpu.make_async_copy(weight_refs[0], whole, local_sem.at[1])]
+    for one in loads:
+        one.start()
+
+    def slices(index, plane):
+        return whole.at[plane, pl.ds(pl.multiple_of(index * share, share), share)]
+
+    def remote(src, dst, send, recv, **target):
+        return pltpu.make_async_remote_copy(
+            src_ref=src, dst_ref=dst, send_sem=send, recv_sem=recv, device_id=target, device_id_type=MESH
+        )
+
+    def plane_at(q):
+        return lax.rem(t + q, nt)
+
+    def to_plane(q):
+        return remote(slices(d, t), slices(d, t), line_send.at[q - 1], line_recv.at[t], tensor=plane_at(q))
+
+    def from_plane(q):
+        p = plane_at(q)
+        return remote(slices(d, p), slices(d, p), line_send.at[q - 1], line_recv.at[p], tensor=p)
+
+    def to_chip(k, q):
+        part = slices(d, plane_at(q))
+        return remote(
+            part, part, chip_send.at[k - 1, q - 1], chip_recv.at[k - 1, q - 1], dp=2 * lax.rem(chip + k, chips) + core
+        )
+
+    def from_chip(k, q):
+        peer = 2 * lax.rem(chip - k + chips, chips) + core
+        part = slices(peer, plane_at(q))
+        return remote(part, part, chip_send.at[k - 1, q - 1], chip_recv.at[k - 1, q - 1], dp=peer)
+
+    def to_core(k, q):
+        part = slices(2 * lax.rem(chip - k + chips, chips) + core, plane_at(q))
+        return remote(part, part, core_send.at[k, q - 1], core_recv.at[k, q - 1], dp=d + 1 - 2 * core)
+
+    def from_core(k, q):
+        part = slices(2 * lax.rem(chip - k + chips, chips) + 1 - core, plane_at(q))
+        return remote(part, part, core_send.at[k, q - 1], core_recv.at[k, q - 1], dp=d + 1 - 2 * core)
+
     first[t] = normed(x_ref[...].astype(jnp.float32), gain_ref[...]).astype(jnp.bfloat16)
-    pl.semaphore_wait(barrier, nt - 1)
+    pl.semaphore_wait(barrier, greeted)
 
     def copy(way, stage, step, piece):
         buf = first if stage == 0 else cot_out
@@ -132,11 +195,9 @@
         buf = first if stage == 0 else cot_out
         rows = buf.shape[1] // pieces
         part = buf.at[jnp.clip(t - sign * step, 0, nt - 1), pl.ds(piece * rows, rows)]
-        pltpu.make_async_remote_copy(
-            src_ref=part, dst_ref=part,
-            send_sem=send_sem.at[way, stage, step - 1, piece],
-            recv_sem=recv_sem.at[way, stage, step - 1, piece],
-            device_id={"tensor": jnp.clip(t + sign, 0, nt - 1)}, device_id_type=MESH,
+        remote(
+            part, part, send_sem.at[way, stage, step - 1, piece], recv_sem.at[way, stage, step - 1, piece],
+            tensor=jnp.clip(t + sign, 0, nt - 1),
         ).wait_recv()
 
     ways = ((0, t, t < nt - 1), (1, nt - 1 - t, t > 0))
@@ -172,10 +233,16 @@
 
     def project(origin):
         rows = pl.ds(pl.multiple_of(origin * QB, QB), QB)
-        for place, weight in enumerate((wq_ref, wk_ref, wv_ref)):
-            qkv[place, rows, :] = dot(first[origin], weight[...], ((1,), (1,))).astype(jnp.bfloat16)
+        for place in range(3):
+            weight = whole[t, pl.ds(place * inner, inner), :]
+            qkv[place, rows, :] = dot(first[origin], weight, ((1,), (1,))).astype(jnp.bfloat16)
 
     tick(0)
+    for one in loads:
+        one.wait()
+    if exchange:
+        for q in range(1, nt):
+            to_plane(q).start()
     project(t)
     for head in range(heads):
         bias[head] = toeplitz(bucket_ref[...], table_ref, head)
@@ -191,19 +258,24 @@
         def _():
             project(t + k)
 
+        if exchange and k == 2:
+            for q in range(1, nt):
+                from_plane(q).wait_recv()
+                for j in range(1, chips):
+                    to_chip(j, q).start()
+                to_core(0, q).start()
+
     starts = [start_ref[0, piece] for piece in range(NPIECE)]
-    keep = [pltpu.make_async_copy(first, first_out, local_sem.at[1]), pltpu.make_async_copy(qkv, qkv_out, local_sem.at[2])]
+    keep = [
+        pltpu.make_async_copy(first, first_out, local_sem.at[5]),
+        pltpu.make_async_copy(qkv, qkv_out, local_sem.at[6]),
+    ]
     for one in keep:
         one.start()
 
     def swap(block):
-        return pltpu.make_async_remote_copy(
-            src_ref=att.at[block], dst_ref=own_out.at[t],
-            send_sem=swap_send.at[block], recv_sem=swap_recv.at[t],
-            device_id={"tensor": block}, device_id_type=MESH,
-        )
-
-    own_att = pltpu.make_async_copy(att.at[t], own_out.at[t], local_sem.at[3])
+        return remote(att.at[block], own.at[t], swap_send.at[block], swap_recv.at[t], tensor=block)
+
     for block in range(LEN // QB):
         att[block] = attend_block(block, head_dim, allowed_block(block, starts), qkv, bias, low, high)
 
@@ -213,29 +285,57 @@
 
         @pl.when(t == block)
         def _():
-            own_att.start()
+            own[t] = att[block]
 
     late = [
-        pltpu.make_async_copy(low, low_out, local_sem.at[4]),
-        pltpu.make_async_copy(high, high_out, local_sem.at[5]),
+        pltpu.make_async_copy(low, low_out, local_sem.at[7]),
+        pltpu.make_async_copy(high, high_out, local_sem.at[8]),
     ]
     for one in late:
         one.start()
-    for k in range(nt, 2 * nt):
+    tick(nt)
+    if exchange:
+        for k in range(1, chips):
+            for q in range(1, nt):
+                from_chip(k, q).wait_recv()
+                to_core(k, q).start()
+    tick(nt + 1)
+    for block in range(nt):
+        @pl.when(t != block)
+        def _():
+            remote(att.at[block], own.at[block], swap_send.at[block], swap_recv.at[block], tensor=block).wait_recv()
+
+    if exchange:
+        for k in range(chips):
+            for q in range(1, nt):
+                from_core(k, q).wait_recv()
+    late += [
+        pltpu.make_async_copy(own, own_out, local_sem.at[9]),
+        pltpu.make_async_copy(whole, whole_out, local_sem.at[10]),
+    ]
+    for one in late[2:]:
+        one.start()
+    total = x_ref[...].astype(jnp.float32)
+    for j in range(nt):
+        total = total + dot(own[j], whole[j, pl.ds(3 * inner, inner), :], ((1,), (0,)))
+    middle_out[...] = total
+    second_out[...] = normed(total, gain2_ref[...]).astype(jnp.bfloat16)
+    for k in range(nt + 2, 2 * nt):
         tick(k)
     for block in range(nt):
         @pl.when(t != block)
         def _():
             swap(block).wait_send()
-            pltpu.make_async_remote_copy(
-                src_ref=att.at[block], dst_ref=own_out.at[block],
-                send_sem=swap_send.at[block], recv_sem=swap_recv.at[block],
-                device_id={"tensor": block}, device_id_type=MESH,
-            ).wait_recv()
-
-    own_att.wait()
+
     for one in keep + late:
         one.wait()
+    if exchange:
+        for q in range(1, nt):
+            to_plane(q).wait_send()
+            for k in range(1, chips):
+                to_chip(k, q).wait_send()
+            for k in range(chips):
+                to_core(k, q).wait_send()
     for piece in range(pieces):
         for way, last, onward in ways:
             for stage in range(2):
@@ -245,39 +345,51 @@
                         copy(way, stage, step, piece).wait_send()
 
 
-def gather_attend(nt, tokens, cotangent, gain, weights, bucket_row, table, starts):
-    heads = table.shape[1]
+def gather_attend(nt, ndp, tokens, cotangent, gain, gain2, weights, bucket_row, table, starts):
+    heads = table.shape[0]
+    rows, width = tokens.shape
     inner = weights[0].shape[0]
-    rows, width = tokens.shape
-    low = jnp.bfloat16
+    low, full = jnp.bfloat16, jnp.float32
     pieces = 2
+    exchange = (4 * inner // ndp) % 16 == 0
+    if not exchange:
+        joined = jnp.concatenate(weights, axis=0)
+        part = joined.shape[0] // ndp
+        mine = lax.dynamic_slice_in_dim(joined, lax.axis_index("dp") * part, part, 0)
+        weights = (lax.all_gather(mine, ("tensor", "dp"), axis=0, tiled=True).reshape(nt, *joined.shape),)
+    chips = ndp // 2
     smem = pl.BlockSpec(memory_space=pltpu.SMEM)
     hbm = pl.BlockSpec(memory_space=pl.ANY)
     vmem = pl.BlockSpec(memory_space=pltpu.VMEM)
     shapes = (
         (nt, rows, width), (nt, rows, width), (3, LEN, inner), (heads, HALF, HALF), (heads, HALF, LEN),
-        (nt, rows, inner),
+        (nt, rows, inner), (nt, 4 * inner, width),
     )
     dma = pltpu.SemaphoreType.DMA
     return pl.pallas_call(
-        functools.partial(gather_attend_kernel, nt, pieces, heads, inner // heads),
-        out_shape=tuple(jax.ShapeDtypeStruct(shape, low) for shape in shapes),
-        in_specs=[vmem, hbm] + [vmem] * 5 + [smem, smem],
-        out_specs=(hbm,) * 6,
+        functools.partial(gather_attend_kernel, nt, ndp, pieces, heads, inner // heads, exchange),
+        out_shape=tuple(jax.ShapeDtypeStruct(shape, low) for shape in shapes)
+        + (jax.ShapeDtypeStruct((rows, width), full), jax.ShapeDtypeStruct((rows, width), low)),
+        in_specs=[vmem, hbm, vmem, vmem, vmem, smem, smem] + [hbm] * len(weights),
+        out_specs=(hbm,) * 7 + (vmem, vmem),
         scratch_shapes=[
             pltpu.VMEM((nt, rows, width), low),
             pltpu.VMEM((3, LEN, inner), low),
             pltpu.VMEM((heads, HALF, HALF), low),
             pltpu.VMEM((heads, HALF, LEN), low),
-            pltpu.VMEM((heads, QB, SPAN), jnp.float32),
+            pltpu.VMEM((heads, QB, SPAN), full),
             pltpu.VMEM((nt, rows, inner), low),
-            dma((2, 2, nt, pieces)), dma((2, 2, nt, pieces)), dma((nt,)), dma((nt,)), dma((6,)),
+            pltpu.VMEM((nt, rows, inner), low),
+            pltpu.VMEM((nt, 4 * inner, width), low),
+            dma((2, 2, nt, pieces)), dma((2, 2, nt, pieces)), dma((nt,)), dma((nt,)),
+            dma((nt - 1,)), dma((nt,)), dma((chips - 1, nt - 1)), dma((chips - 1, nt - 1)),
+            dma((chips, nt - 1)), dma((chips, nt - 1)), dma((11,)),
         ],
         compiler_params=pltpu.CompilerParams(
             vmem_limit_bytes=VMEM_LIMIT, collective_id=0, has_side_effects=True
         ),
         name="gather_attend",
-    )(tokens, cotangent, gain[None, :], *weights, bucket_row, table, starts)
+    )(tokens, cotangent, gain[None, :], gain2[None, :], bucket_row, table, starts, *weights)
 
 
 def fold_diagonals(grid):
@@ -300,9 +412,9 @@
 
 def feed_kernel(
     nt, pieces,
-    x_ref, own_ref, wo_ref, gain_ref, cot_own_ref, cot_hbm, wg_hbm, wu_hbm, wd_hbm,
+    middle, second_ref, gain_ref, cot_own_ref, whole_hbm, cot_hbm, wg_hbm, wu_hbm, wd_hbm,
     base_out, gm_out, gain_out, ga_out, lo_out, grads_out,
-    buf, cot, wg, wu, wd, hid, gg, gu, gs, lo, mate_in, acc_in, far_in, middle, grads, mate_lo,
+    buf, cot, wg, wu, wd, hid, gg, gu, gs, lo, wo, mate_in, acc_in, far_in, grads, mate_lo,
     send_sem, recv_sem, rs_send, rs_recv, lo_sem, local_sem,
 ):
     t = lax.axis_index("tensor")
@@ -313,13 +425,12 @@
     ]
     for one in loads:
         one.start()
-    row_count = x_ref.shape[0]
+    row_count = middle.shape[0]
     size = row_count // pieces
-    total = x_ref[...].astype(jnp.float32)
-    for j in range(nt):
-        total = total + dot(own_ref[j], wo_ref[j], ((1,), (0,)))
-    middle[...] = total
-    buf[t] = normed(total, gain_ref[...]).astype(jnp.bfloat16)
+    inner = wo.shape[1]
+    wo_load = pltpu.make_async_copy(whole_hbm.at[:, pl.ds(3 * inner, inner)], wo, local_sem.at[4])
+    wo_load.start()
+    buf[t] = second_ref[...]
     keep = []
     pl.semaphore_wait(barrier, nt - 1)
     mate = t + 1 - 2 * lax.rem(t, 2)
@@ -482,6 +593,7 @@
     keep.append(pltpu.make_async_copy(grads, grads_out, local_sem.at[6]))
     keep[-1].start()
 
+    wo_load.wait()
     for piece in range(pieces):
         rows = pl.ds(piece * size, size)
         to_mate(piece).wait_recv()
@@ -504,7 +616,7 @@
             gain_out[...] += part
         grad_low = grad_middle.astype(jnp.bfloat16)
         for j in range(nt):
-            ga_out[j, rows] = dot(grad_low, wo_ref[j], ((1,), (1,))).astype(jnp.bfloat16)
+            ga_out[j, rows] = dot(grad_low, wo[j], ((1,), (1,))).astype(jnp.bfloat16)
 
     lo_swap.wait()
     base_out[...] = middle[...] + lo[t].astype(jnp.float32) + mate_lo[...].astype(jnp.float32)
@@ -528,14 +640,14 @@
                 to_far(origin, piece).wait_send()
 
 
-def feed(nt, tokens, attended, out_all, gain, cotangent, cot_all, gate_weight, up_weight, down_weight):
-    rows, width = tokens.shape
+def feed(nt, middle, second, gain, cotangent, whole, cot_all, gate_weight, up_weight, down_weight):
+    rows, width = middle.shape
     hidden = gate_weight.shape[0]
     low, full = jnp.bfloat16, jnp.float32
     pieces = 2
     hbm = pl.BlockSpec(memory_space=pl.ANY)
     vmem = pl.BlockSpec(memory_space=pltpu.VMEM)
-    inner = attended.shape[2]
+    inner = whole.shape[1] // 4
     dma = pltpu.SemaphoreType.DMA
     shape = jax.ShapeDtypeStruct
     return pl.pallas_call(
@@ -544,22 +656,23 @@
             shape((rows, width), full), shape((rows, width), full), shape((1, width), full),
             shape((nt, rows, inner), low), shape((nt, rows, width), low), shape((3, width, hidden), low),
         ),
-        in_specs=[vmem] * 5 + [hbm] * 4,
+        in_specs=[vmem] * 4 + [hbm] * 5,
         out_specs=(vmem, vmem, vmem, vmem, hbm, hbm),
         scratch_shapes=[
             pltpu.VMEM((nt, rows, width), low), pltpu.VMEM((nt, rows, width), low),
             pltpu.VMEM((hidden, width), low), pltpu.VMEM((hidden, width), low), pltpu.VMEM((hidden, width), low),
             pltpu.VMEM((nt * rows, hidden), low), pltpu.VMEM((nt * rows, hidden), low), pltpu.VMEM((nt * rows, hidden), low),
             pltpu.VMEM((nt, rows, width), low), pltpu.VMEM((nt, rows, width), low),
+            pltpu.VMEM((nt, inner, width), low),
             pltpu.VMEM((rows, width), low), pltpu.VMEM((2, rows, width), low), pltpu.VMEM((rows, width), low),
-            pltpu.VMEM((rows, width), full), pltpu.VMEM((3, width, hidden), low), pltpu.VMEM((rows, width), low),
+            pltpu.VMEM((3, width, hidden), low), pltpu.VMEM((rows, width), low),
             dma((2, nt, pieces)), dma((2, nt, pieces)), dma((5, pieces)), dma((4, pieces)), dma((2,)), dma((7,)),
         ],
         compiler_params=pltpu.CompilerParams(
             vmem_limit_bytes=VMEM_LIMIT, collective_id=1, has_side_effects=True
         ),
         name="feed",
-    )(tokens, attended, out_all, gain[None, :], cotangent, cot_all, gate_weight, up_weight, down_weight)
+    )(middle, second, gain[None, :], cotangent, whole, cot_all, gate_weight, up_weight, down_weight)
 
 
 def back_kernel(
@@ -592,7 +705,8 @@
     loads = [
         pltpu.make_async_copy(a, b, local_sem.at[i])
         for i, (a, b) in enumerate(
-            ((qkv_hbm, qkv), (low_hbm, low), (high_hbm, high), (first_hbm, first), (weight_hbm, weight),
+            ((qkv_hbm, qkv), (low_hbm, low), (high_hbm, high), (first_hbm, first),
+             (weight_hbm.at[:, pl.ds(0, weight.shape[1])], weight),
              (lo_hbm.at[near], lo.at[lax.rem(near, 2)]), (lo_hbm.at[far], lo.at[lax.rem(far, 2)]))
         )
     ]
@@ -942,22 +1056,12 @@
 ):
     nt, ndp = lax.axis_size("tensor"), lax.axis_size("dp")
     bucket_row = jnp.pad(bucket_index, (0, 1))[None, :]
-    first_weights = (query_weight.T, key_weight.T, value_weight.T)
-
-    def whole(rows):
-        part = rows.shape[0] // ndp
-        mine = lax.dynamic_slice_in_dim(rows, lax.axis_index("dp") * part, part, 0)
-        return lax.all_gather(mine, ("tensor", "dp"), axis=0, tiled=True).reshape(nt, *rows.shape)
-
-    out_all = whole(out_weight.T)
-    first_all, cot_all, qkv, probs_low, probs_high, attended = gather_attend(
-        nt, tokens, cotangent, first_gain, first_weights, bucket_row, bucket_table, piece_start
+    weights = (query_weight.T, key_weight.T, value_weight.T, out_weight.T)
+    first_all, cot_all, qkv, probs_low, probs_high, attended, whole, middle, second = gather_attend(
+        nt, ndp, tokens, cotangent, first_gain, second_gain, weights, bucket_row, bucket_table.T, piece_start
     )
-    joined, attended = lax.optimization_barrier((jnp.concatenate(first_weights, axis=0), attended))
-    weights_all = whole(joined)
     base, grad_middle, second_part, grad_attended, layer_parts, feed_grads = feed(
-        nt, tokens, attended, out_all, second_gain, cotangent, cot_all,
-        gate_weight.T, up_weight.T, down_weight.T,
+        nt, middle, second, second_gain, cotangent, whole, cot_all, gate_weight.T, up_weight.T, down_weight.T
     )
     feed_sums = lax.psum_scatter(feed_grads, "dp", scatter_dimension=1, tiled=True).astype(jnp.float32)
     (
@@ -965,7 +1069,7 @@
         query_grad, key_grad, value_grad, out_grad,
     ) = back(
         nt, ndp, grad_attended, grad_middle, base, tokens, first_gain, second_part, attended, bucket_row,
-        qkv, probs_low, probs_high, first_all, weights_all, layer_parts,
+        qkv, probs_low, probs_high, first_all, whole, layer_parts,
     )
     return (
         layer_out,

time: 419 us -> 386 us (0.921)
  Pallas kernels: 376 us -> 349 us
    pallas_call x1, Pallas kernels: 142 us -> 108 us  [feed(): pl.pallas_call(functools.partial(feed_kernel, nt, pieces), out_shape=(sha...]
    pallas_call x1, Pallas kernels: 132 us -> 139 us  [gather_attend(): pl.pallas_call(functools.partial(gather_attend_kernel, nt, ndp, pieces, h...]
  transfers between devices with their start and end apart: 3 -> 1, of which waited for: 0 -> 0; matrix products, arithmetic and copies ran while one was open for 2% -> 1% of each run, Pallas kernels for 92% -> 27%
where the time goes in v5:
time: 386 us; the launch traced here: 378 us
  Pallas kernels  349 us (90%)
  between operations  14.6 us (4%)
  local copies, waits for them, and re-layouts  10.4 us (3%)
  other arithmetic  4.18 us (1%)
    pallas_call x1, Pallas kernels, gather_attend(): pl.pallas_call(functools.partial(gather_attend_kernel, nt, ndp, pieces, h...  139 us
    pallas_call x1, Pallas kernels, feed(): pl.pallas_call(functools.partial(feed_kernel, nt, pieces), out_shape=(sha...  108 us
    pallas_call x1, Pallas kernels, back(): pl.pallas_call(functools.partial(back_kernel, nt, ndp, pieces, heads, hea...  103 us
  transfers between devices with their start and end apart: 1, of which 0 were waited for; matrix products, arithmetic and copies ran while one was open for 1% of the time, Pallas kernels for 27%

profile of v5, /device:TPU:0, one launch (start us, length us, event | category | flops | bytes accessed | tf_op | source)
XLA Modules:
  0.0 378.4 jit_solution(17362862695512206935)
XLA Ops:
  7.2 0.0 reduce-scatter.2.cloned.1.call-start
  7.2 1.3 broadcast_in_dim.11.gain_ref
  8.5 1.3 broadcast_in_dim.12.gain2_ref.gain_ref
  9.8 1.3 pad.4
  11.1 138.5 %gather_attend.1 = (bf16[4,256,1536]{2,1,0:T(8,128)(2,1)}, bf16[4,256,1536]{2,1,0:T(8,128)(2,1)}, bf16[3,1024,192]{2,1,0:T(8,128)(2,1)}, bf16[3,512,512]{2,1,0:T...) custom-call(bf16[256,1536]{1,0:T(8,128)(2,1)} %x_ref.3, ...), custom_call_target="tpu_custom_call" | custom-call | tf_op jit(solution)/shard_map/gather_attend/pallas_call | solution.py:369
  149.6 108.0 %feed.1 = (f32[256,1536]{1,0:T(8,128)}, f32[256,1536]{1,0:T(8,128)}, f32[1,1536]{1,0:T(1,128)}, bf16[4,256,192]{2,1,0:T(8,128)(2,1)}, bf16[4,256,1536]{2,1,0:T(8,128)(2,1)}, /*index=5*/bf16[3,1536,992]{2,1,0:T(8,128)(2,1)}) custom-call(f32[256,1536]{1,0:T(8,128)} %get-tuple-element.36.middle, bf16[256,1536]{1,0:T(8,128)(2,1)} %get-tuple-element.37.second_ref, ...), custom_call_target="tpu_custom_call" | custom-call | tf_op jit(solution)/shard_map/feed/pallas_call | solution.py:653
  257.6 0.0 reduce-scatter.2.cloned.1.call-update
  257.7 102.7 %back.1 = (bf16[256,1536]{1,0:T(8,128)(2,1)}, bf16[256,1536]{1,0:T(8,128)(2,1)}, f32[1,1536]{1,0:T(1,128)}, f32[1,1536]{1,0:T(1,128)}, f32[3,32]{1,0:T(4,128)}, ...) custom-call(bf16[4,256,192]{2,1,0:T(8,128)(2,1)} %get-tuple-element.40.ga_ref, ...), custom_call_target="tpu_custom_call" | custom-call | flops 60000002048 | bytes 200000000 | tf_op jit(solution)/shard_map/back/pallas_call | solution.py:1007
  360.4 1.3 reduce
  361.7 1.3 reduce.1
  363.0 0.0 reduce-scatter.2.cloned.1.call-done
  363.0 1.6 convert_element_type.3
  364.6 0.0 copy-start.1
  364.6 0.0 copy-start
  364.6 0.0 copy-start.5
  364.6 0.0 copy-start.4
  364.6 1.5 slice_bitcast_fusion
  366.1 0.0 copy-start.3
  366.1 0.0 copy-done.1
  366.1 0.9 copy.33
  367.0 0.0 copy-done
  367.0 0.9 copy.34
  367.8 0.0 copy-done.5
  367.8 0.7 copy.35
  368.5 0.0 copy-done.4
  368.5 0.7 copy.36
  369.2 0.0 copy-done.3
  369.2 0.7 copy.37
  369.9 0.0 copy-done.2
  369.9 0.7 copy.38
  370.6 0.0 copy-done.6
  370.6 0.6 copy.39
  (2 shorter events, 0.0 us)
Async XLA Ops:
  7.2 355.8 %reduce-scatter.2.cloned.1.call-start = ((), (), s32[]{:S(2)}) async-start(), calls=%async_computation.1 | async-start | bytes 10616832 | tf_op jit(solution)/shard_map/reduce_scatter | solution.py:1066
  364.6 1.5 copy-start.1
  364.6 2.4 copy-start
  364.6 3.3 copy-start.5
  364.6 3.9 %copy-start.4 = (f32[192,192]{1,0:T(8,128)S(1)}, f32[192,192]{1,0:T(8,128)}, u32[]{:S(2)}) copy-start(f32[192,192]{1,0:T(8,128)} %get-tuple-element.79) | copy-start | bytes 442372
  366.1 3.1 copy-start.3
  366.1 3.8 %copy-start.2 = (f32[192,192]{1,0:T(8,128)S(1)}, f32[192,192]{1,0:T(8,128)}, u32[]{:S(2)}) copy-start(f32[192,192]{1,0:T(8,128)} %get-tuple-element.81) | copy-start | bytes 442372
  366.1 4.5 %copy-start.6 = (f32[3,32]{1,0:T(4,128)S(1)}, f32[3,32]{1,0:T(4,128)}, u32[]{:S(2)}) copy-start(f32[3,32]{1,0:T(4,128)} %get-tuple-element.57) | copy-start | bytes 1156
Sparse Core Ops, SparseCore 0:
  257.8 94.9 reduce-scatter.1
